TPU v7x, 32 devices: a whole 2x2x4 slice. The times are simulated.
32 devices in a mesh: seq: 8 (over y, x, core), head: 4 (over z).
Axes of the slice: x: 2, y: 2, z: 4, core: 2. Of those that a mesh axis runs over, the one named last changes fastest.
Arguments:
- features: bfloat16 [4096, 4096], P('seq', 'head'), may hold values from -6 to 6
- key_weight: bfloat16 [4096, 4096], P(None, 'head'), may hold values from -0.09375 to 0.09375
- value_weight: bfloat16 [4096, 4096], P(None, 'head'), may hold values from -0.09375 to 0.09375
- queries: bfloat16 [4096, 4096], P('seq', 'head'), may hold values from -6 to 6
- log_decay: float32 [4096, 32], P('seq', 'head'), may hold values from -1.5 to 0, as said below
- out_grad: bfloat16 [4096, 4096], P('seq', 'head'), may hold values from -6 to 6
Outputs:
- attended: bfloat16 [4096, 4096], P('seq', 'head')
- query_grad: bfloat16 [4096, 4096], P('seq', 'head')
- feature_grad: bfloat16 [4096, 4096], P('seq', 'head')
- key_weight_grad: float32 [4096, 4096], P('seq', 'head')
- value_weight_grad: float32 [4096, 4096], P('seq', 'head')
Inputs may be any that keep to these rules, and one draw needn't show every extreme that they name: `log_decay`: every entry is negative.
All inputs are finite; a program needn't handle non-finite values.
Results may differ from a plain program's by a relative error of at most 0.014.
Values may be sent and summed in bfloat16 or wider, within the bound.
No kernel may reach another device: no remote copies, remote signals or barrier semaphores. Data moves between devices by JAX's collectives and lax.ppermute only.
A program may use at most 192 MiB of HBM per device.

v0:
```python
import functools

import jax
import jax.numpy as jnp
from jax import lax
from jax.experimental import pallas as pl
from jax.experimental.pallas import tpu as pltpu
from jax.sharding import PartitionSpec as P

BF = jnp.bfloat16
F32 = jnp.float32
NT = (((1,), (1,)), ((), ()))
TN = (((0,), (0,)), ((), ()))
VMEM_LIMIT = 60 * 1024 * 1024


def dot(a, b):
    return jnp.dot(a, b, preferred_element_type=F32)


def dot_nt(a, b):
    return lax.dot_general(a, b, NT, preferred_element_type=F32)


def dot_tn(a, b):
    return lax.dot_general(a, b, TN, preferred_element_type=F32)


def params(**more):
    return pltpu.CompilerParams(vmem_limit_bytes=VMEM_LIMIT, **more)


def after(x, *done):
    return lax.optimization_barrier((x, *done))[0]


def cost(flops, data):
    return pl.CostEstimate(flops=flops, bytes_accessed=data, transcendentals=0)


def last_kv_kernel(width, pieces, index_ref, *refs):
    parts = refs[:pieces]
    kw_ref, vw_ref, ka_ref, va_ref, tail_ref, k_ref, v_ref, s_ref, held = refs[pieces:]

    @pl.when(pl.program_id(0) == 0)
    def _():
        rows = held.shape[0] // (pieces // 2)
        for i in range(pieces // 2):
            held[i * rows : (i + 1) * rows, :] = parts[2 * i][...] + parts[2 * i + 1][...]

    f = held[...]
    keys = (ka_ref[...] + dot(f, kw_ref[...])).astype(BF)
    values = (va_ref[...] + dot(f, vw_ref[...])).astype(BF)
    k_ref[...] = keys
    v_ref[...] = values
    scaled = (keys.astype(F32) * tail_ref[...]).astype(BF)
    for i in range(s_ref.shape[0]):
        cut = slice(i * width, (i + 1) * width)
        s_ref[i] = dot_tn(scaled[:, cut], values[:, cut]).astype(BF)


def last_kv(parts, index, key_weight, value_weight, key_sum, value_sum, tail, width, per):
    tokens, proj = key_sum.shape
    depth = parts[0].shape[1]
    cols = width * per
    whole = [pl.BlockSpec(p.shape, lambda j, d: (0, 0)) for p in parts]
    weight = pl.BlockSpec((depth, cols), lambda j, d: (d[0], j))
    column = pl.BlockSpec((tokens, cols), lambda j, d: (0, j))
    state = pl.BlockSpec((per, width, width), lambda j, d: (j, 0, 0))
    return pl.pallas_call(
        functools.partial(last_kv_kernel, width, len(parts)),
        grid_spec=pltpu.PrefetchScalarGridSpec(
            num_scalar_prefetch=1,
            grid=(proj // cols,),
            in_specs=whole + [weight, weight, column, column, column],
            out_specs=[column, column, state],
            scratch_shapes=[pltpu.VMEM((tokens, depth), BF)],
        ),
        out_shape=[
            jax.ShapeDtypeStruct((tokens, proj), BF),
            jax.ShapeDtypeStruct((tokens, proj), BF),
            jax.ShapeDtypeStruct((proj // width, width, width), BF),
        ],
        compiler_params=params(),
        cost_estimate=cost(4 * tokens * depth * proj, 12 * tokens * proj + 4 * depth * proj),
        name="last_kv",
    )(index, *parts, key_weight, value_weight, key_sum, value_sum, tail)


def causal_tiles(tokens):
    tile = min(256, tokens)
    for row in range(tokens // tile):
        yield slice(row * tile, (row + 1) * tile), slice(0, (row + 1) * tile)


def anti_tiles(tokens):
    tile = min(256, tokens)
    for row in range(tokens // tile):
        yield slice(row * tile, (row + 1) * tile), slice(row * tile, tokens)


def local_kernel(width, q_ref, k_ref, v_ref, dec_ref, mix_ref):
    for i in range(dec_ref.shape[0]):
        cut = slice(i * width, (i + 1) * width)
        for rows, seen in causal_tiles(q_ref.shape[0]):
            scores = dot_nt(q_ref[rows, cut], k_ref[seen, cut])
            weights = (scores * dec_ref[i, rows, seen].astype(F32)).astype(BF)
            mix_ref[rows, cut] = dot(weights, v_ref[seen, cut])


def norm_kernel(width, q_ref, g_ref, mix_ref, grow_ref, qt_ref, s_ref, att_ref, hg_ref, r_ref):
    for i in range(s_ref.shape[0]):
        cut = slice(i * width, (i + 1) * width)
        mixed = mix_ref[:, cut] + grow_ref[:, cut] * dot(q_ref[:, cut], s_ref[i])
        grad = g_ref[:, cut].astype(F32)
        scale = lax.rsqrt(jnp.mean(mixed * mixed, axis=-1, keepdims=True) + 1e-06)
        projection = jnp.mean(grad * mixed, axis=-1, keepdims=True)
        att_ref[:, cut] = (mixed * scale).astype(BF)
        head_grad = (scale * grad - mixed * (scale * scale * scale * projection)).astype(BF)
        hg_ref[:, cut] = head_grad
        r_ref[i] = dot(qt_ref[cut, :], head_grad).astype(BF)


def back_query_kernel(width, k_ref, v_ref, hg_ref, dec_ref, grow_ref, s_ref, qg_ref):
    for i in range(s_ref.shape[0]):
        cut = slice(i * width, (i + 1) * width)
        for rows, seen in causal_tiles(k_ref.shape[0]):
            pairs = dot_nt(hg_ref[rows, cut], v_ref[seen, cut])
            pairs = (pairs * dec_ref[i, rows, seen].astype(F32)).astype(BF)
            carried = grow_ref[rows, cut] * dot_nt(hg_ref[rows, cut], s_ref[i])
            qg_ref[rows, cut] = (dot(pairs, k_ref[seen, cut]) + carried).astype(BF)


def back_keys_kernel(width, q_ref, k_ref, v_ref, hg_ref, dect_ref, kg_ref, vg_ref):
    for i in range(dect_ref.shape[0]):
        cut = slice(i * width, (i + 1) * width)
        for rows, seen in anti_tiles(q_ref.shape[0]):
            decay = dect_ref[i, rows, seen].astype(F32)
            pairs = (dot_nt(v_ref[rows, cut], hg_ref[seen, cut]) * decay).astype(BF)
            kg_ref[rows, cut] = dot(pairs, q_ref[seen, cut])
            weights = (dot_nt(k_ref[rows, cut], q_ref[seen, cut]) * decay).astype(BF)
            vg_ref[rows, cut] = dot(weights, hg_ref[seen, cut])


def close_kernel(width, k_ref, v_ref, kl_ref, vl_ref, tail_ref, r_ref, grads_ref):
    for i in range(r_ref.shape[0]):
        cut = slice(i * width, (i + 1) * width)
        tail = tail_ref[:, cut]
        grads_ref[0, :, cut] = (kl_ref[:, cut] + tail * dot_nt(v_ref[:, cut], r_ref[i])).astype(BF)
        grads_ref[1, :, cut] = (vl_ref[:, cut] + tail * dot(k_ref[:, cut], r_ref[i])).astype(BF)


def per_head(kernel, args, kinds, outs, heads, width, per, flops, name):
    tokens = args[0].shape[0]
    specs = {
        "col": pl.BlockSpec((tokens, width * per), lambda j: (0, j)),
        "row": pl.BlockSpec((width * per, tokens), lambda j: (j, 0)),
        "dec": pl.BlockSpec((per, tokens, tokens), lambda j: (j, 0, 0)),
        "state": pl.BlockSpec((per, width, width), lambda j: (j, 0, 0)),
        "pair": pl.BlockSpec((2, tokens, width * per), lambda j: (0, 0, j)),
    }
    shapes = {
        "col": (tokens, heads * width),
        "state": (heads, width, width),
        "pair": (2, tokens, heads * width),
    }
    data = sum(a.size * a.dtype.itemsize for a in args)
    return pl.pallas_call(
        functools.partial(kernel, width),
        grid=(heads // per,),
        in_specs=[specs[k] for k in kinds],
        out_specs=[specs[k] for k, _ in outs],
        out_shape=[jax.ShapeDtypeStruct(shapes[k], t) for k, t in outs],
        compiler_params=params(),
        cost_estimate=cost(flops, data),
        name=name,
    )(*args)


def feature_kernel(index_ref, grads_ref, kw_ref, vw_ref, out_ref):
    total = dot_nt(grads_ref[0], kw_ref[...]) + dot_nt(grads_ref[1], vw_ref[...])
    out_ref[...] = total.astype(BF)


def feature_term(index, grads, key_weight, value_weight, span):
    _, tokens, proj = grads.shape
    tile = min(256, span)
    steps = span // tile
    weight = pl.BlockSpec((tile, proj), lambda j, d: (d[0] * steps + j, 0))
    return pl.pallas_call(
        feature_kernel,
        grid_spec=pltpu.PrefetchScalarGridSpec(
            num_scalar_prefetch=1,
            grid=(steps,),
            in_specs=[pl.BlockSpec(grads.shape, lambda j, d: (0, 0, 0)), weight, weight],
            out_specs=pl.BlockSpec((tokens, tile), lambda j, d: (0, j)),
        ),
        out_shape=jax.ShapeDtypeStruct((tokens, span), BF),
        compiler_params=params(),
        cost_estimate=cost(4 * tokens * proj * span, 4 * proj * (tokens + span)),
        name="feature_term",
    )(index[None], grads, key_weight, value_weight)


def weight_kernel(count, index_ref, fo_ref, fp_ref, go_ref, gp_ref, *refs):
    total = dot(fo_ref[0], go_ref[0]) + dot(fp_ref[0], gp_ref[0])
    for r in refs[:count]:
        total += r[...].astype(F32)
    refs[count][...] = total.astype(refs[count].dtype)


def weight_term(index, which, own_t, partner_t, grads, partner_grads, adds, kind):
    _, tokens, proj = grads.shape
    span = own_t.shape[1]
    tile = min(256, proj)
    rows = pl.BlockSpec((1, span, tokens), lambda j, d: (d[0], 0, 0))
    grad = pl.BlockSpec((1, tokens, tile), lambda j, d: (which, 0, j))
    column = pl.BlockSpec((span, tile), lambda j, d: (0, j))
    return pl.pallas_call(
        functools.partial(weight_kernel, len(adds)),
        grid_spec=pltpu.PrefetchScalarGridSpec(
            num_scalar_prefetch=1,
            grid=(proj // tile,),
            in_specs=[rows, rows, grad, grad] + [column] * len(adds),
            out_specs=column,
        ),
        out_shape=jax.ShapeDtypeStruct((span, proj), kind),
        compiler_params=params(),
        cost_estimate=cost(4 * tokens * proj * span, 4 * tokens * (proj + span)),
        name="weight_term",
    )(index[None], own_t, partner_t, grads, partner_grads, *adds)


def turn_kernel(count, info_ref, *refs):
    shards, (own_ref, other_ref, held, turned, sem) = refs[: 2 * count - 1], refs[2 * count - 1 :]
    relative = pl.program_id(0) - info_ref[0]
    core = info_ref[1]
    for i, shard in enumerate(shards):
        offset = i if i < count else count - 1 - i

        @pl.when(relative == offset)
        def _():
            copy = pltpu.make_async_copy(shard, held, sem)
            copy.start()
            copy.wait()

    turned[...] = held[...].T
    rows = own_ref.shape[1]
    own_ref[0] = turned[pl.ds(pl.multiple_of(core * rows, rows), rows), :]
    other_ref[0] = turned[pl.ds(pl.multiple_of((1 - core) * rows, rows), rows), :]


def turn_features(info, shards, count):
    tokens, depth = shards[0].shape
    half = pl.BlockSpec((1, depth // 2, tokens), lambda j, d: (j, 0, 0))
    return pl.pallas_call(
        functools.partial(turn_kernel, count),
        grid_spec=pltpu.PrefetchScalarGridSpec(
            num_scalar_prefetch=1,
            grid=(count,),
            in_specs=[pl.BlockSpec(memory_space=pl.ANY)] * len(shards),
            out_specs=[half, half],
            scratch_shapes=[
                pltpu.VMEM((tokens, depth), BF),
                pltpu.VMEM((depth, tokens), BF),
                pltpu.SemaphoreType.DMA,
            ],
        ),
        out_shape=[jax.ShapeDtypeStruct((count, depth // 2, tokens), BF)] * 2,
        compiler_params=params(),
        cost_estimate=cost(0, 16 * tokens * depth * count),
        name="turn_features",
    )(info, *shards)


def merge_states(earlier, later):
    return (earlier[0] * later[0], later[0][:, None, None] * earlier[1] + later[1])


def entering(x, axis, backward):
    count = lax.axis_size(axis)
    place = lax.axis_index(axis)
    ahead = count - 1 - place if backward else place
    gathered = tuple(lax.all_gather(a.astype(BF), axis) for a in x)
    state = (jnp.ones_like(x[0]), jnp.zeros_like(x[1]))

    def one(hop, state):
        source = count - 1 - hop if backward else hop
        item = tuple(
            lax.dynamic_index_in_dim(a, source, 0, False).astype(own.dtype)
            for a, own in zip(gathered, x)
        )
        return merge_states(state, item)

    return lax.fori_loop(0, ahead, one, state)[1].astype(BF)


def swap(x, bit, keep=None):
    pairs = [(s, s ^ bit) for s in range(8) if keep is None or keep(s)]
    return lax.ppermute(x, "seq", pairs)


def gather_totals(own):
    place = lax.axis_index("seq")
    held = own[None]
    for bit in (1, 2, 4):
        other = swap(held, bit)
        upper = (place & bit) != 0
        held = jnp.concatenate(
            [jnp.where(upper, other, held), jnp.where(upper, held, other)], axis=0
        )
    return held


def entering_chips(state, totals, backward, first_wait, second_wait):
    place = lax.axis_index("seq")
    core = lax.rem(place, 2)
    half = state.shape[0] // 2
    ahead_of = (lambda bit: (place & bit) == 0) if backward else (lambda bit: (place & bit) != 0)
    decay = jnp.exp(totals)[:, :, None, None]

    def halves(a):
        return lax.dynamic_slice_in_dim(a, core * half, half, 0)

    def join(own, other, bit, own_factor, other_factor):
        late = ahead_of(bit)
        own, other = own.astype(F32), other.astype(F32)
        return jnp.where(late, own_factor * other + own, other_factor * own + other)

    partner = swap(state, 1)
    own_decay, partner_decay = decay[place], decay[place ^ 1]
    chip = join(halves(state), halves(partner), 1, halves(own_decay), halves(partner_decay)).astype(BF)
    beside = after(swap(chip, 2), *first_wait)
    chip_decay = halves(own_decay * partner_decay)
    beside_decay = halves(decay[place ^ 2] * decay[place ^ 3])
    pair = join(chip, beside, 2, chip_decay, beside_decay).astype(BF)
    keep = (lambda s: (s & 4) != 0) if backward else (lambda s: (s & 4) == 0)
    passed = after(swap(pair, 4, keep), *second_wait).astype(F32)
    entered = jnp.where(ahead_of(2), beside_decay * passed + beside.astype(F32), passed).astype(BF)
    other = swap(entered, 1)
    whole = jnp.where(
        core == 0, jnp.concatenate([entered, other]), jnp.concatenate([other, entered])
    )
    step = partner_decay * whole.astype(F32) + partner.astype(F32)
    return jnp.where(ahead_of(1), step.astype(BF), whole)


def line_pairs(count, step, up):
    if up:
        return [(i, i + 1) for i in range(step - 1, count - 1)]
    return [(i, i - 1) for i in range(1, count - step + 1)]


def scatter_pairs(count, step, up):
    if up:
        return [(i, i + 1) for i in range(0, min(step, count - 1))]
    return [(i, i - 1) for i in range(max(1, count - step), count)]


def per_device(features, key_weight, value_weight, queries, log_decay, out_grad):
    tokens, proj = queries.shape
    depth = features.shape[1]
    model = key_weight.shape[0]
    heads = log_decay.shape[1]
    width = proj // heads
    per = 2 if heads % 2 == 0 else 1
    count = lax.axis_size("head")
    blocks = lax.axis_size("seq")
    here = lax.axis_index("head")
    place = lax.axis_index("seq")
    chips = blocks == 8 and model == 8 * 512 and count == 4

    cum = jnp.cumsum(log_decay, axis=0)
    total = cum[-1]
    growth = jnp.exp(cum)
    tail = jnp.exp(total[None, :] - cum)
    grow = jnp.repeat(growth, width, axis=1)
    tails = jnp.repeat(tail, width, axis=1)
    positions = jnp.arange(tokens)
    causal = (positions[:, None] >= positions[None, :])[None]
    cum_t = cum.T
    gap = cum_t[:, :, None] - cum_t[:, None, :]
    decay = jnp.where(causal, jnp.exp(jnp.where(causal, gap, 0.0)), 0.0).astype(BF)
    causal_t = (positions[:, None] <= positions[None, :])[None]
    decay_t = jnp.where(causal_t, jnp.exp(jnp.where(causal_t, -gap, 0.0)), 0.0).astype(BF)
    query_t = (queries.astype(F32) * grow).astype(BF).T

    up = down = features
    ups, downs = [], []

    def rows_of(weight, index):
        return lax.dynamic_slice_in_dim(weight, index * depth, depth, 0)

    key_sum = dot(features, rows_of(key_weight, here))
    value_sum = dot(features, rows_of(value_weight, here))
    for step in range(1, count):
        up = lax.ppermute(up, "head", line_pairs(count, step, True))
        down = lax.ppermute(down, "head", line_pairs(count, step, False))
        ups.append(up)
        downs.append(down)
        if 2 * step >= count:
            index = jnp.where(here >= step, here - step, jnp.minimum(here + step, count - 1))
            shards = [(up + down, index)]
        else:
            shards = [
                (up, jnp.maximum(here - step, 0)),
                (down, jnp.minimum(here + step, count - 1)),
            ]
        if step < count - 1:
            for shard, index in shards:
                key_sum = key_sum + dot(shard, rows_of(key_weight, index))
                value_sum = value_sum + dot(shard, rows_of(value_weight, index))
    totals = gather_totals(total) if chips else total
    key_sum = after(key_sum, totals, decay, decay_t, query_t, grow, tails)
    keys, values, local_state = last_kv(
        (up, down), index[None], key_weight, value_weight, key_sum, value_sum, tails, width, per
    )

    pair_flops = 2 * heads * tokens * tokens * width
    each = functools.partial(per_head, heads=heads, width=width, per=per)
    (mix,) = each(
        local_kernel,
        (queries, keys, values, decay),
        ("col", "col", "col", "dec"),
        (("col", F32),),
        flops=2 * pair_flops,
        name="local_mix",
    )
    if chips:
        chip, core = place // 2, lax.rem(place, 2)
        own_t, other_t = turn_features(jnp.stack([here, core]), (features, *downs, *ups), count)
        incoming = entering_chips(local_state, totals, False, (mix,), (own_t,))
        partner_t = swap(other_t, 1)
    else:
        incoming = entering((jnp.exp(total), local_state.astype(F32)), "seq", False)
    attended, head_grad, local_reverse = each(
        norm_kernel,
        (queries, out_grad, mix, grow, query_t, incoming),
        ("col", "col", "col", "col", "row", "state"),
        (("col", BF), ("col", BF), ("state", BF)),
        flops=pair_flops // 2,
        name="norm_grad",
    )
    (query_grad,) = each(
        back_query_kernel,
        (keys, values, head_grad, decay, grow, incoming),
        ("col", "col", "col", "dec", "col", "state"),
        (("col", BF),),
        flops=2 * pair_flops,
        name="back_query",
    )
    key_local, value_local = each(
        back_keys_kernel,
        (queries, keys, values, head_grad, decay_t),
        ("col", "col", "col", "col", "dec"),
        (("col", F32), ("col", F32)),
        flops=4 * pair_flops,
        name="back_keys",
    )
    if chips:
        outgoing = entering_chips(local_reverse, totals, True, (query_grad,), (key_local,))
    else:
        outgoing = entering((jnp.exp(total), local_reverse.astype(F32)), "seq", True)
    (grads,) = each(
        close_kernel,
        (keys, values, key_local, value_local, tails, outgoing),
        ("col", "col", "col", "col", "col", "state"),
        (("pair", BF),),
        flops=pair_flops // 2,
        name="close_back",
    )

    def term(index, done):
        return feature_term(after(index, *done), grads, key_weight, value_weight, depth)

    def add(*terms):
        return sum(t.astype(F32) for t in terms).astype(BF)

    def scatter_indices(step):
        upward = jnp.minimum(here + count - step, count - 1)
        downward = jnp.maximum(here - count + step, 0)
        return upward, downward, jnp.where(here < step, upward, downward)

    def send(step, up_sum, down_sum):
        return (
            lax.ppermute(up_sum, "head", scatter_pairs(count, step, True)),
            lax.ppermute(down_sum, "head", scatter_pairs(count, step, False)),
        )

    def feature_step(step, up, down, done):
        upward, downward, either = scatter_indices(step)
        if 2 * step <= count:
            own = term(either, done)
            total = own if up is None else add(own, up, down)
            return send(step, total, total), total
        own_up = term(upward, done)
        own_down = term(downward, (own_up,))
        up_sum = add(own_up, up)
        return send(step, up_sum, add(own_down, down)), own_down

    norm = (tokens * blocks) ** (-0.5)
    if not chips:
        up = down = None
        done = (grads,)
        for step in range(1, count):
            (up, down), last = feature_step(step, up, down, done)
            done = (last,)
        feature_grad = add(term(here, done), up, down)
        gathered = lax.all_gather(features, "head", axis=1, tiled=True)
        both = jnp.concatenate([grads[0], grads[1]], axis=1)
        summed = lax.psum_scatter(
            lax.dot_general(gathered, both, TN, preferred_element_type=F32).astype(BF),
            "seq",
            scatter_dimension=0,
            tiled=True,
        ).astype(F32)
        summed = summed * norm
        return attended, query_grad, feature_grad, summed[:, :proj], summed[:, proj:]

    partner_grads = swap(grads, 1)

    def block(target, which, adds, done, kind=BF):
        return weight_term(
            after(target, *done), which, own_t, partner_t, grads, partner_grads, adds, kind
        )

    (up, down), last = feature_step(1, None, None, (grads,))
    key_far = block(chip ^ 3, 0, [], (last,))
    value_far = block(chip ^ 3, 1, [], (key_far,))
    key_near = block(chip ^ 1, 0, [], (value_far,))
    value_near = block(chip ^ 2, 1, [], (key_near,))
    got_key_far, got_value_far = swap(key_far, 2), swap(value_far, 4)
    got_key_near, got_value_near = swap(key_near, 2), swap(value_near, 4)
    (up, down), last = feature_step(2, up, down, (value_near,))
    key_pass = block(chip ^ 2, 0, [got_key_far], (last,))
    value_pass = block(chip ^ 1, 1, [got_value_far], (key_pass,))
    got_key, got_value = swap(key_pass, 4), swap(value_pass, 2)
    (up, down), last = feature_step(3, up, down, (value_pass,))
    feature_own = term(here, (last,))
    key_own = block(chip, 0, [], (feature_own,), F32)
    value_own = block(chip, 1, [], (key_own,), F32)
    feature_grad = add(feature_own, up, down)
    key_out = (key_own + got_key_near.astype(F32) + got_key.astype(F32)) * norm
    value_out = (value_own + got_value_near.astype(F32) + got_value.astype(F32)) * norm
    return attended, query_grad, feature_grad, key_out, value_out


def solution(mesh):
    spread = P("seq", "head")
    return jax.shard_map(
        per_device,
        mesh=mesh,
        in_specs=(spread, P(None, "head"), P(None, "head"), spread, spread, spread),
        out_specs=(spread,) * 5,
        check_vma=False,
    )
```

profile of v0, /device:TPU:0, one launch (start us, length us, event | category | flops | bytes accessed | tf_op | source)
XLA Modules:
  0.0 294.4 jit_solution(2709034845665479003)
XLA Ops:
  1.9 6.6 %collective-permute-start = (bf16[512,1024]{1,0:T(8,128)(2,1)}, bf16[512,1024]{1,0:T(8,128)(2,1)}, u32[]{:S(2)}, u32[]{:S(2)}) collective-permute-start(bf16[512,1024]{1,0:T(8,128)(2,1)} %refs_0_.1), channel_id=1, source_target_pairs={{0,1},{1,2},{2,3},{4,5},{5,6},{6,7},{8,9},{9,10},{10,11},{12,13},{... | collective-permute-start | bytes 3145736 | tf_op jit(solution)/shard_map/ppermute | solution.py:397
  8.5 2.2 reduce-window.6
  12.9 4.6 %fusion.13 = f32[1024,512]{0,1:T(8,128)} fusion(bf16[512,1024]{1,0:T(8,128)(2,1)} %refs_0_.1, bf16[4096,1024]{1,0:T(8,128)(2,1)} %vw_ref.9, s32[]{:T(128)S(6)} %select_n.177), kind=kOutput, calls=%fused_computation.25 | convolution fusion | flops 1073741824 | bytes 5242884 | tf_op jit(solution)/shard_map/dot_general | solution.py:18
  17.5 4.2 %fusion.21 = f32[1024,512]{0,1:T(8,128)} fusion(bf16[512,1024]{1,0:T(8,128)(2,1)S(1)} %copy-done.16, bf16[4096,1024]{1,0:T(8,128)(2,1)} %kw_ref.9, s32[]{:T(128)S(6)} %select_n.177), kind=kOutput, calls=%fused_computation.34 | convolution fusion | flops 1073741824 | bytes 5242884 | tf_op jit(solution)/shard_map/dot_general | solution.py:18
  24.9 6.1 %fusion.6 = (bf16[8,512,512]{2,1,0:T(8,128)(2,1)}, bf16[8,512,512]{2,1,0:T(8,128)(2,1)}) fusion(f32[8,512]{1,0:T(8,128)S(1)} %add_bitcast_fusion.1, pred[512,512]{1,0:T(8,128)(4,1)S(1)} %get-tuple-element.77, pred[512,512]{1,0:T(8,128)(4,1)} %get-tuple-element.78), kind=kLoop, calls=%fused_computation.8 | loop fusion | flops 16777216 | bytes 8929280 | tf_op jit(solution)/shard_map/convert_element_type | solution.py:385
  31.4 2.0 collective-permute-start.7
  35.1 2.0 collective-permute-start.8
  37.7 3.0 %copy_bitcast_fusion = (f32[512,1024]{1,0:T(8,128)}, f32[512,1024]{1,0:T(8,128)}) fusion(f32[64,8,8,128]{3,2,1,0:T(8,128)S(1)} %bitcast.61, f32[64,8,8,128]{3,2,1,0:T(8,128)S(1)} %bitcast.60), kind=kLoop, calls=%fused_computation.9 | loop fusion | bytes 8388608 | tf_op jit(solution)/shard_map/reshape | solution.py:378
  43.1 3.3 %fusion.19 = f32[1024,512]{0,1:T(8,128)S(1)} fusion(bf16[512,1024]{1,0:T(8,128)(2,1)} %collective-permute-done.refs_4_, bf16[4096,1024]{1,0:T(8,128)(2,1)} %kw_ref.9, s32[]{:T(128)S(6)} %select_n.178), kind=kOutput, calls=%fused_computation.32 | convolution fusion | flops 1073741824 | bytes 5242884 | tf_op jit(solution)/shard_map/dot_general | solution.py:18
  46.4 3.3 %fusion.11 = f32[1024,512]{0,1:T(8,128)S(1)} fusion(bf16[512,1024]{1,0:T(8,128)(2,1)} %collective-permute-done.refs_4_, bf16[4096,1024]{1,0:T(8,128)(2,1)} %vw_ref.9, s32[]{:T(128)S(6)} %select_n.178), kind=kOutput, calls=%fused_computation.23 | convolution fusion | flops 1073741824 | bytes 5242884 | tf_op jit(solution)/shard_map/dot_general | solution.py:18
  49.7 2.5 fusion.17
  52.3 2.7 fusion.9
  55.0 12.2 %collective-permute-done.4.refs_2_ = bf16[512,1024]{1,0:T(8,128)(2,1)S(1)} collective-permute-done((bf16[512,1024]{1,0:T(8,128)(2,1)}, bf16[512,1024]{1,0:T(8,128)(2,1)S(1)}, u32[]{:S(2)}, u32[]{:S(2)}) %collective-permute-start.4) | collective-permute-done | bytes 1048608 | tf_op jit(solution)/shard_map/ppermute | solution.py:398
  69.4 2.6 bitcast_add_fusion.1.refs_4_
  72.1 2.6 bitcast_add_fusion.refs_5_
  74.7 17.5 %collective-permute-done.5.refs_1_.refs_3_ = bf16[512,1024]{1,0:T(8,128)(2,1)S(1)} collective-permute-done((bf16[512,1024]{1,0:T(8,128)(2,1)S(1)}, bf16[512,1024]{1,0:T(8,128)(2,1)S(1)}, u32[]{:S(2)}, u32[]{:S(2)}) %collective-permute-start.5) | collective-permute-done | bytes 1048608 | tf_op jit(solution)/shard_map/ppermute | solution.py:398
  93.5 8.3 %last_kv.1 = (bf16[512,1024]{1,0:T(8,128)(2,1)}, bf16[512,1024]{1,0:T(8,128)(2,1)}, bf16[8,128,128]{2,1,0:T(8,128)(2,1)}) custom-call(s32[1]{0:T(128)} %bitcast.index_ref, bf16[512,1024]{1,0:T(8,128)(2,1)} %copy-done.12, bf16[512,1024]{1,0:T(8,128)(2,1)} %copy-done.11, bf16[4096,1024]{1,0:T(8,128)(2,1)} %kw_ref.9, bf16[4096,1024]{1,0:T(8,128)(2,1)} %vw_ref.9, ...), custom_call_target="tpu_custom_call" | custom-call | flops 2147483648 | bytes 10485760 | tf_op jit(solution)/shard_map/last_kv/pallas_call | solution.py:70
  106.3 6.9 %local_mix.1.mix_ref = f32[512,1024]{1,0:T(8,128)} custom-call(bf16[512,1024]{1,0:T(8,128)(2,1)} %q_ref.5, bf16[512,1024]{1,0:T(8,128)(2,1)} %get-tuple-element.34.k_ref, bf16[512,1024]{1,0:T(8,128)(2,1)} %get-tuple-element.35.v_ref, bf16[8,512,512]{2,1,0:T(8,128)(2,1)} %get-tuple-element.67.dec_ref), custom_call_target="tpu_custom_call" | custom-call | flops 1073741824 | bytes 7340032 | tf_op jit(solution)/shard_map/local_mix/pallas_call | solution.py:168
  113.4 2.4 collective-permute-start.11
  116.4 9.3 %turn_features.1 = (bf16[4,512,512]{2,1,0:T(8,128)(2,1)}, bf16[4,512,512]{2,1,0:T(8,128)(2,1)}) custom-call(s32[2]{0:T(128)} %pad_add_fusion.info_ref, bf16[512,1024]{1,0:T(8,128)(2,1)} %refs_0_.1, bf16[512,1024]{1,0:T(8,128)(2,1)} %collective-permute-done.3.refs_1_, bf16[512,1024]{1,0:T(8,128)(2,1)} %copy-done.1, bf16[512,1024]{1,0:T(8,128)(2,1)} %copy-done.11, ...), custom_call_target="tpu_custom_call" | custom-call | bytes 33554432 | tf_op jit(solution)/shard_map/turn_features/pallas_call | solution.py:256
  128.2 5.9 %norm_grad.1 = (bf16[512,1024]{1,0:T(8,128)(2,1)}, bf16[512,1024]{1,0:T(8,128)(2,1)}, bf16[8,128,128]{2,1,0:T(8,128)(2,1)}) custom-call(bf16[512,1024]{1,0:T(8,128)(2,1)} %q_ref.5, bf16[512,1024]{1,0:T(8,128)(2,1)} %g_ref.1, f32[512,1024]{1,0:T(8,128)} %local_mix.1.mix_ref, f32[512,1024]{1,0:T(8,128)} %get-tuple-element.80.grow_ref, ...), custom_call_target="tpu_custom_call" | custom-call | flops 268435456 | bytes 7602176 | tf_op jit(solution)/shard_map/norm_grad/pallas_call | solution.py:168
  137.7 6.8 %back_query.1 = bf16[512,1024]{1,0:T(8,128)(2,1)} custom-call(bf16[512,1024]{1,0:T(8,128)(2,1)} %get-tuple-element.34.k_ref, bf16[512,1024]{1,0:T(8,128)(2,1)} %get-tuple-element.35.v_ref, bf16[512,1024]{1,0:T(8,128)(2,1)} %get-tuple-element.41.hg_ref, bf16[8,512,512]{2,1,0:T(8,128)(2,1)} %get-tuple-element.67.dec_ref, ...), custom_call_target="tpu_custom_call" | custom-call | flops 1073741824 | bytes 9699328 | tf_op jit(solution)/shard_map/back_query/pallas_call | solution.py:168
  145.9 8.6 %back_keys.1 = (f32[512,1024]{1,0:T(8,128)}, f32[512,1024]{1,0:T(8,128)}) custom-call(bf16[512,1024]{1,0:T(8,128)(2,1)} %q_ref.5, bf16[512,1024]{1,0:T(8,128)(2,1)} %get-tuple-element.34.k_ref, bf16[512,1024]{1,0:T(8,128)(2,1)} %get-tuple-element.35.v_ref, bf16[512,1024]{1,0:T(8,128)(2,1)} %get-tuple-element.41.hg_ref, ...), custom_call_target="tpu_custom_call" | custom-call | flops 2147483648 | bytes 8388608 | tf_op jit(solution)/shard_map/back_keys/pallas_call | solution.py:168
  156.9 5.7 %close_back.1.grads_ref.go_ref = bf16[2,512,1024]{2,1,0:T(8,128)(2,1)} custom-call(bf16[512,1024]{1,0:T(8,128)(2,1)} %get-tuple-element.34.k_ref, bf16[512,1024]{1,0:T(8,128)(2,1)} %get-tuple-element.35.v_ref, f32[512,1024]{1,0:T(8,128)} %get-tuple-element.42.kl_ref, f32[512,1024]{1,0:T(8,128)} %get-tuple-element.43.vl_ref, ...), custom_call_target="tpu_custom_call" | custom-call | flops 268435456 | bytes 8650752 | tf_op jit(solution)/shard_map/close_back/pallas_call | solution.py:168
  162.8 6.3 %feature_term.5 = bf16[512,1024]{1,0:T(8,128)(2,1)} custom-call(s32[1]{0:T(128)} %bitcast.16.index_ref, bf16[2,512,1024]{2,1,0:T(8,128)(2,1)} %close_back.1.grads_ref.go_ref, bf16[4096,1024]{1,0:T(8,128)(2,1)} %kw_ref.9, bf16[4096,1024]{1,0:T(8,128)(2,1)} %vw_ref.9), custom_call_target="tpu_custom_call" | custom-call | flops 2147483648 | bytes 6291456 | tf_op jit(solution)/shard_map/feature_term/pallas_call | solution.py:190
  169.8 2.4 collective-permute-start.19
  173.5 4.8 %weight_term.8 = bf16[512,1024]{1,0:T(8,128)(2,1)} custom-call(s32[1]{0:T(128)} %bitcast.17.index_ref, bf16[4,512,512]{2,1,0:T(8,128)(2,1)} %get-tuple-element.38.fo_ref, bf16[4,512,512]{2,1,0:T(8,128)(2,1)} %copy-done, bf16[2,512,1024]{2,1,0:T(8,128)(2,1)} %close_back.1.grads_ref.go_ref, bf16[2,512,1024]{2,1,0:T(8,128)(2,1)} %collective-permute-done.18.gp_ref), custom_call_target="tpu_custom_call" | custom-call | flops 1073741824 | bytes 3145728 | tf_op jit(solution)/shard_map/weight_term/pallas_call | solution.py:219
  179.8 4.8 %weight_term.9 = bf16[512,1024]{1,0:T(8,128)(2,1)} custom-call(s32[1]{0:T(128)} %bitcast.18.index_ref, bf16[4,512,512]{2,1,0:T(8,128)(2,1)} %get-tuple-element.38.fo_ref, bf16[4,512,512]{2,1,0:T(8,128)(2,1)} %copy-done, bf16[2,512,1024]{2,1,0:T(8,128)(2,1)} %close_back.1.grads_ref.go_ref, bf16[2,512,1024]{2,1,0:T(8,128)(2,1)} %collective-permute-done.18.gp_ref), custom_call_target="tpu_custom_call" | custom-call | flops 1073741824 | bytes 3145728 | tf_op jit(solution)/shard_map/weight_term/pallas_call | solution.py:219
  184.6 2.6 collective-permute-start.22
  187.2 4.8 %weight_term.10 = bf16[512,1024]{1,0:T(8,128)(2,1)} custom-call(s32[1]{0:T(128)} %bitcast.19.index_ref, bf16[4,512,512]{2,1,0:T(8,128)(2,1)} %get-tuple-element.38.fo_ref, bf16[4,512,512]{2,1,0:T(8,128)(2,1)} %copy-done, bf16[2,512,1024]{2,1,0:T(8,128)(2,1)} %close_back.1.grads_ref.go_ref, bf16[2,512,1024]{2,1,0:T(8,128)(2,1)} %collective-permute-done.18.gp_ref), custom_call_target="tpu_custom_call" | custom-call | flops 1073741824 | bytes 3145728 | tf_op jit(solution)/shard_map/weight_term/pallas_call | solution.py:219
  192.0 4.8 %weight_term.11 = bf16[512,1024]{1,0:T(8,128)(2,1)} custom-call(s32[1]{0:T(128)} %bitcast.20.index_ref, bf16[4,512,512]{2,1,0:T(8,128)(2,1)} %get-tuple-element.38.fo_ref, bf16[4,512,512]{2,1,0:T(8,128)(2,1)} %copy-done, bf16[2,512,1024]{2,1,0:T(8,128)(2,1)} %close_back.1.grads_ref.go_ref, bf16[2,512,1024]{2,1,0:T(8,128)(2,1)} %collective-permute-done.18.gp_ref), custom_call_target="tpu_custom_call" | custom-call | flops 1073741824 | bytes 3145728 | tf_op jit(solution)/shard_map/weight_term/pallas_call | solution.py:219
  196.8 6.3 %feature_term.6 = bf16[512,1024]{1,0:T(8,128)(2,1)} custom-call(s32[1]{0:T(128)} %bitcast.21.index_ref, bf16[2,512,1024]{2,1,0:T(8,128)(2,1)} %close_back.1.grads_ref.go_ref, bf16[4096,1024]{1,0:T(8,128)(2,1)} %kw_ref.9, bf16[4096,1024]{1,0:T(8,128)(2,1)} %vw_ref.9), custom_call_target="tpu_custom_call" | custom-call | flops 2147483648 | bytes 6291456 | tf_op jit(solution)/shard_map/feature_term/pallas_call | solution.py:190
  203.1 3.1 %add_convert_fusion.3 = bf16[512,1024]{1,0:T(8,128)(2,1)} fusion(bf16[512,1024]{1,0:T(8,128)(2,1)S(1)} %collective-permute-done.20, bf16[512,1024]{1,0:T(8,128)(2,1)} %collective-permute-done.19, bf16[512,1024]{1,0:T(8,128)(2,1)} %feature_term.6), kind=kLoop, calls=%fused_computation.18 | loop fusion | flops 3145728 | bytes 4194304 | tf_op jit(solution)/shard_map/convert_element_type | solution.py:477
  208.3 5.1 %weight_term.12 = bf16[512,1024]{1,0:T(8,128)(2,1)} custom-call(s32[1]{0:T(128)} %bitcast.22.index_ref, bf16[4,512,512]{2,1,0:T(8,128)(2,1)} %get-tuple-element.38.fo_ref, bf16[4,512,512]{2,1,0:T(8,128)(2,1)} %copy-done, bf16[2,512,1024]{2,1,0:T(8,128)(2,1)} %close_back.1.grads_ref.go_ref, bf16[2,512,1024]{2,1,0:T(8,128)(2,1)} %collective-permute-done.18.gp_ref, ...), custom_call_target="tpu_custom_call" | custom-call | flops 1073741824 | bytes 3145728 | tf_op jit(solution)/shard_map/weight_term/pallas_call | solution.py:219
  214.4 5.1 %weight_term.13 = bf16[512,1024]{1,0:T(8,128)(2,1)} custom-call(s32[1]{0:T(128)} %bitcast.23.index_ref, bf16[4,512,512]{2,1,0:T(8,128)(2,1)} %get-tuple-element.38.fo_ref, bf16[4,512,512]{2,1,0:T(8,128)(2,1)} %copy-done, bf16[2,512,1024]{2,1,0:T(8,128)(2,1)} %close_back.1.grads_ref.go_ref, bf16[2,512,1024]{2,1,0:T(8,128)(2,1)} %collective-permute-done.18.gp_ref, ...), custom_call_target="tpu_custom_call" | custom-call | flops 1073741824 | bytes 3145728 | tf_op jit(solution)/shard_map/weight_term/pallas_call | solution.py:219
  219.4 6.3 %feature_term.7 = bf16[512,1024]{1,0:T(8,128)(2,1)} custom-call(s32[1]{0:T(128)} %bitcast.24.index_ref, bf16[2,512,1024]{2,1,0:T(8,128)(2,1)} %close_back.1.grads_ref.go_ref, bf16[4096,1024]{1,0:T(8,128)(2,1)} %kw_ref.9, bf16[4096,1024]{1,0:T(8,128)(2,1)} %vw_ref.9), custom_call_target="tpu_custom_call" | custom-call | flops 2147483648 | bytes 6291456 | tf_op jit(solution)/shard_map/feature_term/pallas_call | solution.py:190
  225.8 6.3 %feature_term.8 = bf16[512,1024]{1,0:T(8,128)(2,1)} custom-call(s32[1]{0:T(128)} %bitcast.25.index_ref, bf16[2,512,1024]{2,1,0:T(8,128)(2,1)} %close_back.1.grads_ref.go_ref, bf16[4096,1024]{1,0:T(8,128)(2,1)} %kw_ref.9, bf16[4096,1024]{1,0:T(8,128)(2,1)} %vw_ref.9), custom_call_target="tpu_custom_call" | custom-call | flops 2147483648 | bytes 6291456 | tf_op jit(solution)/shard_map/feature_term/pallas_call | solution.py:190
  232.1 1.7 add_convert_fusion.1
  236.6 7.1 %collective-permute-start.24 = (bf16[512,1024]{1,0:T(8,128)(2,1)}, bf16[512,1024]{1,0:T(8,128)(2,1)}, u32[]{:S(2)}, u32[]{:S(2)}) collective-permute-start(bf16[512,1024]{1,0:T(8,128)(2,1)} %add_convert_fusion.2), channel_id=1, source_target_pairs={{0,1},{1,2},{2,3},{4,5},{5,6},{6,7},{8,9},{9,10},{10,11},{12,13},{... | collective-permute-start | bytes 3145736 | tf_op jit(solution)/shard_map/ppermute | solution.py:486
  244.2 2.0 collective-permute-start.29
  246.3 15.9 %collective-permute-done.26 = bf16[512,1024]{1,0:T(8,128)(2,1)S(1)} collective-permute-done((bf16[512,1024]{1,0:T(8,128)(2,1)S(1)}, bf16[512,1024]{1,0:T(8,128)(2,1)S(1)}, u32[]{:S(2)}, u32[]{:S(2)}) %collective-permute-start.26) | collective-permute-done | bytes 1048608 | tf_op jit(solution)/shard_map/ppermute | solution.py:487
  263.7 6.3 %feature_term.9 = bf16[512,1024]{1,0:T(8,128)(2,1)} custom-call(s32[1]{0:T(128)} %bitcast.26.index_ref, bf16[2,512,1024]{2,1,0:T(8,128)(2,1)} %close_back.1.grads_ref.go_ref, bf16[4096,1024]{1,0:T(8,128)(2,1)} %kw_ref.9, bf16[4096,1024]{1,0:T(8,128)(2,1)} %vw_ref.9), custom_call_target="tpu_custom_call" | custom-call | flops 2147483648 | bytes 6291456 | tf_op jit(solution)/shard_map/feature_term/pallas_call | solution.py:190
  270.0 4.9 %weight_term.14 = f32[512,1024]{1,0:T(8,128)} custom-call(s32[1]{0:T(128)} %bitcast.27.index_ref, bf16[4,512,512]{2,1,0:T(8,128)(2,1)} %get-tuple-element.38.fo_ref, bf16[4,512,512]{2,1,0:T(8,128)(2,1)} %copy-done, bf16[2,512,1024]{2,1,0:T(8,128)(2,1)} %close_back.1.grads_ref.go_ref, bf16[2,512,1024]{2,1,0:T(8,128)(2,1)} %collective-permute-done.18.gp_ref), custom_call_target="tpu_custom_call" | custom-call | flops 1073741824 | bytes 3145728 | tf_op jit(solution)/shard_map/weight_term/pallas_call | solution.py:219
  274.9 5.1 %weight_term.15 = f32[512,1024]{1,0:T(8,128)} custom-call(s32[1]{0:T(128)} %bitcast.28.index_ref, bf16[4,512,512]{2,1,0:T(8,128)(2,1)} %get-tuple-element.38.fo_ref, bf16[4,512,512]{2,1,0:T(8,128)(2,1)} %copy-done, bf16[2,512,1024]{2,1,0:T(8,128)(2,1)} %close_back.1.grads_ref.go_ref, bf16[2,512,1024]{2,1,0:T(8,128)(2,1)} %collective-permute-done.18.gp_ref), custom_call_target="tpu_custom_call" | custom-call | flops 1073741824 | bytes 3145728 | tf_op jit(solution)/shard_map/weight_term/pallas_call | solution.py:219
  280.1 3.3 %add_convert_fusion = bf16[512,1024]{1,0:T(8,128)(2,1)} fusion(bf16[512,1024]{1,0:T(8,128)(2,1)} %copy-done.15, bf16[512,1024]{1,0:T(8,128)(2,1)} %collective-permute-done.24, bf16[512,1024]{1,0:T(8,128)(2,1)S(1)} %copy-done.9), kind=kLoop, calls=%fused_computation.15 | loop fusion | flops 3145728 | bytes 4194304 | tf_op jit(solution)/shard_map/convert_element_type | solution.py:477
  283.4 3.6 %add_multiply_fusion.1 = f32[512,1024]{1,0:T(8,128)} fusion(bf16[512,1024]{1,0:T(8,128)(2,1)} %collective-permute-done.28, f32[512,1024]{1,0:T(8,128)S(1)} %copy-done.5, bf16[512,1024]{1,0:T(8,128)(2,1)} %collective-permute-done.27), kind=kLoop, calls=%fused_computation.14 | loop fusion | flops 2621440 | bytes 6291456 | tf_op jit(solution)/shard_map/mul | solution.py:543
  286.9 4.1 %collective-permute-done.29 = bf16[512,1024]{1,0:T(8,128)(2,1)} collective-permute-done((bf16[512,1024]{1,0:T(8,128)(2,1)S(1)}, bf16[512,1024]{1,0:T(8,128)(2,1)}, u32[]{:S(2)}, u32[]{:S(2)}) %collective-permute-start.29) | collective-permute-done | bytes 1048608 | tf_op jit(solution)/shard_map/ppermute | solution.py:300
  291.0 3.4 %add_multiply_fusion = f32[512,1024]{1,0:T(8,128)} fusion(bf16[512,1024]{1,0:T(8,128)(2,1)} %collective-permute-done.30, f32[512,1024]{1,0:T(8,128)S(1)} %copy-done.4, bf16[512,1024]{1,0:T(8,128)(2,1)} %collective-permute-done.29), kind=kLoop, calls=%fused_computation.13 | loop fusion | flops 2621440 | bytes 6291456 | tf_op jit(solution)/shard_map/mul | solution.py:544
  (131 shorter events, 41.8 us)
Async XLA Ops:
  0.6 40.1 %collective-permute-start.3 = (bf16[512,1024]{1,0:T(8,128)(2,1)}, bf16[512,1024]{1,0:T(8,128)(2,1)}, u32[]{:S(2)}, u32[]{:S(2)}) collective-permute-start(bf16[512,1024]{1,0:T(8,128)(2,1)} %refs_0_.1), channel_id=1, source_target_pairs={{1,0},{2,1},{3,2},{5,4},{6,5},{7,6},{9,8},{10,9},{11,10},{13,12},{... | collective-permute-start | bytes 3145736 | tf_op jit(solution)/shard_map/ppermute | solution.py:398
  1.9 40.4 %collective-permute-start = (bf16[512,1024]{1,0:T(8,128)(2,1)}, bf16[512,1024]{1,0:T(8,128)(2,1)}, u32[]{:S(2)}, u32[]{:S(2)}) collective-permute-start(bf16[512,1024]{1,0:T(8,128)(2,1)} %refs_0_.1), channel_id=1, source_target_pairs={{0,1},{1,2},{2,3},{4,5},{5,6},{6,7},{8,9},{9,10},{10,11},{12,13},{... | collective-permute-start | bytes 3145736 | tf_op jit(solution)/shard_map/ppermute | solution.py:397
  11.1 19.9 %collective-permute-start.6 = (f32[1,8]{0,1:T(8,128)S(1)}, f32[1,8]{0,1:T(8,128)S(1)}, u32[]{:S(2)}, u32[]{:S(2)}) collective-permute-start(f32[1,8]{0,1:T(8,128)S(1)} %slice.13), channel_id=1, source_target_pairs={{0,4},{4,0},{8,12},{12,8},{16,20},{20,16},{24,28},{28,24},{1,5},{5... | collective-permute-start | bytes 104 | tf_op jit(solution)/shard_map/ppermute | solution.py:300
  12.9 4.6 %copy-start.16 = (bf16[512,1024]{1,0:T(8,128)(2,1)S(1)}, bf16[512,1024]{1,0:T(8,128)(2,1)}, u32[]{:S(2)}) copy-start(bf16[512,1024]{1,0:T(8,128)(2,1)} %refs_0_.1) | copy-start | bytes 3145732
  21.7 1.6 copy-start.3
  31.4 3.6 %collective-permute-start.7 = (f32[2,8]{1,0:T(2,128)S(1)}, f32[2,8]{1,0:T(2,128)S(1)}, u32[]{:S(2)}, u32[]{:S(2)}) collective-permute-start(f32[2,8]{1,0:T(2,128)S(1)} %pad_maximum_fusion.2), channel_id=1, source_target_pairs={{0,8},{4,12},{8,0},{12,4},{16,24},{20,28},{24,16},{28,20},{1,9},{5... | collective-permute-start | bytes 200 | tf_op jit(solution)/shard_map/ppermute | solution.py:300
  35.1 5.6 %collective-permute-start.8 = (f32[4,8]{1,0:T(4,128)S(1)}, f32[4,8]{1,0:T(4,128)S(1)}, u32[]{:S(2)}, u32[]{:S(2)}) collective-permute-start(f32[4,8]{1,0:T(4,128)S(1)} %pad_maximum_fusion.1), channel_id=1, source_target_pairs={{0,16},{4,20},{8,24},{12,28},{16,0},{20,4},{24,8},{28,12},{1,17},{... | collective-permute-start | bytes 392 | tf_op jit(solution)/shard_map/ppermute | solution.py:300
  37.7 12.0 %slice-start = ((s8[8388608]{0:T(1024)(128)(4,1)}), s8[4194304]{0:T(1024)(128)(4,1)S(1)}, s32[]{:S(2)}) async-start(s8[8388608]{0:T(1024)(128)(4,1)} %bitcast.55), calls=%async_computation | async-start | bytes 8388608
  40.7 9.0 %slice-start.1 = ((s8[8388608]{0:T(1024)(128)(4,1)}), s8[4194304]{0:T(1024)(128)(4,1)S(1)}, s32[]{:S(2)}) async-start(s8[8388608]{0:T(1024)(128)(4,1)} %bitcast.55), calls=%async_computation.1 | async-start | bytes 8388608
  40.7 26.5 %collective-permute-start.4 = (bf16[512,1024]{1,0:T(8,128)(2,1)}, bf16[512,1024]{1,0:T(8,128)(2,1)S(1)}, u32[]{:S(2)}, u32[]{:S(2)}) collective-permute-start(bf16[512,1024]{1,0:T(8,128)(2,1)} %collective-permute-done.3.refs_1_), channel_id=1, source_target_pairs={{1,0},{2,1},{5,4},{6,5},{9,8},{10,9},{13,12},{14,13},{17,16},{18,1... | collective-permute-start | bytes 3145736 | tf_op jit(solution)/shard_map/ppermute | solution.py:398
  42.3 26.2 %collective-permute-start.1 = (bf16[512,1024]{1,0:T(8,128)(2,1)}, bf16[512,1024]{1,0:T(8,128)(2,1)S(1)}, u32[]{:S(2)}, u32[]{:S(2)}) collective-permute-start(bf16[512,1024]{1,0:T(8,128)(2,1)} %collective-permute-done.refs_4_), channel_id=1, source_target_pairs={{1,2},{2,3},{5,6},{6,7},{9,10},{10,11},{13,14},{14,15},{17,18},{18... | collective-permute-start | bytes 3145736 | tf_op jit(solution)/shard_map/ppermute | solution.py:397
  43.0 9.2 %slice-start.2 = ((s8[8388608]{0:T(1024)(128)(4,1)}), s8[4194304]{0:T(1024)(128)(4,1)S(1)}, s32[]{:S(2)}) async-start(s8[8388608]{0:T(1024)(128)(4,1)} %bitcast.57), calls=%async_computation.2 | async-start | bytes 8388608
  46.4 5.9 %slice-start.3 = ((s8[8388608]{0:T(1024)(128)(4,1)}), s8[4194304]{0:T(1024)(128)(4,1)S(1)}, s32[]{:S(2)}) async-start(s8[8388608]{0:T(1024)(128)(4,1)} %bitcast.57), calls=%async_computation.3 | async-start | bytes 8388608
  52.3 17.1 %copy-start.7 = (f32[1024,512]{0,1:T(8,128)S(1)}, f32[1024,512]{0,1:T(8,128)}, u32[]{:S(2)}) copy-start(f32[1024,512]{0,1:T(8,128)} %fusion.21) | copy-start | bytes 6291460
  55.0 17.1 %copy-start.6 = (f32[1024,512]{0,1:T(8,128)S(1)}, f32[1024,512]{0,1:T(8,128)}, u32[]{:S(2)}) copy-start(f32[1024,512]{0,1:T(8,128)} %fusion.13) | copy-start | bytes 6291460
  67.2 4.9 %copy-start.1 = (bf16[512,1024]{1,0:T(8,128)(2,1)}, bf16[512,1024]{1,0:T(8,128)(2,1)S(1)}, u32[]{:S(2)}) copy-start(bf16[512,1024]{1,0:T(8,128)(2,1)S(1)} %collective-permute-done.4.refs_2_) | copy-start | bytes 3145732
  67.2 25.0 %collective-permute-start.5 = (bf16[512,1024]{1,0:T(8,128)(2,1)S(1)}, bf16[512,1024]{1,0:T(8,128)(2,1)S(1)}, u32[]{:S(2)}, u32[]{:S(2)}) collective-permute-start(bf16[512,1024]{1,0:T(8,128)(2,1)S(1)} %collective-permute-done.4.refs_2_), channel_id=1, source_target_pairs={{1,0},{5,4},{9,8},{13,12},{17,16},{21,20},{25,24},{29,28}} | collective-permute-start | bytes 3145736 | tf_op jit(solution)/shard_map/ppermute | solution.py:398
  68.5 3.6 %copy-start.2 = (bf16[512,1024]{1,0:T(8,128)(2,1)}, bf16[512,1024]{1,0:T(8,128)(2,1)S(1)}, u32[]{:S(2)}) copy-start(bf16[512,1024]{1,0:T(8,128)(2,1)S(1)} %collective-permute-done.1.refs_5_) | copy-start | bytes 3145732
  68.5 23.7 %collective-permute-start.2 = (bf16[512,1024]{1,0:T(8,128)(2,1)S(1)}, bf16[512,1024]{1,0:T(8,128)(2,1)S(1)}, u32[]{:S(2)}, u32[]{:S(2)}) collective-permute-start(bf16[512,1024]{1,0:T(8,128)(2,1)S(1)} %collective-permute-done.1.refs_5_), channel_id=1, source_target_pairs={{2,3},{6,7},{10,11},{14,15},{18,19},{22,23},{26,27},{30,31}} | collective-permute-start | bytes 3145736 | tf_op jit(solution)/shard_map/ppermute | solution.py:397
  101.9 1.8 collective-permute-start.9
  104.7 8.6 %collective-permute-start.10 = (bf16[4,128,128]{2,1,0:T(8,128)(2,1)S(1)}, bf16[4,128,128]{2,1,0:T(8,128)(2,1)S(1)}, u32[]{:S(2)}, u32[]{:S(2)}) collective-permute-start(bf16[4,128,128]{2,1,0:T(8,128)(2,1)S(1)} %fusion.33), channel_id=1, source_target_pairs={{0,8},{4,12},{8,0},{12,4},{16,24},{20,28},{24,16},{28,20},{1,9},{5... | collective-permute-start | bytes 393224 | tf_op jit(solution)/shard_map/ppermute | solution.py:300
  113.4 12.3 %collective-permute-start.11 = (bf16[4,128,128]{2,1,0:T(8,128)(2,1)S(1)}, bf16[4,128,128]{2,1,0:T(8,128)(2,1)S(1)}, u32[]{:S(2)}, u32[]{:S(2)}) collective-permute-start(bf16[4,128,128]{2,1,0:T(8,128)(2,1)S(1)} %fusion.35), channel_id=1, source_target_pairs={{0,16},{4,20},{8,24},{12,28},{1,17},{5,21},{9,25},{13,29},{2,18},{... | collective-permute-start | bytes 393224 | tf_op jit(solution)/shard_map/ppermute | solution.py:300
  116.4 9.6 %copy-start.10 = (bf16[1024,512]{0,1:T(8,128)(2,1)S(1)}, bf16[1024,512]{0,1:T(8,128)(2,1)}, u32[]{:S(2)}) copy-start(bf16[1024,512]{0,1:T(8,128)(2,1)} %fusion.27) | copy-start | bytes 3145732
  125.9 1.4 collective-permute-start.12
  134.1 1.9 collective-permute-start.13
  137.0 7.4 %collective-permute-start.14 = (bf16[4,128,128]{2,1,0:T(8,128)(2,1)S(1)}, bf16[4,128,128]{2,1,0:T(8,128)(2,1)S(1)}, u32[]{:S(2)}, u32[]{:S(2)}) collective-permute-start(bf16[4,128,128]{2,1,0:T(8,128)(2,1)S(1)} %fusion.38), channel_id=1, source_target_pairs={{0,8},{4,12},{8,0},{12,4},{16,24},{20,28},{24,16},{28,20},{1,9},{5... | collective-permute-start | bytes 393224 | tf_op jit(solution)/shard_map/ppermute | solution.py:300
  144.6 9.9 %collective-permute-start.15 = (bf16[4,128,128]{2,1,0:T(8,128)(2,1)S(1)}, bf16[4,128,128]{2,1,0:T(8,128)(2,1)S(1)}, u32[]{:S(2)}, u32[]{:S(2)}) collective-permute-start(bf16[4,128,128]{2,1,0:T(8,128)(2,1)S(1)} %fusion.40), channel_id=1, source_target_pairs={{16,0},{20,4},{24,8},{28,12},{17,1},{21,5},{25,9},{29,13},{18,2},{... | collective-permute-start | bytes 393224 | tf_op jit(solution)/shard_map/ppermute | solution.py:300
  154.6 1.4 collective-permute-start.16
  154.8 17.4 %collective-permute-start.17 = (bf16[4,512,512]{2,1,0:T(8,128)(2,1)}, bf16[4,512,512]{2,1,0:T(8,128)(2,1)S(1)}, u32[]{:S(2)}, u32[]{:S(2)}) collective-permute-start(bf16[4,512,512]{2,1,0:T(8,128)(2,1)} %get-tuple-element.49), channel_id=1, source_target_pairs={{0,4},{4,0},{8,12},{12,8},{16,20},{20,16},{24,28},{28,24},{1,5},{5... | collective-permute-start | bytes 6291464 | tf_op jit(solution)/shard_map/ppermute | solution.py:300
  162.6 9.6 %collective-permute-start.18 = (bf16[2,512,1024]{2,1,0:T(8,128)(2,1)}, bf16[2,512,1024]{2,1,0:T(8,128)(2,1)}, u32[]{:S(2)}, u32[]{:S(2)}) collective-permute-start(bf16[2,512,1024]{2,1,0:T(8,128)(2,1)} %close_back.1.grads_ref.go_ref), channel_id=1, source_target_pairs={{0,4},{4,0},{8,12},{12,8},{16,20},{20,16},{24,28},{28,24},{1,5},{5... | collective-permute-start | bytes 6291464 | tf_op jit(solution)/shard_map/ppermute | solution.py:300
  169.0 34.0 %collective-permute-start.20 = (bf16[512,1024]{1,0:T(8,128)(2,1)}, bf16[512,1024]{1,0:T(8,128)(2,1)S(1)}, u32[]{:S(2)}, u32[]{:S(2)}) collective-permute-start(bf16[512,1024]{1,0:T(8,128)(2,1)} %feature_term.5), channel_id=1, source_target_pairs={{3,2},{7,6},{11,10},{15,14},{19,18},{23,22},{27,26},{31,30}} | collective-permute-start | bytes 3145736 | tf_op jit(solution)/shard_map/ppermute | solution.py:487
  169.8 33.3 %collective-permute-start.19 = (bf16[512,1024]{1,0:T(8,128)(2,1)}, bf16[512,1024]{1,0:T(8,128)(2,1)}, u32[]{:S(2)}, u32[]{:S(2)}) collective-permute-start(bf16[512,1024]{1,0:T(8,128)(2,1)} %feature_term.5), channel_id=1, source_target_pairs={{0,1},{4,5},{8,9},{12,13},{16,17},{20,21},{24,25},{28,29}} | collective-permute-start | bytes 3145736 | tf_op jit(solution)/shard_map/ppermute | solution.py:486
  178.3 30.0 %collective-permute-start.21 = (bf16[512,1024]{1,0:T(8,128)(2,1)}, bf16[512,1024]{1,0:T(8,128)(2,1)}, u32[]{:S(2)}, u32[]{:S(2)}) collective-permute-start(bf16[512,1024]{1,0:T(8,128)(2,1)} %weight_term.8), channel_id=1, source_target_pairs={{0,8},{4,12},{8,0},{12,4},{16,24},{20,28},{24,16},{28,20},{1,9},{5... | collective-permute-start | bytes 3145736 | tf_op jit(solution)/shard_map/ppermute | solution.py:300
  184.6 28.9 %collective-permute-start.22 = (bf16[512,1024]{1,0:T(8,128)(2,1)}, bf16[512,1024]{1,0:T(8,128)(2,1)S(1)}, u32[]{:S(2)}, u32[]{:S(2)}) collective-permute-start(bf16[512,1024]{1,0:T(8,128)(2,1)} %weight_term.9), channel_id=1, source_target_pairs={{0,16},{4,20},{8,24},{12,28},{16,0},{20,4},{24,8},{28,12},{1,17},{... | collective-permute-start | bytes 3145736 | tf_op jit(solution)/shard_map/ppermute | solution.py:300
  206.2 25.8 %collective-permute-start.25 = (bf16[512,1024]{1,0:T(8,128)(2,1)}, bf16[512,1024]{1,0:T(8,128)(2,1)S(1)}, u32[]{:S(2)}, u32[]{:S(2)}) collective-permute-start(bf16[512,1024]{1,0:T(8,128)(2,1)} %add_convert_fusion.3), channel_id=1, source_target_pairs={{2,1},{3,2},{6,5},{7,6},{10,9},{11,10},{14,13},{15,14},{18,17},{19... | collective-permute-start | bytes 3145736 | tf_op jit(solution)/shard_map/ppermute | solution.py:487
  207.0 28.3 %collective-permute-start.23 = (bf16[512,1024]{1,0:T(8,128)(2,1)}, bf16[512,1024]{1,0:T(8,128)(2,1)S(1)}, u32[]{:S(2)}, u32[]{:S(2)}) collective-permute-start(bf16[512,1024]{1,0:T(8,128)(2,1)} %add_convert_fusion.3), channel_id=1, source_target_pairs={{0,1},{1,2},{4,5},{5,6},{8,9},{9,10},{12,13},{13,14},{16,17},{17,1... | collective-permute-start | bytes 3145736 | tf_op jit(solution)/shard_map/ppermute | solution.py:486
  232.1 3.2 %copy-start.8 = (bf16[512,1024]{1,0:T(8,128)(2,1)S(1)}, bf16[512,1024]{1,0:T(8,128)(2,1)}, u32[]{:S(2)}) copy-start(bf16[512,1024]{1,0:T(8,128)(2,1)} %feature_term.7) | copy-start | bytes 3145732
  233.8 9.9 %copy-start.14 = (bf16[512,1024]{1,0:T(8,128)(2,1)S(1)}, bf16[512,1024]{1,0:T(8,128)(2,1)}, u32[]{:S(2)}) copy-start(bf16[512,1024]{1,0:T(8,128)(2,1)} %weight_term.10) | copy-start | bytes 3145732
  233.8 10.5 %copy-start.13 = (bf16[512,1024]{1,0:T(8,128)(2,1)S(1)}, bf16[512,1024]{1,0:T(8,128)(2,1)}, u32[]{:S(2)}) copy-start(bf16[512,1024]{1,0:T(8,128)(2,1)} %weight_term.11) | copy-start | bytes 3145732
  233.8 28.4 %collective-permute-start.26 = (bf16[512,1024]{1,0:T(8,128)(2,1)S(1)}, bf16[512,1024]{1,0:T(8,128)(2,1)S(1)}, u32[]{:S(2)}, u32[]{:S(2)}) collective-permute-start(bf16[512,1024]{1,0:T(8,128)(2,1)S(1)} %add_convert_fusion.1), channel_id=1, source_target_pairs={{1,0},{2,1},{3,2},{5,4},{6,5},{7,6},{9,8},{10,9},{11,10},{13,12},{... | collective-permute-start | bytes 3145736 | tf_op jit(solution)/shard_map/ppermute | solution.py:487
  236.6 43.4 %collective-permute-start.24 = (bf16[512,1024]{1,0:T(8,128)(2,1)}, bf16[512,1024]{1,0:T(8,128)(2,1)}, u32[]{:S(2)}, u32[]{:S(2)}) collective-permute-start(bf16[512,1024]{1,0:T(8,128)(2,1)} %add_convert_fusion.2), channel_id=1, source_target_pairs={{0,1},{1,2},{2,3},{4,5},{5,6},{6,7},{8,9},{9,10},{10,11},{12,13},{... | collective-permute-start | bytes 3145736 | tf_op jit(solution)/shard_map/ppermute | solution.py:486
  243.7 39.7 %collective-permute-start.27 = (bf16[512,1024]{1,0:T(8,128)(2,1)S(1)}, bf16[512,1024]{1,0:T(8,128)(2,1)}, u32[]{:S(2)}, u32[]{:S(2)}) collective-permute-start(bf16[512,1024]{1,0:T(8,128)(2,1)S(1)} %copy-done.14), channel_id=1, source_target_pairs={{0,8},{4,12},{8,0},{12,4},{16,24},{20,28},{24,16},{28,20},{1,9},{5... | collective-permute-start | bytes 3145736 | tf_op jit(solution)/shard_map/ppermute | solution.py:300
  244.2 39.1 %collective-permute-start.28 = (bf16[512,1024]{1,0:T(8,128)(2,1)}, bf16[512,1024]{1,0:T(8,128)(2,1)}, u32[]{:S(2)}, u32[]{:S(2)}) collective-permute-start(bf16[512,1024]{1,0:T(8,128)(2,1)} %weight_term.12), channel_id=1, source_target_pairs={{0,16},{4,20},{8,24},{12,28},{16,0},{20,4},{24,8},{28,12},{1,17},{... | collective-permute-start | bytes 3145736 | tf_op jit(solution)/shard_map/ppermute | solution.py:300
  244.2 46.8 %collective-permute-start.29 = (bf16[512,1024]{1,0:T(8,128)(2,1)S(1)}, bf16[512,1024]{1,0:T(8,128)(2,1)}, u32[]{:S(2)}, u32[]{:S(2)}) collective-permute-start(bf16[512,1024]{1,0:T(8,128)(2,1)S(1)} %copy-done.13), channel_id=1, source_target_pairs={{0,16},{4,20},{8,24},{12,28},{16,0},{20,4},{24,8},{28,12},{1,17},{... | collective-permute-start | bytes 3145736 | tf_op jit(solution)/shard_map/ppermute | solution.py:300
  263.2 27.9 %collective-permute-start.30 = (bf16[512,1024]{1,0:T(8,128)(2,1)}, bf16[512,1024]{1,0:T(8,128)(2,1)}, u32[]{:S(2)}, u32[]{:S(2)}) collective-permute-start(bf16[512,1024]{1,0:T(8,128)(2,1)} %weight_term.13), channel_id=1, source_target_pairs={{0,8},{4,12},{8,0},{12,4},{16,24},{20,28},{24,16},{28,20},{1,9},{5... | collective-permute-start | bytes 3145736 | tf_op jit(solution)/shard_map/ppermute | solution.py:300
  274.9 5.1 %copy-start.9 = (bf16[512,1024]{1,0:T(8,128)(2,1)S(1)}, bf16[512,1024]{1,0:T(8,128)(2,1)}, u32[]{:S(2)}) copy-start(bf16[512,1024]{1,0:T(8,128)(2,1)} %feature_term.9) | copy-start | bytes 3145732
  280.1 3.3 %copy-start.5 = (f32[512,1024]{1,0:T(8,128)S(1)}, f32[512,1024]{1,0:T(8,128)}, u32[]{:S(2)}) copy-start(f32[512,1024]{1,0:T(8,128)} %weight_term.14) | copy-start | bytes 6291460
  283.4 7.7 %copy-start.4 = (f32[512,1024]{1,0:T(8,128)S(1)}, f32[512,1024]{1,0:T(8,128)}, u32[]{:S(2)}) copy-start(f32[512,1024]{1,0:T(8,128)} %weight_term.15) | copy-start | bytes 6291460
  (5 other events, 5.6 us)
where the time goes:
time: 296 us; the launch traced here: 294 us
  Pallas kernels  122 us (41%)
  waiting for transfers between devices  55.1 us (19%)
  starting transfers between devices  44.5 us (15%)
  other arithmetic  32.8 us (11%)
  matrix products  25.8 us (9%)
  local copies, waits for them, and re-layouts  12.7 us (4%)
    pallas_call x8, Pallas kernels, weight_term(): pl.pallas_call(functools.partial(weight_kernel, len(adds)), grid_spec=plt...  39.3 us
    pallas_call x5, Pallas kernels, per_head(): pl.pallas_call(functools.partial(kernel, width), grid=(heads // per,), in...  33.9 us
    pallas_call x5, Pallas kernels, feature_term(): pl.pallas_call(feature_kernel, grid_spec=pltpu.PrefetchScalarGridSpec(num...  31.5 us
    ppermute x3, waiting for transfers between devices, per_device(): down = lax.ppermute(down, 'head', line_pairs(count, step, False))  29.7 us
    dot_general x8, matrix products, dot(): return jnp.dot(a, b, preferred_element_type=F32)  25.8 us
    ppermute x19, starting transfers between devices, swap(): return lax.ppermute(x, 'seq', pairs)  18.5 us
    ppermute x3, waiting for transfers between devices, send(): lax.ppermute(down_sum, 'head', scatter_pairs(count, step, False))  16 us
    ppermute x3, starting transfers between devices, send(): lax.ppermute(up_sum, 'head', scatter_pairs(count, step, True))  10.8 us
  transfers between devices with their start and end apart: 31, of which 8 were waited for; matrix products, arithmetic and copies ran while one was open for 20% of the time, Pallas kernels for 37%

commit v1 on v0

v1 whole, which is shorter than its diff:
```python
import functools

import jax
import jax.numpy as jnp
from jax import lax
from jax.experimental import pallas as pl
from jax.experimental.pallas import tpu as pltpu
from jax.sharding import PartitionSpec as P

BF = jnp.bfloat16
F32 = jnp.float32
NT = (((1,), (1,)), ((), ()))
TN = (((0,), (0,)), ((), ()))
MIB = 1024 * 1024


def dot(a, b):
    return jnp.dot(a, b, preferred_element_type=F32)


def dot_nt(a, b):
    return lax.dot_general(a, b, NT, preferred_element_type=F32)


def dot_tn(a, b):
    return lax.dot_general(a, b, TN, preferred_element_type=F32)


def params(limit=16):
    return pltpu.CompilerParams(vmem_limit_bytes=limit * MIB)


def after(x, *done):
    return lax.optimization_barrier((x, *done))[0]


def after_all(*arrays):
    return lax.optimization_barrier(arrays)


SMALL = pl.CostEstimate(flops=1, bytes_accessed=1, transcendentals=0)


def tiles(tokens, causal):
    tile = min(256, tokens)
    for row in range(tokens // tile):
        first, last = row * tile, (row + 1) * tile
        yield slice(first, last), slice(0, last) if causal else slice(first, tokens)


def column(cum_ref, head):
    lanes = lax.broadcasted_iota(jnp.int32, cum_ref.shape, 1)
    return jnp.sum(jnp.where(lanes == head, cum_ref[...], 0.0), axis=1, keepdims=True)


def decay_tile(across, down, rows, seen, causal):
    shape = (rows.stop - rows.start, seen.stop - seen.start)
    one = rows.start + lax.broadcasted_iota(jnp.int32, shape, 0)
    two = seen.start + lax.broadcasted_iota(jnp.int32, shape, 1)
    gap = down[rows] - across[:, seen]
    if causal:
        return jnp.where(two <= one, jnp.exp(gap), 0.0)
    return jnp.where(one <= two, jnp.exp(-gap), 0.0)


def heads_of(per, width):
    for i in range(per):
        yield i, pl.program_id(0) * per + i, slice(i * width, (i + 1) * width)


def state_kernel(width, per, cum_ref, k_ref, v_ref, s_ref):
    for i, head, cut in heads_of(per, width):
        down = column(cum_ref, head)
        tail = jnp.exp(down[-1:] - down)
        scaled = (k_ref[:, cut].astype(F32) * tail).astype(BF)
        s_ref[i] = dot_tn(scaled, v_ref[:, cut]).astype(BF)


def local_kernel(width, per, cum_ref, cumt_ref, q_ref, k_ref, v_ref, mix_ref):
    for i, head, cut in heads_of(per, width):
        down, across = column(cum_ref, head), cumt_ref[pl.ds(head, 1), :]
        for rows, seen in tiles(q_ref.shape[0], True):
            scores = dot_nt(q_ref[rows, cut], k_ref[seen, cut])
            weights = (scores * decay_tile(across, down, rows, seen, True)).astype(BF)
            mix_ref[rows, cut] = dot(weights, v_ref[seen, cut]).astype(mix_ref.dtype)


def norm_kernel(width, per, cum_ref, q_ref, g_ref, mix_ref, s_ref, att_ref, hg_ref, r_ref):
    for i, head, cut in heads_of(per, width):
        grow = jnp.exp(column(cum_ref, head))
        carried = grow * dot(q_ref[:, cut], s_ref[i])
        mixed = mix_ref[:, cut].astype(F32) + carried
        grad = g_ref[:, cut].astype(F32)
        scale = lax.rsqrt(jnp.mean(mixed * mixed, axis=-1, keepdims=True) + 1e-06)
        projection = jnp.mean(grad * mixed, axis=-1, keepdims=True)
        att_ref[:, cut] = (mixed * scale).astype(BF)
        head_grad = (scale * grad - mixed * (scale * scale * scale * projection)).astype(BF)
        hg_ref[:, cut] = head_grad
        grown = (q_ref[:, cut].astype(F32) * grow).astype(BF)
        r_ref[i] = dot_tn(grown, head_grad).astype(BF)


def back_query_kernel(width, per, cum_ref, cumt_ref, k_ref, v_ref, hg_ref, s_ref, qg_ref):
    for i, head, cut in heads_of(per, width):
        down, across = column(cum_ref, head), cumt_ref[pl.ds(head, 1), :]
        grow = jnp.exp(down)
        for rows, seen in tiles(k_ref.shape[0], True):
            pairs = dot_nt(hg_ref[rows, cut], v_ref[seen, cut])
            pairs = (pairs * decay_tile(across, down, rows, seen, True)).astype(BF)
            carried = grow[rows] * dot_nt(hg_ref[rows, cut], s_ref[i])
            qg_ref[rows, cut] = (dot(pairs, k_ref[seen, cut]) + carried).astype(BF)


def back_keys_kernel(width, per, cum_ref, cumt_ref, q_ref, k_ref, v_ref, hg_ref, kg_ref, vg_ref):
    for i, head, cut in heads_of(per, width):
        down, across = column(cum_ref, head), cumt_ref[pl.ds(head, 1), :]
        for rows, seen in tiles(q_ref.shape[0], False):
            decay = decay_tile(across, down, rows, seen, False)
            pairs = (dot_nt(v_ref[rows, cut], hg_ref[seen, cut]) * decay).astype(BF)
            kg_ref[rows, cut] = dot(pairs, q_ref[seen, cut]).astype(kg_ref.dtype)
            weights = (dot_nt(k_ref[rows, cut], q_ref[seen, cut]) * decay).astype(BF)
            vg_ref[rows, cut] = dot(weights, hg_ref[seen, cut]).astype(vg_ref.dtype)


def close_kernel(width, per, cum_ref, k_ref, v_ref, kl_ref, vl_ref, r_ref, kg_ref, vg_ref):
    for i, head, cut in heads_of(per, width):
        down = column(cum_ref, head)
        tail = jnp.exp(down[-1:] - down)
        key_carried = tail * dot_nt(v_ref[:, cut], r_ref[i])
        value_carried = tail * dot(k_ref[:, cut], r_ref[i])
        kg_ref[:, cut] = (kl_ref[:, cut].astype(F32) + key_carried).astype(BF)
        vg_ref[:, cut] = (vl_ref[:, cut].astype(F32) + value_carried).astype(BF)


def per_head(kernel, args, kinds, outs, tokens, heads, width, per, name, limit=60):
    specs = {
        "cum": pl.BlockSpec((tokens, heads), lambda j: (0, 0)),
        "cumt": pl.BlockSpec((heads, tokens), lambda j: (0, 0)),
        "col": pl.BlockSpec((tokens, width * per), lambda j: (0, j)),
        "state": pl.BlockSpec((per, width, width), lambda j: (j, 0, 0)),
    }
    shapes = {"col": (tokens, heads * width), "state": (heads, width, width)}
    return pl.pallas_call(
        functools.partial(kernel, width, per),
        grid=(heads // per,),
        in_specs=[specs[k] for k in kinds],
        out_specs=[specs[k] for k in outs],
        out_shape=[jax.ShapeDtypeStruct(shapes[k], BF) for k in outs],
        compiler_params=params(limit),
        cost_estimate=SMALL,
        name=name,
    )(*args)


def feature_kernel(count, index_ref, kg_ref, vg_ref, kw_ref, vw_ref, *refs):
    total = dot_nt(kg_ref[...], kw_ref[...]) + dot_nt(vg_ref[...], vw_ref[...])
    for r in refs[:count]:
        total += r[...].astype(F32)
    refs[count][0] = total.astype(BF)


def feature_terms(indices, key_grad, value_grad, key_weight, value_weight, adds, span):
    tokens, proj = key_grad.shape
    tile = min(512, span)
    steps = span // tile
    whole = pl.BlockSpec((tokens, proj), lambda i, j, d: (0, 0))
    weight = pl.BlockSpec((tile, proj), lambda i, j, d: (d[i] * steps + j, 0))
    number = indices.shape[0]
    return pl.pallas_call(
        functools.partial(feature_kernel, len(adds)),
        grid_spec=pltpu.PrefetchScalarGridSpec(
            num_scalar_prefetch=1,
            grid=(number, steps),
            in_specs=[whole, whole, weight, weight]
            + [pl.BlockSpec((tokens, tile), lambda i, j, d: (0, j))] * len(adds),
            out_specs=pl.BlockSpec((1, tokens, tile), lambda i, j, d: (i, 0, j)),
        ),
        out_shape=jax.ShapeDtypeStruct((number, tokens, span), BF),
        compiler_params=params(60),
        cost_estimate=SMALL,
        name="feature_terms",
    )(indices, key_grad, value_grad, key_weight, value_weight, *adds)


def weight_kernel(index_ref, fo_ref, fp_ref, go_ref, gp_ref, out_ref):
    total = dot(fo_ref[0], go_ref[...]) + dot(fp_ref[0], gp_ref[...])
    out_ref[0] = total.astype(out_ref.dtype)


def weight_terms(slots, own_t, partner_t, grad, partner_grad, kind):
    tokens, proj = grad.shape
    span = own_t.shape[1]
    number = slots.shape[0]
    tile = min(512, proj)
    rows = pl.BlockSpec((1, span, tokens), lambda j, i, d: (d[i], 0, 0))
    cols = pl.BlockSpec((tokens, tile), lambda j, i, d: (0, j))
    return pl.pallas_call(
        weight_kernel,
        grid_spec=pltpu.PrefetchScalarGridSpec(
            num_scalar_prefetch=1,
            grid=(proj // tile, number),
            in_specs=[rows, rows, cols, cols],
            out_specs=pl.BlockSpec((1, span, tile), lambda j, i, d: (i, 0, j)),
        ),
        out_shape=jax.ShapeDtypeStruct((number, span, proj), kind),
        compiler_params=params(60),
        cost_estimate=SMALL,
        name="weight_terms",
    )(slots, own_t, partner_t, grad, partner_grad)


def turn_kernel(aliased, core_ref, *refs):
    shards, (own_ref, other_ref, held, turned, sem) = refs[aliased:-5], refs[-5:]
    core = core_ref[0]
    for i, shard in enumerate(shards):

        @pl.when(pl.program_id(0) == i)
        def _():
            copy = pltpu.make_async_copy(shard, held, sem)
            copy.start()
            copy.wait()

    turned[...] = held[...].T
    rows = own_ref.shape[1]
    own_ref[0] = turned[pl.ds(pl.multiple_of(core * rows, rows), rows), :]
    other_ref[0] = turned[pl.ds(pl.multiple_of((1 - core) * rows, rows), rows), :]


def turn_features(core, shards, first, slots, held=()):
    tokens, depth = shards[0].shape
    half = pl.BlockSpec((1, depth // 2, tokens), lambda j, d: (first + j, 0, 0))
    aliased = len(held)
    return pl.pallas_call(
        functools.partial(turn_kernel, aliased),
        grid_spec=pltpu.PrefetchScalarGridSpec(
            num_scalar_prefetch=1,
            grid=(len(shards),),
            in_specs=[pl.BlockSpec(memory_space=pl.ANY)] * (aliased + len(shards)),
            out_specs=[half, half],
            scratch_shapes=[
                pltpu.VMEM((tokens, depth), BF),
                pltpu.VMEM((depth, tokens), BF),
                pltpu.SemaphoreType.DMA,
            ],
        ),
        out_shape=[jax.ShapeDtypeStruct((slots, depth // 2, tokens), BF)] * 2,
        input_output_aliases={1 + i: i for i in range(aliased)},
        compiler_params=params(),
        cost_estimate=SMALL,
        name="turn_features",
    )(core[None], *held, *shards)


def merge_states(earlier, later):
    return (earlier[0] * later[0], later[0][:, None, None] * earlier[1] + later[1])


def entering(x, axis, backward):
    count = lax.axis_size(axis)
    place = lax.axis_index(axis)
    ahead = count - 1 - place if backward else place
    gathered = tuple(lax.all_gather(a.astype(BF), axis) for a in x)
    state = (jnp.ones_like(x[0]), jnp.zeros_like(x[1]))

    def one(hop, state):
        source = count - 1 - hop if backward else hop
        item = tuple(
            lax.dynamic_index_in_dim(a, source, 0, False).astype(own.dtype)
            for a, own in zip(gathered, x)
        )
        return merge_states(state, item)

    return lax.fori_loop(0, ahead, one, state)[1].astype(BF)


def swap(x, bit, keep=None):
    pairs = [(s, s ^ bit) for s in range(8) if keep is None or keep(s)]
    return lax.ppermute(x, "seq", pairs)


def gather_totals(own):
    place = lax.axis_index("seq")
    held = own[None]
    for bit in (1, 2, 4):
        other = swap(held, bit)
        upper = (place & bit) != 0
        held = jnp.concatenate(
            [jnp.where(upper, other, held), jnp.where(upper, held, other)], axis=0
        )
    return held


def entering_chips(state, totals, backward, first_wait, second_wait):
    place = lax.axis_index("seq")
    core = lax.rem(place, 2)
    half = state.shape[0] // 2
    ahead_of = (lambda bit: (place & bit) == 0) if backward else (lambda bit: (place & bit) != 0)
    decay = jnp.exp(totals)[:, :, None, None]

    def halves(a):
        return lax.dynamic_slice_in_dim(a, core * half, half, 0)

    def join(own, other, bit, own_factor, other_factor):
        late = ahead_of(bit)
        own, other = own.astype(F32), other.astype(F32)
        return jnp.where(late, own_factor * other + own, other_factor * own + other)

    partner = swap(state, 1)
    own_decay, partner_decay = decay[place], decay[place ^ 1]
    chip = join(halves(state), halves(partner), 1, halves(own_decay), halves(partner_decay)).astype(BF)
    beside = after(swap(chip, 2), *first_wait)
    chip_decay = halves(own_decay * partner_decay)
    beside_decay = halves(decay[place ^ 2] * decay[place ^ 3])
    pair = join(chip, beside, 2, chip_decay, beside_decay).astype(BF)
    keep = (lambda s: (s & 4) != 0) if backward else (lambda s: (s & 4) == 0)
    passed = after(swap(pair, 4, keep), *second_wait).astype(F32)
    entered = jnp.where(ahead_of(2), beside_decay * passed + beside.astype(F32), passed).astype(BF)
    other = swap(entered, 1)
    whole = jnp.where(
        core == 0, jnp.concatenate([entered, other]), jnp.concatenate([other, entered])
    )
    step = partner_decay * whole.astype(F32) + partner.astype(F32)
    return jnp.where(ahead_of(1), step.astype(BF), whole)


def line_pairs(count, step, up):
    if up:
        return [(i, i + 1) for i in range(step - 1, count - 1)]
    return [(i, i - 1) for i in range(1, count - step + 1)]


def scatter_pairs(count, step, up):
    if up:
        return [(i, i + 1) for i in range(0, min(step, count - 1))]
    return [(i, i - 1) for i in range(max(1, count - step), count)]


def per_device(features, key_weight, value_weight, queries, log_decay, out_grad):
    tokens, proj = queries.shape
    depth = features.shape[1]
    model = key_weight.shape[0]
    heads = log_decay.shape[1]
    width = proj // heads
    per = 2 if heads % 2 == 0 else 1
    count = lax.axis_size("head")
    blocks = lax.axis_size("seq")
    here = lax.axis_index("head")
    place = lax.axis_index("seq")
    chips = blocks == 8 and model == 8 * 512 and count == 4

    cum = jnp.cumsum(log_decay, axis=0)
    cum_t = cum.T
    total = cum[-1]

    up = down = features

    def rows_of(weight, index):
        return lax.dynamic_slice_in_dim(weight, index * depth, depth, 0)

    def project(sums, shard, index):
        key_part = dot(shard, rows_of(key_weight, index))
        value_part = dot(shard, rows_of(value_weight, index))
        return [key_part, value_part] if sums is None else [sums[0] + key_part, sums[1] + value_part]

    if chips:
        core = lax.rem(place, 2)
        totals = gather_totals(total)
    sums = project(None, features, here)
    slots = [features]
    turned = ()
    for step in range(1, count):
        up = lax.ppermute(up, "head", line_pairs(count, step, True))
        down = lax.ppermute(down, "head", line_pairs(count, step, False))
        if chips and step == count - 2:
            turned = turn_features(core, slots, 0, 5)
            up, down, sums, turned, totals = after_all(up, down, sums, turned, totals)
        else:
            up, down, sums = after_all(up, down, sums)
        if 2 * step >= count:
            index = jnp.where(here >= step, here - step, jnp.minimum(here + step, count - 1))
            shards = [(up + down, index)]
        else:
            shards = [
                (down, jnp.minimum(here + step, count - 1)),
                (up, jnp.maximum(here - step, 0)),
            ]
        slots += [shard for shard, _ in shards]
        for shard, index in shards:
            sums = project(sums, shard, index)
    key_sum, value_sum = sums
    keys, values = key_sum.astype(BF), value_sum.astype(BF)

    each = functools.partial(per_head, tokens=tokens, heads=heads, width=width, per=per)
    (local_state,) = each(
        state_kernel,
        (cum, keys, values),
        ("cum", "col", "col"),
        ("state",),
        name="local_state",
        limit=16,
    )
    (mix,) = each(
        local_kernel,
        (cum, cum_t, queries, keys, values),
        ("cum", "cumt", "col", "col", "col"),
        ("col",),
        name="local_mix",
    )
    if chips:
        own_t, other_t = turn_features(core, slots[3:], 3, 5, turned)
        partner_t = swap(other_t, 1)
        incoming = entering_chips(local_state, totals, False, (mix,), (own_t,))
    else:
        incoming = entering((jnp.exp(total), local_state.astype(F32)), "seq", False)
    attended, head_grad, local_reverse = each(
        norm_kernel,
        (cum, queries, out_grad, mix, incoming),
        ("cum", "col", "col", "col", "state"),
        ("col", "col", "state"),
        name="norm_grad",
    )
    (query_grad,) = each(
        back_query_kernel,
        (cum, cum_t, keys, values, head_grad, incoming),
        ("cum", "cumt", "col", "col", "col", "state"),
        ("col",),
        name="back_query",
    )
    key_local, value_local = each(
        back_keys_kernel,
        (cum, cum_t, queries, keys, values, head_grad),
        ("cum", "cumt", "col", "col", "col", "col"),
        ("col", "col"),
        name="back_keys",
    )
    if chips:
        outgoing = entering_chips(local_reverse, totals, True, (query_grad,), (key_local,))
    else:
        outgoing = entering((jnp.exp(total), local_reverse.astype(F32)), "seq", True)
    key_grad, value_grad = each(
        close_kernel,
        (cum, keys, values, key_local, value_local, outgoing),
        ("cum", "col", "col", "col", "col", "state"),
        ("col", "col"),
        name="close_back",
    )

    def terms(indices, done, adds=()):
        indices = after(jnp.stack(indices), *done)
        return feature_terms(indices, key_grad, value_grad, key_weight, value_weight, adds, depth)

    def add(*terms):
        return sum(t.astype(F32) for t in terms).astype(BF)

    def scatter_indices(step):
        upward = jnp.minimum(here + count - step, count - 1)
        downward = jnp.maximum(here - count + step, 0)
        return upward, downward, jnp.where(here < step, upward, downward)

    def send(step, up_sum, down_sum):
        return (
            lax.ppermute(up_sum, "head", scatter_pairs(count, step, True)),
            lax.ppermute(down_sum, "head", scatter_pairs(count, step, False)),
        )

    def feature_step(step, up, down, done):
        upward, downward, either = scatter_indices(step)
        if 2 * step <= count:
            total = terms([either], done, () if up is None else (up, down))[0]
            return send(step, total, total), total
        both = terms([upward, downward], done)
        return send(step, add(both[0], up), add(both[1], down)), both

    norm = (tokens * blocks) ** (-0.5)
    if not chips:
        up = down = None
        done = (key_grad,)
        for step in range(1, count):
            (up, down), last = feature_step(step, up, down, done)
            done = (last,)
        feature_grad = terms([here], done, (up, down))[0]
        gathered = lax.all_gather(features, "head", axis=1, tiled=True)
        both = jnp.concatenate([key_grad, value_grad], axis=1)
        summed = lax.psum_scatter(
            lax.dot_general(gathered, both, TN, preferred_element_type=F32).astype(BF),
            "seq",
            scatter_dimension=0,
            tiled=True,
        ).astype(F32)
        summed = summed * norm
        return attended, query_grad, feature_grad, summed[:, :proj], summed[:, proj:]

    chip = place // 2
    pairs = [(g, swap(g, 1)) for g in (key_grad, value_grad)]

    def blocks_for(targets, which, done, kind=BF):
        offset = after(jnp.stack(targets), *done) - here
        far = jnp.abs(offset)
        slot = jnp.where(far < 2, jnp.where(offset < 0, 2, far), far + 1)
        return weight_terms(slot, own_t, partner_t, *pairs[which], kind)

    (up, down), last = feature_step(1, None, None, (key_grad,))
    key_away = blocks_for([chip ^ 3, chip ^ 1], 0, (last,))
    got_key = swap(key_away, 2)
    value_away = blocks_for([chip ^ 3, chip ^ 2], 1, (key_away,))
    got_value = swap(value_away, 4)
    upward, downward, either = scatter_indices(2)
    last = terms([either], (value_away,))[0]
    total = add(last, up, down)
    up, down = send(2, total, total)
    upward, downward, _ = scatter_indices(3)
    feature_up, feature_down, feature_own = last = terms([upward, downward, here], (total,))
    key_pass = blocks_for([chip ^ 2], 0, (last,))
    value_pass = blocks_for([chip ^ 1], 1, (key_pass,))
    key_own = blocks_for([chip], 0, (value_pass,), F32)[0]
    value_own = blocks_for([chip], 1, (key_own,), F32)[0]
    up = after(up, value_own)
    up, down = send(3, add(feature_up, up), add(feature_down, down))
    key_passed = swap(add(key_pass[0], got_key[0]), 4)
    value_passed = swap(add(value_pass[0], got_value[0]), 2)
    feature_grad = add(feature_own, up, down)
    key_out = (key_own + got_key[1].astype(F32) + key_passed.astype(F32)) * norm
    value_out = (value_own + got_value[1].astype(F32) + value_passed.astype(F32)) * norm
    return attended, query_grad, feature_grad, key_out, value_out


def solution(mesh):
    spread = P("seq", "head")
    return jax.shard_map(
        per_device,
        mesh=mesh,
        in_specs=(spread, P(None, "head"), P(None, "head"), spread, spread, spread),
        out_specs=(spread,) * 5,
        check_vma=False,
    )
```

time: 296 us -> 272 us (0.919)
  Pallas kernels: 122 us -> 91.5 us
  matrix products: 25.8 us -> 33.7 us
  waiting for transfers between devices: 55.1 us -> 49.2 us
  starting transfers between devices: 44.5 us -> 48.9 us
    pallas_call x20 -> x17, Pallas kernels: 122 us -> 91.5 us  [the longest x6 33.2 us: per_head(): pl.pallas_call(functools.partial(kernel, width, per), grid=(heads // per,...]
    ppermute x3, waiting for transfers between devices: 16 us -> 0.01 us  [send(): lax.ppermute(down_sum, 'head', scatter_pairs(count, step, False))]
    dot_general x8 -> x10, matrix products: 25.8 us -> 33.7 us  [dot(): return jnp.dot(a, b, preferred_element_type=F32)]
    ppermute x19 -> x18, waiting for transfers between devices: 9.45 us -> 16 us  [swap(): return lax.ppermute(x, 'seq', pairs)]
    ppermute x3, waiting for transfers between devices: 0.01 us -> 6.51 us  [send(): lax.ppermute(up_sum, 'head', scatter_pairs(count, step, True))]
    convert_element_type x4 -> x5, other arithmetic: 9.52 us -> 15.1 us  [add(): return sum((t.astype(F32) for t in terms)).astype(BF)]
    add x0 -> x4, other arithmetic: none -> 5.12 us  [the longest x2 4.02 us: per_device(): shards = [(up + down, index)]]
    convert_element_type x1 -> x2, other arithmetic: 6.13 us -> 1.01 us  [per_device(): keys, values = (key_sum.astype(BF), value_sum.astype(BF))]
  transfers between devices with their start and end apart: 31 -> 30, of which waited for: 8 -> 13; matrix products, arithmetic and copies ran while one was open for 20% -> 22% of each run, Pallas kernels for 37% -> 31%
where the time goes in v1:
time: 272 us; the launch traced here: 271 us
  Pallas kernels  91.5 us (34%)
  waiting for transfers between devices  49.2 us (18%)
  starting transfers between devices  48.9 us (18%)
  other arithmetic  35.4 us (13%)
  matrix products  33.7 us (12%)
  local copies, waits for them, and re-layouts  10.7 us (4%)
    dot_general x10, matrix products, dot(): return jnp.dot(a, b, preferred_element_type=F32)  33.7 us
    pallas_call x6, Pallas kernels, per_head(): pl.pallas_call(functools.partial(kernel, width, per), grid=(heads // per,...  33.2 us
    pallas_call x6, Pallas kernels, weight_terms(): pl.pallas_call(weight_kernel, grid_spec=pltpu.PrefetchScalarGridSpec(num_...  29.6 us
    ppermute x3, waiting for transfers between devices, per_device(): down = lax.ppermute(down, 'head', line_pairs(count, step, False))  25.1 us
    pallas_call x3, Pallas kernels, feature_terms(): pl.pallas_call(functools.partial(feature_kernel, len(adds)), grid_spec=pl...  23.7 us
    ppermute x18, starting transfers between devices, swap(): return lax.ppermute(x, 'seq', pairs)  19.4 us
    ppermute x18, waiting for transfers between devices, swap(): return lax.ppermute(x, 'seq', pairs)  16 us
    convert_element_type x5, other arithmetic, add(): return sum((t.astype(F32) for t in terms)).astype(BF)  15.1 us
  transfers between devices with their start and end apart: 30, of which 13 were waited for; matrix products, arithmetic and copies ran while one was open for 22% of the time, Pallas kernels for 31%

profile of v1, /device:TPU:0, one launch (start us, length us, event | category | flops | bytes accessed | tf_op | source)
XLA Modules:
  0.0 270.7 jit_solution(5286416428397765973)
XLA Ops:
  0.6 5.9 %collective-permute-start = (bf16[512,1024]{1,0:T(8,128)(2,1)}, bf16[512,1024]{1,0:T(8,128)(2,1)}, u32[]{:S(2)}, u32[]{:S(2)}) collective-permute-start(bf16[512,1024]{1,0:T(8,128)(2,1)} %refs_0_.1), channel_id=1, source_target_pairs={{0,1},{1,2},{2,3},{4,5},{5,6},{6,7},{8,9},{9,10},{10,11},{12,13},{... | collective-permute-start | bytes 3145736 | tf_op jit(solution)/shard_map/ppermute | solution.py:372
  7.9 2.2 reduce-window.6
  10.6 4.6 %fusion.30 = f32[512,1024]{1,0:T(8,128)} fusion(bf16[512,1024]{1,0:T(8,128)(2,1)} %refs_0_.1, bf16[4096,1024]{1,0:T(8,128)(2,1)} %kw_ref.5, s32[]{:T(128)S(6)} %select_n.207), kind=kOutput, calls=%fused_computation.42 | convolution fusion | flops 1073741824 | bytes 5242884 | tf_op jit(solution)/shard_map/dot_general | solution.py:18
  15.2 4.2 %fusion.33 = f32[512,1024]{1,0:T(8,128)} fusion(bf16[512,1024]{1,0:T(8,128)(2,1)S(1)} %copy-done.11, bf16[4096,1024]{1,0:T(8,128)(2,1)} %vw_ref.5, s32[]{:T(128)S(6)} %select_n.207), kind=kOutput, calls=%fused_computation.43 | convolution fusion | flops 1073741824 | bytes 5242884 | tf_op jit(solution)/shard_map/dot_general | solution.py:18
  20.9 2.1 collective-permute-done.5
  24.6 2.1 collective-permute-done.6
  28.3 5.1 %collective-permute-done.1.refs_1_ = bf16[512,1024]{1,0:T(8,128)(2,1)} collective-permute-done((bf16[512,1024]{1,0:T(8,128)(2,1)}, bf16[512,1024]{1,0:T(8,128)(2,1)}, u32[]{:S(2)}, u32[]{:S(2)}) %collective-permute-start.1) | collective-permute-done | bytes 1048608 | tf_op jit(solution)/shard_map/ppermute | solution.py:373
  36.3 3.2 %fusion.24 = f32[512,1024]{1,0:T(8,128)S(1)} fusion(bf16[512,1024]{1,0:T(8,128)(2,1)} %collective-permute-done.1.refs_1_, bf16[4096,1024]{1,0:T(8,128)(2,1)} %kw_ref.5, s32[]{:T(128)S(6)} %select_n.208), kind=kOutput, calls=%fused_computation.36 | convolution fusion | flops 1073741824 | bytes 5242884 | tf_op jit(solution)/shard_map/dot_general | solution.py:18
  39.5 3.2 %fusion.20 = f32[512,1024]{1,0:T(8,128)S(1)} fusion(bf16[512,1024]{1,0:T(8,128)(2,1)} %collective-permute-done.1.refs_1_, bf16[4096,1024]{1,0:T(8,128)(2,1)} %vw_ref.5, s32[]{:T(128)S(6)} %select_n.208), kind=kOutput, calls=%fused_computation.31 | convolution fusion | flops 1073741824 | bytes 5242884 | tf_op jit(solution)/shard_map/dot_general | solution.py:18
  42.8 3.9 %turn_features.2 = (bf16[5,512,512]{2,1,0:T(8,128)(2,1)S(1)}, bf16[5,512,512]{2,1,0:T(8,128)(2,1)S(1)}) custom-call(s32[1]{0:T(128)} %bitcast.7.core_ref, bf16[512,1024]{1,0:T(8,128)(2,1)S(1)} %copy-done.12, bf16[512,1024]{1,0:T(8,128)(2,1)} %collective-permute-done.1.refs_1_, bf16[512,1024]{1,0:T(8,128)(2,1)} %collective-permute-done.refs_2_), custom_call_target="tpu_custom_call" | custom-call | flops 1 | bytes 1 | tf_op jit(solution)/shard_map/turn_features/pallas_call | solution.py:233
  48.2 4.7 %add_add_fusion.1 = f32[512,1024]{1,0:T(8,128)} fusion(f32[512,1024]{1,0:T(8,128)S(1)} %copy-done.19, f32[512,1024]{1,0:T(8,128)S(1)} %fusion.24, bf16[512,1024]{1,0:T(8,128)(2,1)} %collective-permute-done.refs_2_, bf16[4096,1024]{1,0:T(8,128)(2,1)} %kw_ref.5, s32[]{:T(128)S(6)} %select_n.209), kind=kOutput, calls=%fused_computation.35 | convolution fusion | flops 1074790400 | bytes 9437188 | tf_op jit(solution)/shard_map/dot_general | solution.py:18
  52.8 4.5 %add_add_fusion = f32[512,1024]{1,0:T(8,128)} fusion(f32[512,1024]{1,0:T(8,128)S(1)} %copy-done.18, f32[512,1024]{1,0:T(8,128)S(1)} %fusion.20, bf16[512,1024]{1,0:T(8,128)(2,1)} %collective-permute-done.refs_2_, bf16[4096,1024]{1,0:T(8,128)(2,1)} %vw_ref.5, s32[]{:T(128)S(6)} %select_n.209), kind=kOutput, calls=%fused_computation.30 | convolution fusion | flops 1074790400 | bytes 9437188 | tf_op jit(solution)/shard_map/dot_general | solution.py:18
  57.4 5.0 %collective-permute-done.3 = bf16[512,1024]{1,0:T(8,128)(2,1)} collective-permute-done((bf16[512,1024]{1,0:T(8,128)(2,1)}, bf16[512,1024]{1,0:T(8,128)(2,1)}, u32[]{:S(2)}, u32[]{:S(2)}) %collective-permute-start.3) | collective-permute-done | bytes 1048608 | tf_op jit(solution)/shard_map/ppermute | solution.py:373
  65.5 2.1 add.219.refs_2_
  67.6 3.6 %fusion.16 = f32[512,1024]{1,0:T(8,128)S(1)} fusion(bf16[512,1024]{1,0:T(8,128)(2,1)S(1)} %add.219.refs_2_, bf16[4096,1024]{1,0:T(8,128)(2,1)} %kw_ref.5, s32[]{:T(128)S(6)} %select_n.220), kind=kOutput, calls=%fused_computation.26 | convolution fusion | flops 1073741824 | bytes 5242884 | tf_op jit(solution)/shard_map/dot_general | solution.py:18
  74.0 15.0 %collective-permute-done.8 = bf16[512,1024]{1,0:T(8,128)(2,1)} collective-permute-done((bf16[512,1024]{1,0:T(8,128)(2,1)}, bf16[512,1024]{1,0:T(8,128)(2,1)}, u32[]{:S(2)}, u32[]{:S(2)}) %collective-permute-start.8) | collective-permute-done | bytes 1048608 | tf_op jit(solution)/shard_map/ppermute | solution.py:373
  89.0 1.9 add.224.refs_3_
  90.9 3.2 %fusion.12 = f32[512,1024]{1,0:T(8,128)S(1)} fusion(bf16[512,1024]{1,0:T(8,128)(2,1)S(1)} %add.224.refs_3_, bf16[4096,1024]{1,0:T(8,128)(2,1)} %kw_ref.5, s32[]{:T(128)S(6)} %select_n.222), kind=kOutput, calls=%fused_computation.22 | convolution fusion | flops 1073741824 | bytes 5242884 | tf_op jit(solution)/shard_map/dot_general | solution.py:18
  97.0 2.1 local_state.1
  102.6 6.1 %local_mix.1.mix_ref = bf16[512,1024]{1,0:T(8,128)(2,1)} custom-call(f32[512,8]{1,0:T(8,128)} %bitcast.81, f32[8,512]{1,0:T(8,128)} %copy.22.cumt_ref, bf16[512,1024]{1,0:T(8,128)(2,1)} %q_ref.5, bf16[512,1024]{1,0:T(8,128)(2,1)} %copy-done.1, bf16[512,1024]{1,0:T(8,128)(2,1)} %copy-done.2), custom_call_target="tpu_custom_call" | custom-call | flops 1 | bytes 1 | tf_op jit(solution)/shard_map/local_mix/pallas_call | solution.py:143
  108.8 3.4 %collective-permute-start.11 = (bf16[4,128,128]{2,1,0:T(8,128)(2,1)S(1)}, bf16[4,128,128]{2,1,0:T(8,128)(2,1)S(1)}, u32[]{:S(2)}, u32[]{:S(2)}) collective-permute-start(bf16[4,128,128]{2,1,0:T(8,128)(2,1)S(1)} %fusion.43), channel_id=1, source_target_pairs={{0,16},{4,20},{8,24},{12,28},{1,17},{5,21},{9,25},{13,29},{2,18},{... | collective-permute-start | bytes 393224 | tf_op jit(solution)/shard_map/ppermute | solution.py:278
  121.3 6.1 %norm_grad.1 = (bf16[512,1024]{1,0:T(8,128)(2,1)}, bf16[512,1024]{1,0:T(8,128)(2,1)}, bf16[8,128,128]{2,1,0:T(8,128)(2,1)}) custom-call(f32[512,8]{1,0:T(8,128)} %bitcast.82, bf16[512,1024]{1,0:T(8,128)(2,1)} %q_ref.5, bf16[512,1024]{1,0:T(8,128)(2,1)} %g_ref.1, bf16[512,1024]{1,0:T(8,128)(2,1)} %local_mix.1.mix_ref, bf16[8,128,128]{2,1,0:T(8,128)(2,1)} %fusion.38.s_ref), custom_call_target="tpu_custom_call" | custom-call | flops 1 | bytes 1 | tf_op jit(solution)/shard_map/norm_grad/pallas_call | solution.py:143
  130.9 6.0 %back_query.1 = bf16[512,1024]{1,0:T(8,128)(2,1)} custom-call(f32[512,8]{1,0:T(8,128)} %bitcast.83, f32[8,512]{1,0:T(8,128)} %copy.22.cumt_ref, bf16[512,1024]{1,0:T(8,128)(2,1)} %copy-done.1, bf16[512,1024]{1,0:T(8,128)(2,1)} %copy-done.2, bf16[512,1024]{1,0:T(8,128)(2,1)} %get-tuple-element.66.hg_ref, bf16[8,128,128]{2,1,0:T(8,128)(2,1)} %fusion.38.s_ref), custom_call_target="tpu_custom_call" | custom-call | flops 1 | bytes 1 | tf_op jit(solution)/shard_map/back_query/pallas_call | solution.py:143
  138.6 7.8 %back_keys.1 = (bf16[512,1024]{1,0:T(8,128)(2,1)}, bf16[512,1024]{1,0:T(8,128)(2,1)}) custom-call(f32[512,8]{1,0:T(8,128)} %bitcast.84, f32[8,512]{1,0:T(8,128)} %copy.22.cumt_ref, bf16[512,1024]{1,0:T(8,128)(2,1)} %q_ref.5, bf16[512,1024]{1,0:T(8,128)(2,1)} %copy-done.1, bf16[512,1024]{1,0:T(8,128)(2,1)} %copy-done.2, ...), custom_call_target="tpu_custom_call" | custom-call | flops 1 | bytes 1 | tf_op jit(solution)/shard_map/back_keys/pallas_call | solution.py:143
  148.8 5.2 %close_back.1 = (bf16[512,1024]{1,0:T(8,128)(2,1)}, bf16[512,1024]{1,0:T(8,128)(2,1)}) custom-call(f32[512,8]{1,0:T(8,128)} %bitcast.85, bf16[512,1024]{1,0:T(8,128)(2,1)} %copy-done.1, bf16[512,1024]{1,0:T(8,128)(2,1)} %copy-done.2, bf16[512,1024]{1,0:T(8,128)(2,1)} %get-tuple-element.67.kl_ref, bf16[512,1024]{1,0:T(8,128)(2,1)} %get-tuple-element.68.vl_ref, ...), custom_call_target="tpu_custom_call" | custom-call | flops 1 | bytes 1 | tf_op jit(solution)/shard_map/close_back/pallas_call | solution.py:143
  154.5 5.6 %feature_terms.3 = bf16[1,512,1024]{2,1,0:T(8,128)(2,1)} custom-call(s32[1]{0:T(128)} %bitcast.20.index_ref, bf16[512,1024]{1,0:T(8,128)(2,1)} %get-tuple-element.72.kg_ref.go_ref, bf16[512,1024]{1,0:T(8,128)(2,1)} %get-tuple-element.74.vg_ref.go_ref, bf16[4096,1024]{1,0:T(8,128)(2,1)} %kw_ref.5, bf16[4096,1024]{1,0:T(8,128)(2,1)} %vw_ref.5), custom_call_target="tpu_custom_call" | custom-call | flops 1 | bytes 1 | tf_op jit(solution)/shard_map/feature_terms/pallas_call | solution.py:169
  161.7 2.4 collective-permute-start.20
  166.3 7.1 %weight_terms.6 = bf16[2,512,1024]{2,1,0:T(8,128)(2,1)} custom-call(s32[2]{0:T(128)} %get-tuple-element.98.index_ref, bf16[5,512,512]{2,1,0:T(8,128)(2,1)} %copy-done, bf16[5,512,512]{2,1,0:T(8,128)(2,1)} %copy-done.13, bf16[512,1024]{1,0:T(8,128)(2,1)} %get-tuple-element.72.kg_ref.go_ref, bf16[512,1024]{1,0:T(8,128)(2,1)} %collective-permute-done.18.gp_ref), custom_call_target="tpu_custom_call" | custom-call | flops 1 | bytes 1 | tf_op jit(solution)/shard_map/weight_terms/pallas_call | solution.py:197
  175.4 7.1 %weight_terms.7 = bf16[2,512,1024]{2,1,0:T(8,128)(2,1)} custom-call(s32[2]{0:T(128)} %compare_select_fusion.1.index_ref, bf16[5,512,512]{2,1,0:T(8,128)(2,1)} %copy-done, bf16[5,512,512]{2,1,0:T(8,128)(2,1)} %copy-done.13, bf16[512,1024]{1,0:T(8,128)(2,1)} %get-tuple-element.74.vg_ref.go_ref, bf16[512,1024]{1,0:T(8,128)(2,1)} %collective-permute-done.19.gp_ref), custom_call_target="tpu_custom_call" | custom-call | flops 1 | bytes 1 | tf_op jit(solution)/shard_map/weight_terms/pallas_call | solution.py:197
  182.5 2.6 collective-permute-start.28
  185.1 5.6 %feature_terms.4 = bf16[1,512,1024]{2,1,0:T(8,128)(2,1)} custom-call(s32[1]{0:T(128)} %bitcast.16.index_ref, bf16[512,1024]{1,0:T(8,128)(2,1)} %get-tuple-element.72.kg_ref.go_ref, bf16[512,1024]{1,0:T(8,128)(2,1)} %get-tuple-element.74.vg_ref.go_ref, bf16[4096,1024]{1,0:T(8,128)(2,1)} %kw_ref.5, bf16[4096,1024]{1,0:T(8,128)(2,1)} %vw_ref.5), custom_call_target="tpu_custom_call" | custom-call | flops 1 | bytes 1 | tf_op jit(solution)/shard_map/feature_terms/pallas_call | solution.py:169
  190.7 2.5 fusion.9
  193.2 2.3 collective-permute-start.22
  197.8 12.5 %feature_terms.5 = bf16[3,512,1024]{2,1,0:T(8,128)(2,1)} custom-call(s32[3]{0:T(128)} %pad_add_fusion.index_ref, bf16[512,1024]{1,0:T(8,128)(2,1)} %get-tuple-element.72.kg_ref.go_ref, bf16[512,1024]{1,0:T(8,128)(2,1)} %get-tuple-element.74.vg_ref.go_ref, bf16[4096,1024]{1,0:T(8,128)(2,1)} %kw_ref.5, bf16[4096,1024]{1,0:T(8,128)(2,1)} %vw_ref.5), custom_call_target="tpu_custom_call" | custom-call | flops 1 | bytes 1 | tf_op jit(solution)/shard_map/feature_terms/pallas_call | solution.py:169
  210.3 6.5 %collective-permute-done.22 = bf16[512,1024]{1,0:T(8,128)(2,1)} collective-permute-done((bf16[512,1024]{1,0:T(8,128)(2,1)S(1)}, bf16[512,1024]{1,0:T(8,128)(2,1)}, u32[]{:S(2)}, u32[]{:S(2)}) %collective-permute-start.22) | collective-permute-done | bytes 1048608 | tf_op jit(solution)/shard_map/ppermute | solution.py:462
  216.8 4.5 %fusion.5 = (bf16[512,1024]{1,0:T(8,128)(2,1)}, bf16[512,1024]{1,0:T(8,128)(2,1)}) fusion(bf16[512,1024]{1,0:T(8,128)(2,1)} %collective-permute-done.22, bf16[3,512,1024]{2,1,0:T(8,128)(2,1)} %feature_terms.5, bf16[512,1024]{1,0:T(8,128)(2,1)} %collective-permute-done.24), kind=kLoop, calls=%fused_computation.9 | loop fusion | flops 4194304 | bytes 6291456 | tf_op jit(solution)/shard_map/convert_element_type | solution.py:453
  222.6 7.0 %collective-permute-start.23 = (bf16[512,1024]{1,0:T(8,128)(2,1)}, bf16[512,1024]{1,0:T(8,128)(2,1)}, u32[]{:S(2)}, u32[]{:S(2)}) collective-permute-start(bf16[512,1024]{1,0:T(8,128)(2,1)} %get-tuple-element.85), channel_id=1, source_target_pairs={{0,1},{1,2},{2,3},{4,5},{5,6},{6,7},{8,9},{9,10},{10,11},{12,13},{... | collective-permute-start | bytes 3145736 | tf_op jit(solution)/shard_map/ppermute | solution.py:462
  229.6 3.8 %weight_terms.8 = bf16[1,512,1024]{2,1,0:T(8,128)(2,1)} custom-call(s32[1]{0:T(128)S(6)} %select_n.256.index_ref, bf16[5,512,512]{2,1,0:T(8,128)(2,1)} %copy-done, bf16[5,512,512]{2,1,0:T(8,128)(2,1)} %copy-done.13, bf16[512,1024]{1,0:T(8,128)(2,1)} %get-tuple-element.72.kg_ref.go_ref, bf16[512,1024]{1,0:T(8,128)(2,1)} %collective-permute-done.18.gp_ref), custom_call_target="tpu_custom_call" | custom-call | flops 1 | bytes 1 | tf_op jit(solution)/shard_map/weight_terms/pallas_call | solution.py:197
  235.1 2.2 collective-permute-start.27
  237.3 3.8 %weight_terms.9 = bf16[1,512,1024]{2,1,0:T(8,128)(2,1)} custom-call(s32[1]{0:T(128)S(6)} %select_n.258.index_ref, bf16[5,512,512]{2,1,0:T(8,128)(2,1)} %copy-done, bf16[5,512,512]{2,1,0:T(8,128)(2,1)} %copy-done.13, bf16[512,1024]{1,0:T(8,128)(2,1)} %get-tuple-element.74.vg_ref.go_ref, bf16[512,1024]{1,0:T(8,128)(2,1)} %collective-permute-done.19.gp_ref), custom_call_target="tpu_custom_call" | custom-call | flops 1 | bytes 1 | tf_op jit(solution)/shard_map/weight_terms/pallas_call | solution.py:197
  241.1 2.9 %fusion.37 = bf16[512,1024]{1,0:T(8,128)(2,1)} fusion(bf16[1,512,1024]{2,1,0:T(8,128)(2,1)} %weight_terms.9, bf16[2,512,1024]{2,1,0:T(8,128)(2,1)} %collective-permute-done.28), kind=kLoop, calls=%fused_computation.45 | loop fusion | flops 2097152 | bytes 3145728 | tf_op jit(solution)/shard_map/convert_element_type | solution.py:453
  245.4 3.9 %weight_terms.10 = f32[1,512,1024]{2,1,0:T(8,128)} custom-call(s32[1]{0:T(128)S(6)} %select_n.260.index_ref, bf16[5,512,512]{2,1,0:T(8,128)(2,1)} %copy-done, bf16[5,512,512]{2,1,0:T(8,128)(2,1)} %copy-done.13, bf16[512,1024]{1,0:T(8,128)(2,1)} %get-tuple-element.72.kg_ref.go_ref, bf16[512,1024]{1,0:T(8,128)(2,1)} %collective-permute-done.18.gp_ref), custom_call_target="tpu_custom_call" | custom-call | flops 1 | bytes 1 | tf_op jit(solution)/shard_map/weight_terms/pallas_call | solution.py:197
  249.4 4.0 %weight_terms.11 = f32[1,512,1024]{2,1,0:T(8,128)} custom-call(s32[1]{0:T(128)S(6)} %select_n.262.index_ref, bf16[5,512,512]{2,1,0:T(8,128)(2,1)} %copy-done, bf16[5,512,512]{2,1,0:T(8,128)(2,1)} %copy-done.13, bf16[512,1024]{1,0:T(8,128)(2,1)} %get-tuple-element.74.vg_ref.go_ref, bf16[512,1024]{1,0:T(8,128)(2,1)} %collective-permute-done.19.gp_ref), custom_call_target="tpu_custom_call" | custom-call | flops 1 | bytes 1 | tf_op jit(solution)/shard_map/weight_terms/pallas_call | solution.py:197
  253.4 3.6 %fusion.7 = bf16[512,1024]{1,0:T(8,128)(2,1)} fusion(bf16[512,1024]{1,0:T(8,128)(2,1)} %collective-permute-done.25, bf16[512,1024]{1,0:T(8,128)(2,1)} %collective-permute-done.23, bf16[3,512,1024]{2,1,0:T(8,128)(2,1)} %feature_terms.5), kind=kLoop, calls=%fused_computation.12 | loop fusion | flops 3145728 | bytes 4194304 | tf_op jit(solution)/shard_map/convert_element_type | solution.py:453
  257.0 2.0 collective-permute-done.27
  259.0 3.1 %fusion.3 = f32[512,1024]{1,0:T(8,128)} fusion(bf16[512,1024]{1,0:T(8,128)(2,1)} %collective-permute-done.27, bf16[2,512,1024]{2,1,0:T(8,128)(2,1)S(1)} %collective-permute-done.26, f32[1,512,1024]{2,1,0:T(8,128)S(1)} %copy-done.17), kind=kLoop, calls=%fused_computation.5 | loop fusion | flops 2621440 | bytes 6291456 | tf_op jit(solution)/shard_map/mul | solution.py:522
  262.1 5.2 %collective-permute-done.29 = bf16[512,1024]{1,0:T(8,128)(2,1)} collective-permute-done((bf16[512,1024]{1,0:T(8,128)(2,1)}, bf16[512,1024]{1,0:T(8,128)(2,1)}, u32[]{:S(2)}, u32[]{:S(2)}) %collective-permute-start.29) | collective-permute-done | bytes 1048608 | tf_op jit(solution)/shard_map/ppermute | solution.py:278
  267.3 3.4 %fusion.1 = f32[512,1024]{1,0:T(8,128)} fusion(bf16[512,1024]{1,0:T(8,128)(2,1)} %collective-permute-done.29, bf16[2,512,1024]{2,1,0:T(8,128)(2,1)} %collective-permute-done.28, f32[1,512,1024]{2,1,0:T(8,128)S(1)} %copy-done.16), kind=kLoop, calls=%fused_computation.2 | loop fusion | flops 2621440 | bytes 6291456 | tf_op jit(solution)/shard_map/mul | solution.py:523
  (128 shorter events, 52.7 us)
Async XLA Ops:
  0.6 27.7 %collective-permute-start = (bf16[512,1024]{1,0:T(8,128)(2,1)}, bf16[512,1024]{1,0:T(8,128)(2,1)}, u32[]{:S(2)}, u32[]{:S(2)}) collective-permute-start(bf16[512,1024]{1,0:T(8,128)(2,1)} %refs_0_.1), channel_id=1, source_target_pairs={{0,1},{1,2},{2,3},{4,5},{5,6},{6,7},{8,9},{9,10},{10,11},{12,13},{... | collective-permute-start | bytes 3145736 | tf_op jit(solution)/shard_map/ppermute | solution.py:372
  6.6 26.8 %collective-permute-start.1 = (bf16[512,1024]{1,0:T(8,128)(2,1)}, bf16[512,1024]{1,0:T(8,128)(2,1)}, u32[]{:S(2)}, u32[]{:S(2)}) collective-permute-start(bf16[512,1024]{1,0:T(8,128)(2,1)} %refs_0_.1), channel_id=1, source_target_pairs={{1,0},{2,1},{3,2},{5,4},{6,5},{7,6},{9,8},{10,9},{11,10},{13,12},{... | collective-permute-start | bytes 3145736 | tf_op jit(solution)/shard_map/ppermute | solution.py:373
  10.5 88.7 %copy-start.3 = (f32[8,4,128]{0,2,1:T(8,128)}, f32[8,4,128]{0,2,1:T(8,128)S(1)}, u32[]{:S(2)}) copy-start(f32[8,4,128]{0,2,1:T(8,128)S(1)} %copy.19) | copy-start | bytes 49156
  10.5 8.9 %collective-permute-start.4 = (f32[1,8]{1,0:T(1,128)S(1)}, f32[1,8]{1,0:T(1,128)S(1)}, u32[]{:S(2)}, u32[]{:S(2)}) collective-permute-start(f32[1,8]{1,0:T(1,128)S(1)} %slice.29), channel_id=1, source_target_pairs={{0,4},{4,0},{8,12},{12,8},{16,20},{20,16},{24,28},{28,24},{1,5},{5... | collective-permute-start | bytes 104 | tf_op jit(solution)/shard_map/ppermute | solution.py:278
  10.6 4.6 %copy-start.11 = (bf16[512,1024]{1,0:T(8,128)(2,1)S(1)}, bf16[512,1024]{1,0:T(8,128)(2,1)}, u32[]{:S(2)}) copy-start(bf16[512,1024]{1,0:T(8,128)(2,1)} %refs_0_.1) | copy-start | bytes 3145732
  19.4 3.6 %collective-permute-start.5 = (f32[2,8]{1,0:T(2,128)S(1)}, f32[2,8]{1,0:T(2,128)S(1)}, u32[]{:S(2)}, u32[]{:S(2)}) collective-permute-start(f32[2,8]{1,0:T(2,128)S(1)} %pad_maximum_fusion.2), channel_id=1, source_target_pairs={{0,8},{4,12},{8,0},{12,4},{16,24},{20,28},{24,16},{28,20},{1,9},{5... | collective-permute-start | bytes 200 | tf_op jit(solution)/shard_map/ppermute | solution.py:278
  23.0 3.7 %collective-permute-start.6 = (f32[4,8]{1,0:T(4,128)S(1)}, f32[4,8]{1,0:T(4,128)S(1)}, u32[]{:S(2)}, u32[]{:S(2)}) collective-permute-start(f32[4,8]{1,0:T(4,128)S(1)} %pad_maximum_fusion.1), channel_id=1, source_target_pairs={{0,16},{4,20},{8,24},{12,28},{16,0},{20,4},{24,8},{28,12},{1,17},{... | collective-permute-start | bytes 392 | tf_op jit(solution)/shard_map/ppermute | solution.py:278
  33.4 24.0 %collective-permute-start.2 = (bf16[512,1024]{1,0:T(8,128)(2,1)}, bf16[512,1024]{1,0:T(8,128)(2,1)}, u32[]{:S(2)}, u32[]{:S(2)}) collective-permute-start(bf16[512,1024]{1,0:T(8,128)(2,1)} %collective-permute-done.refs_2_), channel_id=1, source_target_pairs={{1,2},{2,3},{5,6},{6,7},{9,10},{10,11},{13,14},{14,15},{17,18},{18... | collective-permute-start | bytes 3145736 | tf_op jit(solution)/shard_map/ppermute | solution.py:372
  35.0 27.3 %collective-permute-start.3 = (bf16[512,1024]{1,0:T(8,128)(2,1)}, bf16[512,1024]{1,0:T(8,128)(2,1)}, u32[]{:S(2)}, u32[]{:S(2)}) collective-permute-start(bf16[512,1024]{1,0:T(8,128)(2,1)} %collective-permute-done.1.refs_1_), channel_id=1, source_target_pairs={{1,0},{2,1},{5,4},{6,5},{9,8},{10,9},{13,12},{14,13},{17,16},{18,1... | collective-permute-start | bytes 3145736 | tf_op jit(solution)/shard_map/ppermute | solution.py:373
  39.5 3.3 %copy-start.12 = (bf16[512,1024]{1,0:T(8,128)(2,1)S(1)}, bf16[512,1024]{1,0:T(8,128)(2,1)}, u32[]{:S(2)}) copy-start(bf16[512,1024]{1,0:T(8,128)(2,1)} %refs_0_.1) | copy-start | bytes 3145732
  42.8 5.4 %copy-start.19 = (f32[512,1024]{1,0:T(8,128)S(1)}, f32[512,1024]{1,0:T(8,128)}, u32[]{:S(2)}) copy-start(f32[512,1024]{1,0:T(8,128)} %fusion.30) | copy-start | bytes 6291460
  46.7 1.5 copy-start.8
  48.2 4.7 %copy-start.18 = (f32[512,1024]{1,0:T(8,128)S(1)}, f32[512,1024]{1,0:T(8,128)}, u32[]{:S(2)}) copy-start(f32[512,1024]{1,0:T(8,128)} %fusion.33) | copy-start | bytes 6291460
  62.3 11.6 %collective-permute-start.7 = (bf16[512,1024]{1,0:T(8,128)(2,1)}, bf16[512,1024]{1,0:T(8,128)(2,1)}, u32[]{:S(2)}, u32[]{:S(2)}) collective-permute-start(bf16[512,1024]{1,0:T(8,128)(2,1)} %collective-permute-done.2), channel_id=1, source_target_pairs={{2,3},{6,7},{10,11},{14,15},{18,19},{22,23},{26,27},{30,31}} | collective-permute-start | bytes 3145736 | tf_op jit(solution)/shard_map/ppermute | solution.py:372
  64.0 25.0 %collective-permute-start.8 = (bf16[512,1024]{1,0:T(8,128)(2,1)}, bf16[512,1024]{1,0:T(8,128)(2,1)}, u32[]{:S(2)}, u32[]{:S(2)}) collective-permute-start(bf16[512,1024]{1,0:T(8,128)(2,1)} %collective-permute-done.3), channel_id=1, source_target_pairs={{1,0},{5,4},{9,8},{13,12},{17,16},{21,20},{25,24},{29,28}} | collective-permute-start | bytes 3145736 | tf_op jit(solution)/shard_map/ppermute | solution.py:373
  65.5 5.7 %copy-start.15 = (f32[512,1024]{1,0:T(8,128)S(1)}, f32[512,1024]{1,0:T(8,128)}, u32[]{:S(2)}) copy-start(f32[512,1024]{1,0:T(8,128)} %add_add_fusion.1) | copy-start | bytes 6291460
  65.5 6.3 %slice-start = ((s8[8388608]{0:T(1024)(128)(4,1)}), s8[4194304]{0:T(1024)(128)(4,1)S(1)}, s32[]{:S(2)}) async-start(s8[8388608]{0:T(1024)(128)(4,1)} %bitcast.86), calls=%async_computation | async-start | bytes 8388608
  67.6 4.2 %copy-start.4 = (bf16[512,1024]{1,0:T(8,128)(2,1)}, bf16[512,1024]{1,0:T(8,128)(2,1)S(1)}, u32[]{:S(2)}) copy-start(bf16[512,1024]{1,0:T(8,128)(2,1)S(1)} %add.219.refs_2_) | copy-start | bytes 3145732
  67.6 4.2 %slice-start.1 = ((s8[8388608]{0:T(1024)(128)(4,1)}), s8[4194304]{0:T(1024)(128)(4,1)S(1)}, s32[]{:S(2)}) async-start(s8[8388608]{0:T(1024)(128)(4,1)} %bitcast.86), calls=%async_computation.1 | async-start | bytes 8388608
  71.8 1.6 copy-start.14
  90.9 3.3 %copy-start.6 = (bf16[512,1024]{1,0:T(8,128)(2,1)}, bf16[512,1024]{1,0:T(8,128)(2,1)S(1)}, u32[]{:S(2)}) copy-start(bf16[512,1024]{1,0:T(8,128)(2,1)S(1)} %add.224.refs_3_) | copy-start | bytes 3145732
  97.0 2.1 copy-start.2
  99.1 1.6 collective-permute-start.9
  100.9 7.8 %collective-permute-start.10 = (bf16[4,128,128]{2,1,0:T(8,128)(2,1)S(1)}, bf16[4,128,128]{2,1,0:T(8,128)(2,1)S(1)}, u32[]{:S(2)}, u32[]{:S(2)}) collective-permute-start(bf16[4,128,128]{2,1,0:T(8,128)(2,1)S(1)} %fusion.41), channel_id=1, source_target_pairs={{0,8},{4,12},{8,0},{12,4},{16,24},{20,28},{24,16},{28,20},{1,9},{5... | collective-permute-start | bytes 393224 | tf_op jit(solution)/shard_map/ppermute | solution.py:278
  108.8 10.1 %collective-permute-start.11 = (bf16[4,128,128]{2,1,0:T(8,128)(2,1)S(1)}, bf16[4,128,128]{2,1,0:T(8,128)(2,1)S(1)}, u32[]{:S(2)}, u32[]{:S(2)}) collective-permute-start(bf16[4,128,128]{2,1,0:T(8,128)(2,1)S(1)} %fusion.43), channel_id=1, source_target_pairs={{0,16},{4,20},{8,24},{12,28},{1,17},{5,21},{9,25},{13,29},{2,18},{... | collective-permute-start | bytes 393224 | tf_op jit(solution)/shard_map/ppermute | solution.py:278
  114.7 1.7 copy-start.9
  118.9 8.5 %copy-start = (bf16[5,512,512]{2,1,0:T(8,128)(2,1)}, bf16[5,512,512]{2,1,0:T(8,128)(2,1)S(1)}, u32[]{:S(2)}) copy-start(bf16[5,512,512]{2,1,0:T(8,128)(2,1)S(1)} %get-tuple-element.63.fo_ref) | copy-start | bytes 7864324
  119.1 1.4 collective-permute-start.12
  127.4 1.8 collective-permute-start.13
  127.6 37.1 %collective-permute-start.17 = (bf16[5,512,512]{2,1,0:T(8,128)(2,1)}, bf16[5,512,512]{2,1,0:T(8,128)(2,1)S(1)}, u32[]{:S(2)}, u32[]{:S(2)}) collective-permute-start(bf16[5,512,512]{2,1,0:T(8,128)(2,1)} %copy-done.10), channel_id=1, source_target_pairs={{0,4},{4,0},{8,12},{12,8},{16,20},{20,16},{24,28},{28,24},{1,5},{5... | collective-permute-start | bytes 7864328 | tf_op jit(solution)/shard_map/ppermute | solution.py:278
  130.3 6.6 %collective-permute-start.14 = (bf16[4,128,128]{2,1,0:T(8,128)(2,1)S(1)}, bf16[4,128,128]{2,1,0:T(8,128)(2,1)S(1)}, u32[]{:S(2)}, u32[]{:S(2)}) collective-permute-start(bf16[4,128,128]{2,1,0:T(8,128)(2,1)S(1)} %fusion.46), channel_id=1, source_target_pairs={{0,8},{4,12},{8,0},{12,4},{16,24},{20,28},{24,16},{28,20},{1,9},{5... | collective-permute-start | bytes 393224 | tf_op jit(solution)/shard_map/ppermute | solution.py:278
  137.0 9.3 %collective-permute-start.15 = (bf16[4,128,128]{2,1,0:T(8,128)(2,1)S(1)}, bf16[4,128,128]{2,1,0:T(8,128)(2,1)S(1)}, u32[]{:S(2)}, u32[]{:S(2)}) collective-permute-start(bf16[4,128,128]{2,1,0:T(8,128)(2,1)S(1)} %fusion.48), channel_id=1, source_target_pairs={{16,0},{20,4},{24,8},{28,12},{17,1},{21,5},{25,9},{29,13},{18,2},{... | collective-permute-start | bytes 393224 | tf_op jit(solution)/shard_map/ppermute | solution.py:278
  146.5 1.4 collective-permute-start.16
  154.0 10.8 %collective-permute-start.18 = (bf16[512,1024]{1,0:T(8,128)(2,1)}, bf16[512,1024]{1,0:T(8,128)(2,1)}, u32[]{:S(2)}, u32[]{:S(2)}) collective-permute-start(bf16[512,1024]{1,0:T(8,128)(2,1)} %get-tuple-element.72.kg_ref.go_ref), channel_id=1, source_target_pairs={{0,4},{4,0},{8,12},{12,8},{16,20},{20,16},{24,28},{28,24},{1,5},{5... | collective-permute-start | bytes 3145736 | tf_op jit(solution)/shard_map/ppermute | solution.py:278
  154.1 21.3 %collective-permute-start.19 = (bf16[512,1024]{1,0:T(8,128)(2,1)}, bf16[512,1024]{1,0:T(8,128)(2,1)}, u32[]{:S(2)}, u32[]{:S(2)}) collective-permute-start(bf16[512,1024]{1,0:T(8,128)(2,1)} %get-tuple-element.74.vg_ref.go_ref), channel_id=1, source_target_pairs={{0,4},{4,0},{8,12},{12,8},{16,20},{20,16},{24,28},{28,24},{1,5},{5... | collective-permute-start | bytes 3145736 | tf_op jit(solution)/shard_map/ppermute | solution.py:278
  160.0 30.7 %collective-permute-start.21 = (bf16[512,1024]{1,0:T(8,128)(2,1)}, bf16[512,1024]{1,0:T(8,128)(2,1)}, u32[]{:S(2)}, u32[]{:S(2)}) collective-permute-start(bf16[512,1024]{1,0:T(8,128)(2,1)} %bitcast.88), channel_id=1, source_target_pairs={{3,2},{7,6},{11,10},{15,14},{19,18},{23,22},{27,26},{31,30}} | collective-permute-start | bytes 3145736 | tf_op jit(solution)/shard_map/ppermute | solution.py:463
  161.7 29.0 %collective-permute-start.20 = (bf16[512,1024]{1,0:T(8,128)(2,1)}, bf16[512,1024]{1,0:T(8,128)(2,1)}, u32[]{:S(2)}, u32[]{:S(2)}) collective-permute-start(bf16[512,1024]{1,0:T(8,128)(2,1)} %bitcast.89), channel_id=1, source_target_pairs={{0,1},{4,5},{8,9},{12,13},{16,17},{20,21},{24,25},{28,29}} | collective-permute-start | bytes 3145736 | tf_op jit(solution)/shard_map/ppermute | solution.py:462
  164.7 1.5 copy-start.13
  173.3 60.1 %collective-permute-start.26 = (bf16[2,512,1024]{2,1,0:T(8,128)(2,1)}, bf16[2,512,1024]{2,1,0:T(8,128)(2,1)S(1)}, u32[]{:S(2)}, u32[]{:S(2)}) collective-permute-start(bf16[2,512,1024]{2,1,0:T(8,128)(2,1)} %weight_terms.6), channel_id=1, source_target_pairs={{0,8},{4,12},{8,0},{12,4},{16,24},{20,28},{24,16},{28,20},{1,9},{5... | collective-permute-start | bytes 6291464 | tf_op jit(solution)/shard_map/ppermute | solution.py:278
  182.5 58.6 %collective-permute-start.28 = (bf16[2,512,1024]{2,1,0:T(8,128)(2,1)}, bf16[2,512,1024]{2,1,0:T(8,128)(2,1)}, u32[]{:S(2)}, u32[]{:S(2)}) collective-permute-start(bf16[2,512,1024]{2,1,0:T(8,128)(2,1)} %weight_terms.7), channel_id=1, source_target_pairs={{0,16},{4,20},{8,24},{12,28},{16,0},{20,4},{24,8},{28,12},{1,17},{... | collective-permute-start | bytes 6291464 | tf_op jit(solution)/shard_map/ppermute | solution.py:278
  193.2 23.6 %collective-permute-start.22 = (bf16[512,1024]{1,0:T(8,128)(2,1)S(1)}, bf16[512,1024]{1,0:T(8,128)(2,1)}, u32[]{:S(2)}, u32[]{:S(2)}) collective-permute-start(bf16[512,1024]{1,0:T(8,128)(2,1)S(1)} %fusion.9), channel_id=1, source_target_pairs={{0,1},{1,2},{4,5},{5,6},{8,9},{9,10},{12,13},{13,14},{16,17},{17,1... | collective-permute-start | bytes 3145736 | tf_op jit(solution)/shard_map/ppermute | solution.py:462
  195.5 21.3 %collective-permute-start.24 = (bf16[512,1024]{1,0:T(8,128)(2,1)S(1)}, bf16[512,1024]{1,0:T(8,128)(2,1)}, u32[]{:S(2)}, u32[]{:S(2)}) collective-permute-start(bf16[512,1024]{1,0:T(8,128)(2,1)S(1)} %fusion.9), channel_id=1, source_target_pairs={{2,1},{3,2},{6,5},{7,6},{10,9},{11,10},{14,13},{15,14},{18,17},{19... | collective-permute-start | bytes 3145736 | tf_op jit(solution)/shard_map/ppermute | solution.py:463
  221.3 32.0 %collective-permute-start.25 = (bf16[512,1024]{1,0:T(8,128)(2,1)}, bf16[512,1024]{1,0:T(8,128)(2,1)}, u32[]{:S(2)}, u32[]{:S(2)}) collective-permute-start(bf16[512,1024]{1,0:T(8,128)(2,1)} %get-tuple-element.86), channel_id=1, source_target_pairs={{1,0},{2,1},{3,2},{5,4},{6,5},{7,6},{9,8},{10,9},{11,10},{13,12},{... | collective-permute-start | bytes 3145736 | tf_op jit(solution)/shard_map/ppermute | solution.py:463
  222.6 30.7 %collective-permute-start.23 = (bf16[512,1024]{1,0:T(8,128)(2,1)}, bf16[512,1024]{1,0:T(8,128)(2,1)}, u32[]{:S(2)}, u32[]{:S(2)}) collective-permute-start(bf16[512,1024]{1,0:T(8,128)(2,1)} %get-tuple-element.85), channel_id=1, source_target_pairs={{0,1},{1,2},{2,3},{4,5},{5,6},{6,7},{8,9},{9,10},{10,11},{12,13},{... | collective-permute-start | bytes 3145736 | tf_op jit(solution)/shard_map/ppermute | solution.py:462
  235.1 23.9 %collective-permute-start.27 = (bf16[512,1024]{1,0:T(8,128)(2,1)S(1)}, bf16[512,1024]{1,0:T(8,128)(2,1)}, u32[]{:S(2)}, u32[]{:S(2)}) collective-permute-start(bf16[512,1024]{1,0:T(8,128)(2,1)S(1)} %fusion.36), channel_id=1, source_target_pairs={{0,16},{4,20},{8,24},{12,28},{16,0},{20,4},{24,8},{28,12},{1,17},{... | collective-permute-start | bytes 3145736 | tf_op jit(solution)/shard_map/ppermute | solution.py:278
  244.0 23.4 %collective-permute-start.29 = (bf16[512,1024]{1,0:T(8,128)(2,1)}, bf16[512,1024]{1,0:T(8,128)(2,1)}, u32[]{:S(2)}, u32[]{:S(2)}) collective-permute-start(bf16[512,1024]{1,0:T(8,128)(2,1)} %fusion.37), channel_id=1, source_target_pairs={{0,8},{4,12},{8,0},{12,4},{16,24},{20,28},{24,16},{28,20},{1,9},{5... | collective-permute-start | bytes 3145736 | tf_op jit(solution)/shard_map/ppermute | solution.py:278
  253.3 5.6 %copy-start.17 = (f32[1,512,1024]{2,1,0:T(8,128)S(1)}, f32[1,512,1024]{2,1,0:T(8,128)}, u32[]{:S(2)}) copy-start(f32[1,512,1024]{2,1,0:T(8,128)} %weight_terms.10) | copy-start | bytes 6291460
  257.0 10.4 %copy-start.16 = (f32[1,512,1024]{2,1,0:T(8,128)S(1)}, f32[1,512,1024]{2,1,0:T(8,128)}, u32[]{:S(2)}) copy-start(f32[1,512,1024]{2,1,0:T(8,128)} %weight_terms.11) | copy-start | bytes 6291460
  (4 other events, 4.9 us)

commit v2 on v1

--- a/solution.py
+++ b/solution.py
@@ -30,11 +30,7 @@
     return pltpu.CompilerParams(vmem_limit_bytes=limit * MIB)
 
 
-def after(x, *done):
-    return lax.optimization_barrier((x, *done))[0]
-
-
-def after_all(*arrays):
+def together(*arrays):
     return lax.optimization_barrier(arrays)
 
 
@@ -245,7 +241,7 @@
         ),
         out_shape=[jax.ShapeDtypeStruct((slots, depth // 2, tokens), BF)] * 2,
         input_output_aliases={1 + i: i for i in range(aliased)},
-        compiler_params=params(),
+        compiler_params=params(60),
         cost_estimate=SMALL,
         name="turn_features",
     )(core[None], *held, *shards)
@@ -308,19 +304,20 @@
     partner = swap(state, 1)
     own_decay, partner_decay = decay[place], decay[place ^ 1]
     chip = join(halves(state), halves(partner), 1, halves(own_decay), halves(partner_decay)).astype(BF)
-    beside = after(swap(chip, 2), *first_wait)
+    beside, first_wait = together(swap(chip, 2), first_wait)
     chip_decay = halves(own_decay * partner_decay)
     beside_decay = halves(decay[place ^ 2] * decay[place ^ 3])
     pair = join(chip, beside, 2, chip_decay, beside_decay).astype(BF)
     keep = (lambda s: (s & 4) != 0) if backward else (lambda s: (s & 4) == 0)
-    passed = after(swap(pair, 4, keep), *second_wait).astype(F32)
+    passed, second_wait = together(swap(pair, 4, keep), second_wait)
+    passed = passed.astype(F32)
     entered = jnp.where(ahead_of(2), beside_decay * passed + beside.astype(F32), passed).astype(BF)
     other = swap(entered, 1)
     whole = jnp.where(
         core == 0, jnp.concatenate([entered, other]), jnp.concatenate([other, entered])
     )
     step = partner_decay * whole.astype(F32) + partner.astype(F32)
-    return jnp.where(ahead_of(1), step.astype(BF), whole)
+    return jnp.where(ahead_of(1), step.astype(BF), whole), first_wait, second_wait
 
 
 def line_pairs(count, step, up):
@@ -365,21 +362,43 @@
     if chips:
         core = lax.rem(place, 2)
         totals = gather_totals(total)
+        chip = place // 2
+
+        def slots_of(*targets):
+            offsets = jnp.stack(targets) - here
+            far = jnp.abs(offsets)
+            return jnp.where(far < 2, jnp.where(offsets < 0, 2, far), far + 1)
+
+        ranks = (
+            slots_of(chip ^ 3, chip ^ 1),
+            slots_of(chip ^ 3, chip ^ 2),
+            slots_of(chip ^ 1),
+            slots_of(chip ^ 2),
+            slots_of(chip),
+        )
     sums = project(None, features, here)
     slots = [features]
     turned = ()
+    merged = None
     for step in range(1, count):
-        up = lax.ppermute(up, "head", line_pairs(count, step, True))
-        down = lax.ppermute(down, "head", line_pairs(count, step, False))
+        upward, downward = line_pairs(count, step, True), line_pairs(count, step, False)
+        if merged is None:
+            up = lax.ppermute(up, "head", upward)
+            down = lax.ppermute(down, "head", downward)
+            got = [up, down]
+        else:
+            got = [lax.ppermute(merged, "head", upward + downward)]
         if chips and step == count - 2:
             turned = turn_features(core, slots, 0, 5)
-            up, down, sums, turned, totals = after_all(up, down, sums, turned, totals)
+            got, sums, turned, totals, ranks = together(got, sums, turned, totals, ranks)
         else:
-            up, down, sums = after_all(up, down, sums)
+            got, sums = together(got, sums)
         if 2 * step >= count:
             index = jnp.where(here >= step, here - step, jnp.minimum(here + step, count - 1))
-            shards = [(up + down, index)]
+            merged = got[0] if len(got) == 1 else got[0] + got[1]
+            shards = [(merged, index)]
         else:
+            up, down = got
             shards = [
                 (down, jnp.minimum(here + step, count - 1)),
                 (up, jnp.maximum(here - step, 0)),
@@ -408,8 +427,11 @@
     )
     if chips:
         own_t, other_t = turn_features(core, slots[3:], 3, 5, turned)
+        incoming, mix, (own_t, other_t) = entering_chips(
+            local_state, totals, False, mix, (own_t, other_t)
+        )
+        incoming, other_t = together(incoming, other_t)
         partner_t = swap(other_t, 1)
-        incoming = entering_chips(local_state, totals, False, (mix,), (own_t,))
     else:
         incoming = entering((jnp.exp(total), local_state.astype(F32)), "seq", False)
     attended, head_grad, local_reverse = each(
@@ -434,7 +456,9 @@
         name="back_keys",
     )
     if chips:
-        outgoing = entering_chips(local_reverse, totals, True, (query_grad,), (key_local,))
+        outgoing, query_grad, (key_local, value_local, partner_t) = entering_chips(
+            local_reverse, totals, True, query_grad, (key_local, value_local, partner_t)
+        )
     else:
         outgoing = entering((jnp.exp(total), local_reverse.astype(F32)), "seq", True)
     key_grad, value_grad = each(
@@ -445,9 +469,10 @@
         name="close_back",
     )
 
-    def terms(indices, done, adds=()):
-        indices = after(jnp.stack(indices), *done)
-        return feature_terms(indices, key_grad, value_grad, key_weight, value_weight, adds, depth)
+    def terms(*indices):
+        return feature_terms(
+            jnp.stack(indices), key_grad, value_grad, key_weight, value_weight, (), depth
+        )
 
     def add(*terms):
         return sum(t.astype(F32) for t in terms).astype(BF)
@@ -455,30 +480,29 @@
     def scatter_indices(step):
         upward = jnp.minimum(here + count - step, count - 1)
         downward = jnp.maximum(here - count + step, 0)
-        return upward, downward, jnp.where(here < step, upward, downward)
+        return upward, downward
+
+    def either_term(step):
+        upward, downward = scatter_indices(step)
+        return terms(jnp.where(here < step, upward, downward))[0]
 
     def send(step, up_sum, down_sum):
-        return (
-            lax.ppermute(up_sum, "head", scatter_pairs(count, step, True)),
-            lax.ppermute(down_sum, "head", scatter_pairs(count, step, False)),
-        )
-
-    def feature_step(step, up, down, done):
-        upward, downward, either = scatter_indices(step)
-        if 2 * step <= count:
-            total = terms([either], done, () if up is None else (up, down))[0]
-            return send(step, total, total), total
-        both = terms([upward, downward], done)
-        return send(step, add(both[0], up), add(both[1], down)), both
+        upward, downward = scatter_pairs(count, step, True), scatter_pairs(count, step, False)
+        if 2 * step < count - 1:
+            return (lax.ppermute(up_sum, "head", upward + downward),)
+        return lax.ppermute(up_sum, "head", upward), lax.ppermute(down_sum, "head", downward)
 
     norm = (tokens * blocks) ** (-0.5)
     if not chips:
-        up = down = None
-        done = (key_grad,)
+        got = ()
         for step in range(1, count):
-            (up, down), last = feature_step(step, up, down, done)
-            done = (last,)
-        feature_grad = terms([here], done, (up, down))[0]
+            if 2 * step <= count:
+                total = add(either_term(step), *got)
+                got = send(step, total, total)
+            else:
+                up_term, down_term = terms(*scatter_indices(step))
+                got = send(step, add(up_term, got[0]), add(down_term, got[1]))
+        feature_grad = add(terms(here)[0], *got)
         gathered = lax.all_gather(features, "head", axis=1, tiled=True)
         both = jnp.concatenate([key_grad, value_grad], axis=1)
         summed = lax.psum_scatter(
@@ -490,37 +514,48 @@
         summed = summed * norm
         return attended, query_grad, feature_grad, summed[:, :proj], summed[:, proj:]
 
-    chip = place // 2
-    pairs = [(g, swap(g, 1)) for g in (key_grad, value_grad)]
-
-    def blocks_for(targets, which, done, kind=BF):
-        offset = after(jnp.stack(targets), *done) - here
-        far = jnp.abs(offset)
-        slot = jnp.where(far < 2, jnp.where(offset < 0, 2, far), far + 1)
-        return weight_terms(slot, own_t, partner_t, *pairs[which], kind)
-
-    (up, down), last = feature_step(1, None, None, (key_grad,))
-    key_away = blocks_for([chip ^ 3, chip ^ 1], 0, (last,))
+    away_x, away_y, one_x, one_y, home = ranks
+    partner_key, partner_value = swap(key_grad, 1), swap(value_grad, 1)
+
+    def blocks_for(slot, grad, partner_grad, kind=BF):
+        return weight_terms(slot, own_t, partner_t, grad, partner_grad, kind)
+
+    first = either_term(1)
+    got = send(1, first, first)
+    key_away = blocks_for(away_x, key_grad, partner_key)
+    key_away, value_grad, partner_value = together(key_away, value_grad, partner_value)
     got_key = swap(key_away, 2)
-    value_away = blocks_for([chip ^ 3, chip ^ 2], 1, (key_away,))
+    value_away = blocks_for(away_y, value_grad, partner_value)
+    value_away, key_grad = together(value_away, key_grad)
     got_value = swap(value_away, 4)
-    upward, downward, either = scatter_indices(2)
-    last = terms([either], (value_away,))[0]
-    total = add(last, up, down)
-    up, down = send(2, total, total)
-    upward, downward, _ = scatter_indices(3)
-    feature_up, feature_down, feature_own = last = terms([upward, downward, here], (total,))
-    key_pass = blocks_for([chip ^ 2], 0, (last,))
-    value_pass = blocks_for([chip ^ 1], 1, (key_pass,))
-    key_own = blocks_for([chip], 0, (value_pass,), F32)[0]
-    value_own = blocks_for([chip], 1, (key_own,), F32)[0]
-    up = after(up, value_own)
-    up, down = send(3, add(feature_up, up), add(feature_down, down))
-    key_passed = swap(add(key_pass[0], got_key[0]), 4)
-    value_passed = swap(add(value_pass[0], got_value[0]), 2)
+    second = either_term(2)
+    got, second = together(got, second)
+    total = add(second, *got)
+    total, value_grad = together(total, value_grad)
+    got = send(2, total, total)
+    ahead = terms(*scatter_indices(3))
+    ahead, key_grad, value_grad = together(ahead, key_grad, value_grad)
+    key_pass = blocks_for(one_y, key_grad, partner_key)
+    value_pass = blocks_for(one_x, value_grad, partner_value)
+    got, key_pass, value_pass = together(got, key_pass, value_pass)
+    up_sum, down_sum = add(ahead[0], got[0]), add(ahead[1], got[1])
+    up_sum, down_sum, got_key = together(up_sum, down_sum, got_key)
+    up, down = send(3, up_sum, down_sum)
+    key_sent = add(key_pass[0], got_key[0])
+    key_sent, got_value = together(key_sent, got_value)
+    got_key_pass = swap(key_sent, 4)
+    value_sent = add(value_pass[0], got_value[0])
+    value_sent, key_grad, value_grad = together(value_sent, key_grad, value_grad)
+    got_value_pass = swap(value_sent, 2)
+    key_own = blocks_for(home, key_grad, partner_key, F32)[0]
+    value_own = blocks_for(home, value_grad, partner_value, F32)[0]
+    feature_own = terms(here)[0]
+    up, key_own, value_own = together(up, key_own, value_own)
     feature_grad = add(feature_own, up, down)
-    key_out = (key_own + got_key[1].astype(F32) + key_passed.astype(F32)) * norm
-    value_out = (value_own + got_value[1].astype(F32) + value_passed.astype(F32)) * norm
+    got_key_pass, feature_grad = together(got_key_pass, feature_grad)
+    key_out = (key_own + got_key[1].astype(F32) + got_key_pass.astype(F32)) * norm
+    got_value_pass, key_out = together(got_value_pass, key_out)
+    value_out = (value_own + got_value[1].astype(F32) + got_value_pass.astype(F32)) * norm
     return attended, query_grad, feature_grad, key_out, value_out
 
 

time: 272 us -> 260 us (0.956)
  waiting for transfers between devices: 49.2 us -> 40.2 us
  Pallas kernels: 91.5 us -> 100 us
  local copies, waits for them, and re-layouts: 10.7 us -> 2.77 us
  other arithmetic: 35.4 us -> 30.6 us
  matrix products: 33.7 us -> 37 us
    ppermute x18, waiting for transfers between devices: 16 us -> 7.97 us  [swap(): return lax.ppermute(x, 'seq', pairs)]
    unnamed x44 -> x36, local copies, waits for them, and re-layouts: 9.53 us -> 1.54 us
    pallas_call x2, Pallas kernels: 4.84 us -> 11.1 us  [turn_features(): pl.pallas_call(functools.partial(turn_kernel, aliased), grid_spec=pltpu.P...]
    ppermute x12 -> x10, starting transfers between devices: 29.5 us -> 25.5 us  [the longest x2 10.5 us: send(): lax.ppermute(up_sum, 'head', upward)]
    dot_general x10, matrix products: 33.7 us -> 37 us  [dot(): return jnp.dot(a, b, preferred_element_type=F32)]
    pallas_call x3 -> x4, Pallas kernels: 23.7 us -> 26.1 us  [feature_terms(): pl.pallas_call(functools.partial(feature_kernel, len(adds)), grid_spec=pl...]
    ppermute x12 -> x10, waiting for transfers between devices: 33.2 us -> 32.3 us  [the longest x1 17.7 us: per_device(): got = [lax.ppermute(merged, 'head', upward + downward)]]
  transfers between devices with their start and end apart: 30 -> 28, of which waited for: 13 -> 12; matrix products, arithmetic and copies ran while one was open for 22% -> 21% of each run, Pallas kernels for 31% -> 36%
where the time goes in v2:
time: 260 us; the launch traced here: 259 us
  Pallas kernels  100 us (38%)
  starting transfers between devices  46.5 us (18%)
  waiting for transfers between devices  40.2 us (15%)
  matrix products  37 us (14%)
  other arithmetic  30.6 us (12%)
  local copies, waits for them, and re-layouts  2.77 us (1%)
    dot_general x10, matrix products, dot(): return jnp.dot(a, b, preferred_element_type=F32)  37 us
    pallas_call x6, Pallas kernels, per_head(): pl.pallas_call(functools.partial(kernel, width, per), grid=(heads // per,...  33.2 us
    pallas_call x6, Pallas kernels, weight_terms(): pl.pallas_call(weight_kernel, grid_spec=pltpu.PrefetchScalarGridSpec(num_...  29.9 us
    pallas_call x4, Pallas kernels, feature_terms(): pl.pallas_call(functools.partial(feature_kernel, len(adds)), grid_spec=pl...  26.1 us
    ppermute x18, starting transfers between devices, swap(): return lax.ppermute(x, 'seq', pairs)  21 us
    ppermute x1, waiting for transfers between devices, per_device(): got = [lax.ppermute(merged, 'head', upward + downward)]  17.7 us
    convert_element_type x5, other arithmetic, add(): return sum((t.astype(F32) for t in terms)).astype(BF)  12.5 us
    pallas_call x2, Pallas kernels, turn_features(): pl.pallas_call(functools.partial(turn_kernel, aliased), grid_spec=pltpu.P...  11.1 us
  transfers between devices with their start and end apart: 28, of which 12 were waited for; matrix products, arithmetic and copies ran while one was open for 21% of the time, Pallas kernels for 36%

profile of v2, /device:TPU:0, one launch (start us, length us, event | category | flops | bytes accessed | tf_op | source)
XLA Modules:
  0.0 258.8 jit_solution(4670599166355456132)
XLA Ops:
  1.9 6.5 %collective-permute-start = (bf16[512,1024]{1,0:T(8,128)(2,1)}, bf16[512,1024]{1,0:T(8,128)(2,1)}, u32[]{:S(2)}, u32[]{:S(2)}) collective-permute-start(bf16[512,1024]{1,0:T(8,128)(2,1)} %refs_0_.1), channel_id=1, source_target_pairs={{0,1},{1,2},{2,3},{4,5},{5,6},{6,7},{8,9},{9,10},{10,11},{12,13},{... | collective-permute-start | bytes 3145736 | tf_op jit(solution)/shard_map/ppermute | solution.py:386
  8.5 2.2 reduce-window.6
  11.2 3.2 %fusion.31 = f32[512,1024]{1,0:T(8,128)S(1)} fusion(bf16[512,1024]{1,0:T(8,128)(2,1)} %refs_0_.1, bf16[4096,1024]{1,0:T(8,128)(2,1)} %vw_ref.7, s32[]{:T(128)S(6)} %select_n.202), kind=kOutput, calls=%fused_computation.41 | convolution fusion | flops 1073741824 | bytes 5242884 | tf_op jit(solution)/shard_map/dot_general | solution.py:18
  14.5 4.2 %fusion.28 = f32[512,1024]{1,0:T(8,128)} fusion(bf16[512,1024]{1,0:T(8,128)(2,1)S(1)} %copy-done.17, bf16[4096,1024]{1,0:T(8,128)(2,1)} %kw_ref.7, s32[]{:T(128)S(6)} %select_n.202), kind=kOutput, calls=%fused_computation.40 | convolution fusion | flops 1073741824 | bytes 5242884 | tf_op jit(solution)/shard_map/dot_general | solution.py:18
  19.3 2.0 collective-permute-start.5
  23.0 2.0 collective-permute-start.6
  26.7 2.4 collective-permute-done.1.refs_1_
  32.2 4.5 %fusion.18 = f32[512,1024]{1,0:T(8,128)} fusion(bf16[512,1024]{1,0:T(8,128)(2,1)} %collective-permute-done.1.refs_1_, bf16[4096,1024]{1,0:T(8,128)(2,1)} %vw_ref.7, s32[]{:T(128)S(6)} %select_n.203), kind=kOutput, calls=%fused_computation.29 | convolution fusion | flops 1073741824 | bytes 5242884 | tf_op jit(solution)/shard_map/dot_general | solution.py:18
  36.7 4.5 %fusion.22 = f32[512,1024]{1,0:T(8,128)} fusion(bf16[512,1024]{1,0:T(8,128)(2,1)} %collective-permute-done.1.refs_1_, bf16[4096,1024]{1,0:T(8,128)(2,1)} %kw_ref.7, s32[]{:T(128)S(6)} %select_n.203), kind=kOutput, calls=%fused_computation.34 | convolution fusion | flops 1073741824 | bytes 5242884 | tf_op jit(solution)/shard_map/dot_general | solution.py:18
  41.2 6.5 %turn_features.2 = (bf16[5,512,512]{2,1,0:T(8,128)(2,1)}, bf16[5,512,512]{2,1,0:T(8,128)(2,1)}) custom-call(s32[1]{0:T(128)} %bitcast.6.core_ref, bf16[512,1024]{1,0:T(8,128)(2,1)} %refs_0_.1, bf16[512,1024]{1,0:T(8,128)(2,1)} %collective-permute-done.1.refs_1_, bf16[512,1024]{1,0:T(8,128)(2,1)} %collective-permute-done.refs_2_), custom_call_target="tpu_custom_call" | custom-call | flops 1 | bytes 1 | tf_op jit(solution)/shard_map/turn_features/pallas_call | solution.py:229
  47.8 5.3 %add_add_fusion = f32[512,1024]{1,0:T(8,128)} fusion(f32[512,1024]{1,0:T(8,128)S(1)} %fusion.31, f32[512,1024]{1,0:T(8,128)} %fusion.18, bf16[512,1024]{1,0:T(8,128)(2,1)} %collective-permute-done.refs_2_, bf16[4096,1024]{1,0:T(8,128)(2,1)} %vw_ref.7, s32[]{:T(128)S(6)} %select_n.204), kind=kOutput, calls=%fused_computation.28 | convolution fusion | flops 1074790400 | bytes 9437188 | tf_op jit(solution)/shard_map/dot_general | solution.py:18
  53.0 3.2 %add_add_fusion.1 = f32[512,1024]{1,0:T(8,128)S(1)} fusion(f32[512,1024]{1,0:T(8,128)S(1)} %copy-done.14, f32[512,1024]{1,0:T(8,128)S(1)} %copy-done.15, bf16[512,1024]{1,0:T(8,128)(2,1)} %collective-permute-done.refs_2_, bf16[4096,1024]{1,0:T(8,128)(2,1)} %kw_ref.7, s32[]{:T(128)S(6)} %select_n.204), kind=kOutput, calls=%fused_computation.33 | convolution fusion | flops 1074790400 | bytes 9437188 | tf_op jit(solution)/shard_map/dot_general | solution.py:18
  56.3 4.1 %collective-permute-done.3 = bf16[512,1024]{1,0:T(8,128)(2,1)} collective-permute-done((bf16[512,1024]{1,0:T(8,128)(2,1)}, bf16[512,1024]{1,0:T(8,128)(2,1)}, u32[]{:S(2)}, u32[]{:S(2)}) %collective-permute-start.3) | collective-permute-done | bytes 1048608 | tf_op jit(solution)/shard_map/ppermute | solution.py:387
  60.4 1.9 add.217.refs_2_
  63.9 3.0 %fusion.12 = f32[512,1024]{1,0:T(8,128)S(1)} fusion(bf16[512,1024]{1,0:T(8,128)(2,1)S(1)} %add.217.refs_2_, bf16[4096,1024]{1,0:T(8,128)(2,1)} %vw_ref.7, s32[]{:T(128)S(6)} %select_n.230), kind=kOutput, calls=%fused_computation.22 | convolution fusion | flops 1073741824 | bytes 5242884 | tf_op jit(solution)/shard_map/dot_general | solution.py:18
  67.5 2.8 %fusion.14 = f32[512,1024]{1,0:T(8,128)S(1)} fusion(bf16[512,1024]{1,0:T(8,128)(2,1)S(1)} %add.217.refs_2_, bf16[4096,1024]{1,0:T(8,128)(2,1)} %kw_ref.7, s32[]{:T(128)S(6)} %select_n.230), kind=kOutput, calls=%fused_computation.24 | convolution fusion | flops 1073741824 | bytes 5242884 | tf_op jit(solution)/shard_map/dot_general | solution.py:18
  70.7 17.7 %collective-permute-done.7.refs_3_ = bf16[512,1024]{1,0:T(8,128)(2,1)} collective-permute-done((bf16[512,1024]{1,0:T(8,128)(2,1)S(1)}, bf16[512,1024]{1,0:T(8,128)(2,1)}, u32[]{:S(2)}, u32[]{:S(2)}) %collective-permute-start.7) | collective-permute-done | bytes 1048608 | tf_op jit(solution)/shard_map/ppermute | solution.py:390
  88.5 3.2 %fusion.8 = f32[512,1024]{1,0:T(8,128)S(1)} fusion(bf16[512,1024]{1,0:T(8,128)(2,1)} %collective-permute-done.7.refs_3_, bf16[4096,1024]{1,0:T(8,128)(2,1)} %vw_ref.7, s32[]{:T(128)S(6)} %select_n.232), kind=kOutput, calls=%fused_computation.17 | convolution fusion | flops 1073741824 | bytes 5242884 | tf_op jit(solution)/shard_map/dot_general | solution.py:18
  91.6 3.2 %fusion.10 = f32[512,1024]{1,0:T(8,128)S(1)} fusion(bf16[512,1024]{1,0:T(8,128)(2,1)} %collective-permute-done.7.refs_3_, bf16[4096,1024]{1,0:T(8,128)(2,1)} %kw_ref.7, s32[]{:T(128)S(6)} %select_n.232), kind=kOutput, calls=%fused_computation.20 | convolution fusion | flops 1073741824 | bytes 5242884 | tf_op jit(solution)/shard_map/dot_general | solution.py:18
  96.4 2.1 local_state.1
  102.0 6.1 %local_mix.1.mix_ref = bf16[512,1024]{1,0:T(8,128)(2,1)} custom-call(f32[512,8]{1,0:T(8,128)} %bitcast.67, f32[8,512]{1,0:T(8,128)} %copy.22.cumt_ref, bf16[512,1024]{1,0:T(8,128)(2,1)} %q_ref.5, bf16[512,1024]{1,0:T(8,128)(2,1)} %copy-done.1, bf16[512,1024]{1,0:T(8,128)(2,1)} %copy-done), custom_call_target="tpu_custom_call" | custom-call | flops 1 | bytes 1 | tf_op jit(solution)/shard_map/local_mix/pallas_call | solution.py:139
  108.2 3.4 %collective-permute-start.10 = (bf16[4,128,128]{2,1,0:T(8,128)(2,1)S(1)}, bf16[4,128,128]{2,1,0:T(8,128)(2,1)S(1)}, u32[]{:S(2)}, u32[]{:S(2)}) collective-permute-start(bf16[4,128,128]{2,1,0:T(8,128)(2,1)S(1)} %fusion.41), channel_id=1, source_target_pairs={{0,16},{4,20},{8,24},{12,28},{1,17},{5,21},{9,25},{13,29},{2,18},{... | collective-permute-start | bytes 393224 | tf_op jit(solution)/shard_map/ppermute | solution.py:274
  111.7 4.6 %turn_features.3 = (bf16[5,512,512]{2,1,0:T(8,128)(2,1)}, bf16[5,512,512]{2,1,0:T(8,128)(2,1)}) custom-call(s32[1]{0:T(128)} %bitcast.6.core_ref, bf16[5,512,512]{2,1,0:T(8,128)(2,1)} %get-tuple-element.95.refs_0_, bf16[5,512,512]{2,1,0:T(8,128)(2,1)} %get-tuple-element.96.refs_1_, ...), custom_call_target="tpu_custom_call", output_to_operand_aliasing={{0}: (1, {}), {1}: (2, {})} | custom-call | flops 1 | bytes 1 | tf_op jit(solution)/shard_map/turn_features/pallas_call | solution.py:229
  118.9 6.1 %norm_grad.1 = (bf16[512,1024]{1,0:T(8,128)(2,1)}, bf16[512,1024]{1,0:T(8,128)(2,1)}, bf16[8,128,128]{2,1,0:T(8,128)(2,1)}) custom-call(f32[512,8]{1,0:T(8,128)} %bitcast.68, bf16[512,1024]{1,0:T(8,128)(2,1)} %q_ref.5, bf16[512,1024]{1,0:T(8,128)(2,1)} %g_ref.1, bf16[512,1024]{1,0:T(8,128)(2,1)} %local_mix.1.mix_ref, bf16[8,128,128]{2,1,0:T(8,128)(2,1)} %fusion.36.s_ref), custom_call_target="tpu_custom_call" | custom-call | flops 1 | bytes 1 | tf_op jit(solution)/shard_map/norm_grad/pallas_call | solution.py:139
  128.4 6.0 %back_query.1 = bf16[512,1024]{1,0:T(8,128)(2,1)} custom-call(f32[512,8]{1,0:T(8,128)} %bitcast.69, f32[8,512]{1,0:T(8,128)} %copy.22.cumt_ref, bf16[512,1024]{1,0:T(8,128)(2,1)} %copy-done.1, bf16[512,1024]{1,0:T(8,128)(2,1)} %copy-done, bf16[512,1024]{1,0:T(8,128)(2,1)} %get-tuple-element.104.hg_ref, bf16[8,128,128]{2,1,0:T(8,128)(2,1)} %fusion.36.s_ref), custom_call_target="tpu_custom_call" | custom-call | flops 1 | bytes 1 | tf_op jit(solution)/shard_map/back_query/pallas_call | solution.py:139
  136.0 7.8 %back_keys.1 = (bf16[512,1024]{1,0:T(8,128)(2,1)}, bf16[512,1024]{1,0:T(8,128)(2,1)}) custom-call(f32[512,8]{1,0:T(8,128)} %bitcast.70, f32[8,512]{1,0:T(8,128)} %copy.22.cumt_ref, bf16[512,1024]{1,0:T(8,128)(2,1)} %q_ref.5, bf16[512,1024]{1,0:T(8,128)(2,1)} %copy-done.1, bf16[512,1024]{1,0:T(8,128)(2,1)} %copy-done, bf16[512,1024]{1,0:T(8,128)(2,1)} %get-tuple-element.104.hg_ref), custom_call_target="tpu_custom_call" | custom-call | flops 1 | bytes 1 | tf_op jit(solution)/shard_map/back_keys/pallas_call | solution.py:139
  146.2 5.2 %close_back.1 = (bf16[512,1024]{1,0:T(8,128)(2,1)}, bf16[512,1024]{1,0:T(8,128)(2,1)}) custom-call(f32[512,8]{1,0:T(8,128)} %bitcast.71, bf16[512,1024]{1,0:T(8,128)(2,1)} %copy-done.1, bf16[512,1024]{1,0:T(8,128)(2,1)} %copy-done, bf16[512,1024]{1,0:T(8,128)(2,1)} %get-tuple-element.110.kl_ref, bf16[512,1024]{1,0:T(8,128)(2,1)} %get-tuple-element.111.vl_ref, ...), custom_call_target="tpu_custom_call" | custom-call | flops 1 | bytes 1 | tf_op jit(solution)/shard_map/close_back/pallas_call | solution.py:139
  152.0 5.6 %feature_terms.4 = bf16[1,512,1024]{2,1,0:T(8,128)(2,1)} custom-call(s32[1]{0:T(128)} %bitcast.18.index_ref, bf16[512,1024]{1,0:T(8,128)(2,1)} %get-tuple-element.140.kg_ref.go_ref, bf16[512,1024]{1,0:T(8,128)(2,1)} %get-tuple-element.141.vg_ref.go_ref, bf16[4096,1024]{1,0:T(8,128)(2,1)} %kw_ref.7, bf16[4096,1024]{1,0:T(8,128)(2,1)} %vw_ref.7), custom_call_target="tpu_custom_call" | custom-call | flops 1 | bytes 1 | tf_op jit(solution)/shard_map/feature_terms/pallas_call | solution.py:165
  160.0 7.1 %weight_terms.6 = bf16[2,512,1024]{2,1,0:T(8,128)(2,1)} custom-call(s32[2]{0:T(128)} %get-tuple-element.118.index_ref, bf16[5,512,512]{2,1,0:T(8,128)(2,1)} %get-tuple-element.116.fo_ref, bf16[5,512,512]{2,1,0:T(8,128)(2,1)} %copy-done.3, bf16[512,1024]{1,0:T(8,128)(2,1)} %get-tuple-element.140.kg_ref.go_ref, bf16[512,1024]{1,0:T(8,128)(2,1)} %copy-done.4), custom_call_target="tpu_custom_call" | custom-call | flops 1 | bytes 1 | tf_op jit(solution)/shard_map/weight_terms/pallas_call | solution.py:193
  168.6 7.1 %weight_terms.7 = bf16[2,512,1024]{2,1,0:T(8,128)(2,1)} custom-call(s32[2]{0:T(128)} %get-tuple-element.115.index_ref, bf16[5,512,512]{2,1,0:T(8,128)(2,1)} %get-tuple-element.116.fo_ref, bf16[5,512,512]{2,1,0:T(8,128)(2,1)} %copy-done.3, bf16[512,1024]{1,0:T(8,128)(2,1)} %get-tuple-element.141.vg_ref.go_ref, bf16[512,1024]{1,0:T(8,128)(2,1)} %copy-done.5), custom_call_target="tpu_custom_call" | custom-call | flops 1 | bytes 1 | tf_op jit(solution)/shard_map/weight_terms/pallas_call | solution.py:193
  175.7 2.6 %collective-permute-start.23 = (bf16[2,512,1024]{2,1,0:T(8,128)(2,1)}, bf16[2,512,1024]{2,1,0:T(8,128)(2,1)}, u32[]{:S(2)}, u32[]{:S(2)}) collective-permute-start(bf16[2,512,1024]{2,1,0:T(8,128)(2,1)} %weight_terms.7), channel_id=1, source_target_pairs={{0,16},{4,20},{8,24},{12,28},{16,0},{20,4},{24,8},{28,12},{1,17},{... | collective-permute-start | bytes 6291464 | tf_op jit(solution)/shard_map/ppermute | solution.py:274
  178.3 5.6 %feature_terms.5 = bf16[1,512,1024]{2,1,0:T(8,128)(2,1)} custom-call(s32[1]{0:T(128)} %bitcast.20.index_ref, bf16[512,1024]{1,0:T(8,128)(2,1)} %get-tuple-element.140.kg_ref.go_ref, bf16[512,1024]{1,0:T(8,128)(2,1)} %get-tuple-element.141.vg_ref.go_ref, bf16[4096,1024]{1,0:T(8,128)(2,1)} %kw_ref.7, bf16[4096,1024]{1,0:T(8,128)(2,1)} %vw_ref.7), custom_call_target="tpu_custom_call" | custom-call | flops 1 | bytes 1 | tf_op jit(solution)/shard_map/feature_terms/pallas_call | solution.py:165
  183.9 2.6 %add_convert_fusion.2 = bf16[512,1024]{1,0:T(8,128)(2,1)} fusion(bf16[512,1024]{1,0:T(8,128)(2,1)S(1)} %collective-permute-done.17, bf16[512,1024]{1,0:T(8,128)(2,1)} %bitcast.74), kind=kLoop, calls=%fused_computation.15 | loop fusion | flops 2097152 | bytes 3145728 | tf_op jit(solution)/shard_map/convert_element_type | solution.py:478
  187.2 4.1 %collective-permute-start.20 = (bf16[512,1024]{1,0:T(8,128)(2,1)}, bf16[512,1024]{1,0:T(8,128)(2,1)}, u32[]{:S(2)}, u32[]{:S(2)}) collective-permute-start(bf16[512,1024]{1,0:T(8,128)(2,1)} %add_convert_fusion.2), channel_id=1, source_target_pairs={{0,1},{1,2},{4,5},{5,6},{8,9},{9,10},{12,13},{13,14},{16,17},{17,1... | collective-permute-start | bytes 3145736 | tf_op jit(solution)/shard_map/ppermute | solution.py:493
  192.0 9.4 %feature_terms.6 = bf16[2,512,1024]{2,1,0:T(8,128)(2,1)} custom-call(s32[2]{0:T(128)} %pad_add_fusion.index_ref, bf16[512,1024]{1,0:T(8,128)(2,1)} %get-tuple-element.140.kg_ref.go_ref, bf16[512,1024]{1,0:T(8,128)(2,1)} %get-tuple-element.141.vg_ref.go_ref, bf16[4096,1024]{1,0:T(8,128)(2,1)} %kw_ref.7, bf16[4096,1024]{1,0:T(8,128)(2,1)} %vw_ref.7), custom_call_target="tpu_custom_call" | custom-call | flops 1 | bytes 1 | tf_op jit(solution)/shard_map/feature_terms/pallas_call | solution.py:165
  201.4 3.8 %weight_terms.9 = bf16[1,512,1024]{2,1,0:T(8,128)(2,1)} custom-call(s32[1]{0:T(128)S(6)} %select_n.220.index_ref, bf16[5,512,512]{2,1,0:T(8,128)(2,1)} %get-tuple-element.116.fo_ref, bf16[5,512,512]{2,1,0:T(8,128)(2,1)} %copy-done.3, bf16[512,1024]{1,0:T(8,128)(2,1)} %get-tuple-element.141.vg_ref.go_ref, bf16[512,1024]{1,0:T(8,128)(2,1)} %copy-done.5), custom_call_target="tpu_custom_call" | custom-call | flops 1 | bytes 1 | tf_op jit(solution)/shard_map/weight_terms/pallas_call | solution.py:193
  205.2 3.9 %weight_terms.8 = bf16[1,512,1024]{2,1,0:T(8,128)(2,1)} custom-call(s32[1]{0:T(128)S(6)} %select_n.222.index_ref, bf16[5,512,512]{2,1,0:T(8,128)(2,1)} %get-tuple-element.116.fo_ref, bf16[5,512,512]{2,1,0:T(8,128)(2,1)} %copy-done.3, bf16[512,1024]{1,0:T(8,128)(2,1)} %get-tuple-element.140.kg_ref.go_ref, bf16[512,1024]{1,0:T(8,128)(2,1)} %copy-done.4), custom_call_target="tpu_custom_call" | custom-call | flops 1 | bytes 1 | tf_op jit(solution)/shard_map/weight_terms/pallas_call | solution.py:193
  209.2 3.8 %collective-permute-done.20 = bf16[512,1024]{1,0:T(8,128)(2,1)} collective-permute-done((bf16[512,1024]{1,0:T(8,128)(2,1)}, bf16[512,1024]{1,0:T(8,128)(2,1)}, u32[]{:S(2)}, u32[]{:S(2)}) %collective-permute-start.20) | collective-permute-done | bytes 1048608 | tf_op jit(solution)/shard_map/ppermute | solution.py:493
  212.9 3.5 %fusion.6 = (bf16[512,1024]{1,0:T(8,128)(2,1)}, bf16[512,1024]{1,0:T(8,128)(2,1)}) fusion(bf16[512,1024]{1,0:T(8,128)(2,1)S(1)} %collective-permute-done.21, bf16[2,512,1024]{2,1,0:T(8,128)(2,1)S(1)} %copy-done.9, bf16[512,1024]{1,0:T(8,128)(2,1)} %collective-permute-done.20), kind=kLoop, calls=%fused_computation.10 | loop fusion | flops 4194304 | bytes 6291456 | tf_op jit(solution)/shard_map/convert_element_type | solution.py:478
  216.5 6.4 %collective-permute-start.25 = (bf16[512,1024]{1,0:T(8,128)(2,1)}, bf16[512,1024]{1,0:T(8,128)(2,1)}, u32[]{:S(2)}, u32[]{:S(2)}) collective-permute-start(bf16[512,1024]{1,0:T(8,128)(2,1)} %get-tuple-element.142), channel_id=1, source_target_pairs={{0,1},{1,2},{2,3},{4,5},{5,6},{6,7},{8,9},{9,10},{10,11},{12,13},{... | collective-permute-start | bytes 3145736 | tf_op jit(solution)/shard_map/ppermute | solution.py:493
  226.1 2.7 %collective-permute-start.24 = (bf16[512,1024]{1,0:T(8,128)(2,1)S(1)}, bf16[512,1024]{1,0:T(8,128)(2,1)}, u32[]{:S(2)}, u32[]{:S(2)}) collective-permute-start(bf16[512,1024]{1,0:T(8,128)(2,1)S(1)} %fusion.34), channel_id=1, source_target_pairs={{0,16},{4,20},{8,24},{12,28},{16,0},{20,4},{24,8},{28,12},{1,17},{... | collective-permute-start | bytes 3145736 | tf_op jit(solution)/shard_map/ppermute | solution.py:274
  231.9 5.6 %feature_terms.7 = bf16[1,512,1024]{2,1,0:T(8,128)(2,1)} custom-call(s32[1]{0:T(128)} %bitcast.11.index_ref, bf16[512,1024]{1,0:T(8,128)(2,1)} %get-tuple-element.140.kg_ref.go_ref, bf16[512,1024]{1,0:T(8,128)(2,1)} %get-tuple-element.141.vg_ref.go_ref, bf16[4096,1024]{1,0:T(8,128)(2,1)} %kw_ref.7, bf16[4096,1024]{1,0:T(8,128)(2,1)} %vw_ref.7), custom_call_target="tpu_custom_call" | custom-call | flops 1 | bytes 1 | tf_op jit(solution)/shard_map/feature_terms/pallas_call | solution.py:165
  237.5 4.0 %weight_terms.11 = f32[1,512,1024]{2,1,0:T(8,128)} custom-call(s32[1]{0:T(128)S(6)} %select_n.224.index_ref, bf16[5,512,512]{2,1,0:T(8,128)(2,1)} %get-tuple-element.116.fo_ref, bf16[5,512,512]{2,1,0:T(8,128)(2,1)} %copy-done.3, bf16[512,1024]{1,0:T(8,128)(2,1)} %get-tuple-element.141.vg_ref.go_ref, bf16[512,1024]{1,0:T(8,128)(2,1)} %copy-done.5), custom_call_target="tpu_custom_call" | custom-call | flops 1 | bytes 1 | tf_op jit(solution)/shard_map/weight_terms/pallas_call | solution.py:193
  241.5 4.0 %weight_terms.10 = f32[1,512,1024]{2,1,0:T(8,128)} custom-call(s32[1]{0:T(128)S(6)} %select_n.224.index_ref, bf16[5,512,512]{2,1,0:T(8,128)(2,1)} %get-tuple-element.116.fo_ref, bf16[5,512,512]{2,1,0:T(8,128)(2,1)} %copy-done.3, bf16[512,1024]{1,0:T(8,128)(2,1)} %get-tuple-element.140.kg_ref.go_ref, bf16[512,1024]{1,0:T(8,128)(2,1)} %copy-done.4), custom_call_target="tpu_custom_call" | custom-call | flops 1 | bytes 1 | tf_op jit(solution)/shard_map/weight_terms/pallas_call | solution.py:193
  245.6 3.1 %collective-permute-done.26 = bf16[512,1024]{1,0:T(8,128)(2,1)} collective-permute-done((bf16[512,1024]{1,0:T(8,128)(2,1)}, bf16[512,1024]{1,0:T(8,128)(2,1)}, u32[]{:S(2)}, u32[]{:S(2)}) %collective-permute-start.26) | collective-permute-done | bytes 1048608 | tf_op jit(solution)/shard_map/ppermute | solution.py:493
  248.6 3.1 %fusion.5 = bf16[512,1024]{1,0:T(8,128)(2,1)} fusion(bf16[512,1024]{1,0:T(8,128)(2,1)} %collective-permute-done.26, bf16[512,1024]{1,0:T(8,128)(2,1)} %collective-permute-done.25, bf16[1,512,1024]{2,1,0:T(8,128)(2,1)S(1)} %copy-done.12), kind=kLoop, calls=%fused_computation.8 | loop fusion | flops 3145728 | bytes 4194304 | tf_op jit(solution)/shard_map/convert_element_type | solution.py:478
  251.8 3.6 %fusion.3 = f32[512,1024]{1,0:T(8,128)} fusion(f32[512,1024]{1,0:T(8,128)S(1)} %bitcast.73, bf16[512,1024]{1,0:T(8,128)(2,1)} %collective-permute-done.24, bf16[2,512,1024]{2,1,0:T(8,128)(2,1)} %collective-permute-done.22), kind=kLoop, calls=%fused_computation.5 | loop fusion | flops 2621440 | bytes 6291456 | tf_op jit(solution)/shard_map/mul | solution.py:556
  255.3 3.4 %fusion.1 = f32[512,1024]{1,0:T(8,128)} fusion(f32[512,1024]{1,0:T(8,128)S(1)} %bitcast.72, bf16[512,1024]{1,0:T(8,128)(2,1)} %collective-permute-done.27, bf16[2,512,1024]{2,1,0:T(8,128)(2,1)} %collective-permute-done.23), kind=kLoop, calls=%fused_computation.2 | loop fusion | flops 2621440 | bytes 6291456 | tf_op jit(solution)/shard_map/mul | solution.py:558
  (113 shorter events, 38.8 us)
Async XLA Ops:
  0.6 28.4 %collective-permute-start.1 = (bf16[512,1024]{1,0:T(8,128)(2,1)}, bf16[512,1024]{1,0:T(8,128)(2,1)}, u32[]{:S(2)}, u32[]{:S(2)}) collective-permute-start(bf16[512,1024]{1,0:T(8,128)(2,1)} %refs_0_.1), channel_id=1, source_target_pairs={{1,0},{2,1},{3,2},{5,4},{6,5},{7,6},{9,8},{10,9},{11,10},{13,12},{... | collective-permute-start | bytes 3145736 | tf_op jit(solution)/shard_map/ppermute | solution.py:387
  1.9 28.3 %collective-permute-start = (bf16[512,1024]{1,0:T(8,128)(2,1)}, bf16[512,1024]{1,0:T(8,128)(2,1)}, u32[]{:S(2)}, u32[]{:S(2)}) collective-permute-start(bf16[512,1024]{1,0:T(8,128)(2,1)} %refs_0_.1), channel_id=1, source_target_pairs={{0,1},{1,2},{2,3},{4,5},{5,6},{6,7},{8,9},{9,10},{10,11},{12,13},{... | collective-permute-start | bytes 3145736 | tf_op jit(solution)/shard_map/ppermute | solution.py:386
  11.1 87.5 %copy-start.2 = (f32[8,4,128]{0,2,1:T(8,128)}, f32[8,4,128]{0,2,1:T(8,128)S(1)}, u32[]{:S(2)}) copy-start(f32[8,4,128]{0,2,1:T(8,128)S(1)} %copy.19) | copy-start | bytes 49156
  11.1 8.2 %collective-permute-start.4 = (f32[1,8]{1,0:T(1,128)S(1)}, f32[1,8]{1,0:T(1,128)S(1)}, u32[]{:S(2)}, u32[]{:S(2)}) collective-permute-start(f32[1,8]{1,0:T(1,128)S(1)} %slice.37), channel_id=1, source_target_pairs={{0,4},{4,0},{8,12},{12,8},{16,20},{20,16},{24,28},{28,24},{1,5},{5... | collective-permute-start | bytes 104 | tf_op jit(solution)/shard_map/ppermute | solution.py:274
  11.2 3.3 %copy-start.17 = (bf16[512,1024]{1,0:T(8,128)(2,1)S(1)}, bf16[512,1024]{1,0:T(8,128)(2,1)}, u32[]{:S(2)}) copy-start(bf16[512,1024]{1,0:T(8,128)(2,1)} %refs_0_.1) | copy-start | bytes 3145732
  19.3 3.6 %collective-permute-start.5 = (f32[2,8]{1,0:T(2,128)S(1)}, f32[2,8]{1,0:T(2,128)S(1)}, u32[]{:S(2)}, u32[]{:S(2)}) collective-permute-start(f32[2,8]{1,0:T(2,128)S(1)} %pad_maximum_fusion.2), channel_id=1, source_target_pairs={{0,8},{4,12},{8,0},{12,4},{16,24},{20,28},{24,16},{28,20},{1,9},{5... | collective-permute-start | bytes 200 | tf_op jit(solution)/shard_map/ppermute | solution.py:274
  23.0 3.7 %collective-permute-start.6 = (f32[4,8]{1,0:T(4,128)S(1)}, f32[4,8]{1,0:T(4,128)S(1)}, u32[]{:S(2)}, u32[]{:S(2)}) collective-permute-start(f32[4,8]{1,0:T(4,128)S(1)} %pad_maximum_fusion.1), channel_id=1, source_target_pairs={{0,16},{4,20},{8,24},{12,28},{16,0},{20,4},{24,8},{28,12},{1,17},{... | collective-permute-start | bytes 392 | tf_op jit(solution)/shard_map/ppermute | solution.py:274
  30.2 26.0 %collective-permute-start.2 = (bf16[512,1024]{1,0:T(8,128)(2,1)}, bf16[512,1024]{1,0:T(8,128)(2,1)S(1)}, u32[]{:S(2)}, u32[]{:S(2)}) collective-permute-start(bf16[512,1024]{1,0:T(8,128)(2,1)} %collective-permute-done.refs_2_), channel_id=1, source_target_pairs={{1,2},{2,3},{5,6},{6,7},{9,10},{10,11},{13,14},{14,15},{17,18},{18... | collective-permute-start | bytes 3145736 | tf_op jit(solution)/shard_map/ppermute | solution.py:386
  30.9 29.5 %collective-permute-start.3 = (bf16[512,1024]{1,0:T(8,128)(2,1)}, bf16[512,1024]{1,0:T(8,128)(2,1)}, u32[]{:S(2)}, u32[]{:S(2)}) collective-permute-start(bf16[512,1024]{1,0:T(8,128)(2,1)} %collective-permute-done.1.refs_1_), channel_id=1, source_target_pairs={{1,0},{2,1},{5,4},{6,5},{9,8},{10,9},{13,12},{14,13},{17,16},{18,1... | collective-permute-start | bytes 3145736 | tf_op jit(solution)/shard_map/ppermute | solution.py:387
  47.8 5.3 %copy-start.14 = (f32[512,1024]{1,0:T(8,128)S(1)}, f32[512,1024]{1,0:T(8,128)}, u32[]{:S(2)}) copy-start(f32[512,1024]{1,0:T(8,128)} %fusion.28) | copy-start | bytes 6291460
  47.8 5.3 %copy-start.15 = (f32[512,1024]{1,0:T(8,128)S(1)}, f32[512,1024]{1,0:T(8,128)}, u32[]{:S(2)}) copy-start(f32[512,1024]{1,0:T(8,128)} %fusion.22) | copy-start | bytes 6291460
  56.3 4.2 %copy-start.16 = (bf16[512,1024]{1,0:T(8,128)(2,1)}, bf16[512,1024]{1,0:T(8,128)(2,1)S(1)}, u32[]{:S(2)}) copy-start(bf16[512,1024]{1,0:T(8,128)(2,1)S(1)} %collective-permute-done.2) | copy-start | bytes 3145732
  62.4 5.1 %copy-start.13 = (bf16[512,1024]{1,0:T(8,128)(2,1)}, bf16[512,1024]{1,0:T(8,128)(2,1)S(1)}, u32[]{:S(2)}) copy-start(bf16[512,1024]{1,0:T(8,128)(2,1)S(1)} %add.217.refs_2_) | copy-start | bytes 3145732
  62.4 26.1 %collective-permute-start.7 = (bf16[512,1024]{1,0:T(8,128)(2,1)S(1)}, bf16[512,1024]{1,0:T(8,128)(2,1)}, u32[]{:S(2)}, u32[]{:S(2)}) collective-permute-start(bf16[512,1024]{1,0:T(8,128)(2,1)S(1)} %add.217.refs_2_), channel_id=1, source_target_pairs={{2,3},{1,0},{6,7},{5,4},{10,11},{9,8},{14,15},{13,12},{18,19},{17,... | collective-permute-start | bytes 3145736 | tf_op jit(solution)/shard_map/ppermute | solution.py:390
  63.9 3.0 %copy-start.6 = (f32[512,1024]{1,0:T(8,128)S(1)}, f32[512,1024]{1,0:T(8,128)}, u32[]{:S(2)}) copy-start(f32[512,1024]{1,0:T(8,128)} %add_add_fusion) | copy-start | bytes 6291460
  95.3 1.0 copy-start
  96.4 5.6 %copy-start.1 = (bf16[512,1024]{1,0:T(8,128)(2,1)}, bf16[512,1024]{1,0:T(8,128)(2,1)S(1)}, u32[]{:S(2)}) copy-start(bf16[512,1024]{1,0:T(8,128)(2,1)S(1)} %add_convert_fusion.4.k_ref) | copy-start | bytes 3145732
  98.5 1.6 collective-permute-start.8
  100.3 7.8 %collective-permute-start.9 = (bf16[4,128,128]{2,1,0:T(8,128)(2,1)S(1)}, bf16[4,128,128]{2,1,0:T(8,128)(2,1)S(1)}, u32[]{:S(2)}, u32[]{:S(2)}) collective-permute-start(bf16[4,128,128]{2,1,0:T(8,128)(2,1)S(1)} %fusion.39), channel_id=1, source_target_pairs={{0,8},{4,12},{8,0},{12,4},{16,24},{20,28},{24,16},{28,20},{1,9},{5... | collective-permute-start | bytes 393224 | tf_op jit(solution)/shard_map/ppermute | solution.py:274
  108.2 8.1 %collective-permute-start.10 = (bf16[4,128,128]{2,1,0:T(8,128)(2,1)S(1)}, bf16[4,128,128]{2,1,0:T(8,128)(2,1)S(1)}, u32[]{:S(2)}, u32[]{:S(2)}) collective-permute-start(bf16[4,128,128]{2,1,0:T(8,128)(2,1)S(1)} %fusion.41), channel_id=1, source_target_pairs={{0,16},{4,20},{8,24},{12,28},{1,17},{5,21},{9,25},{13,29},{2,18},{... | collective-permute-start | bytes 393224 | tf_op jit(solution)/shard_map/ppermute | solution.py:274
  116.4 1.4 collective-permute-start.11
  118.7 25.1 %collective-permute-start.15 = (bf16[5,512,512]{2,1,0:T(8,128)(2,1)}, bf16[5,512,512]{2,1,0:T(8,128)(2,1)S(1)}, u32[]{:S(2)}, u32[]{:S(2)}) collective-permute-start(bf16[5,512,512]{2,1,0:T(8,128)(2,1)} %get-tuple-element.109), channel_id=1, source_target_pairs={{0,4},{4,0},{8,12},{12,8},{16,20},{20,16},{24,28},{28,24},{1,5},{5... | collective-permute-start | bytes 7864328 | tf_op jit(solution)/shard_map/ppermute | solution.py:274
  124.9 1.7 collective-permute-start.12
  127.8 6.6 %collective-permute-start.13 = (bf16[4,128,128]{2,1,0:T(8,128)(2,1)S(1)}, bf16[4,128,128]{2,1,0:T(8,128)(2,1)S(1)}, u32[]{:S(2)}, u32[]{:S(2)}) collective-permute-start(bf16[4,128,128]{2,1,0:T(8,128)(2,1)S(1)} %fusion.44), channel_id=1, source_target_pairs={{0,8},{4,12},{8,0},{12,4},{16,24},{20,28},{24,16},{28,20},{1,9},{5... | collective-permute-start | bytes 393224 | tf_op jit(solution)/shard_map/ppermute | solution.py:274
  134.5 9.3 %collective-permute-start.14 = (bf16[4,128,128]{2,1,0:T(8,128)(2,1)S(1)}, bf16[4,128,128]{2,1,0:T(8,128)(2,1)S(1)}, u32[]{:S(2)}, u32[]{:S(2)}) collective-permute-start(bf16[4,128,128]{2,1,0:T(8,128)(2,1)S(1)} %fusion.46), channel_id=1, source_target_pairs={{16,0},{20,4},{24,8},{28,12},{17,1},{21,5},{25,9},{29,13},{18,2},{... | collective-permute-start | bytes 393224 | tf_op jit(solution)/shard_map/ppermute | solution.py:274
  143.8 7.7 %copy-start.3 = (bf16[5,512,512]{2,1,0:T(8,128)(2,1)}, bf16[5,512,512]{2,1,0:T(8,128)(2,1)S(1)}, u32[]{:S(2)}) copy-start(bf16[5,512,512]{2,1,0:T(8,128)(2,1)S(1)} %collective-permute-done.15.fp_ref) | copy-start | bytes 7864324
  144.0 1.4 collective-permute-start.16
  151.5 7.5 %collective-permute-start.18 = (bf16[512,1024]{1,0:T(8,128)(2,1)}, bf16[512,1024]{1,0:T(8,128)(2,1)S(1)}, u32[]{:S(2)}, u32[]{:S(2)}) collective-permute-start(bf16[512,1024]{1,0:T(8,128)(2,1)} %get-tuple-element.140.kg_ref.go_ref), channel_id=1, source_target_pairs={{0,4},{4,0},{8,12},{12,8},{16,20},{20,16},{24,28},{28,24},{1,5},{5... | collective-permute-start | bytes 3145736 | tf_op jit(solution)/shard_map/ppermute | solution.py:274
  151.7 15.4 %collective-permute-start.19 = (bf16[512,1024]{1,0:T(8,128)(2,1)}, bf16[512,1024]{1,0:T(8,128)(2,1)S(1)}, u32[]{:S(2)}, u32[]{:S(2)}) collective-permute-start(bf16[512,1024]{1,0:T(8,128)(2,1)} %get-tuple-element.141.vg_ref.go_ref), channel_id=1, source_target_pairs={{0,4},{4,0},{8,12},{12,8},{16,20},{20,16},{24,28},{28,24},{1,5},{5... | collective-permute-start | bytes 3145736 | tf_op jit(solution)/shard_map/ppermute | solution.py:274
  157.6 26.3 %collective-permute-start.17 = (bf16[512,1024]{1,0:T(8,128)(2,1)}, bf16[512,1024]{1,0:T(8,128)(2,1)S(1)}, u32[]{:S(2)}, u32[]{:S(2)}) collective-permute-start(bf16[512,1024]{1,0:T(8,128)(2,1)} %bitcast.75), channel_id=1, source_target_pairs={{0,1},{3,2},{4,5},{7,6},{8,9},{11,10},{12,13},{15,14},{16,17},{19,... | collective-permute-start | bytes 3145736 | tf_op jit(solution)/shard_map/ppermute | solution.py:492
  159.0 1.0 copy-start.4
  167.1 1.6 copy-start.5
  167.1 49.4 %collective-permute-start.22 = (bf16[2,512,1024]{2,1,0:T(8,128)(2,1)}, bf16[2,512,1024]{2,1,0:T(8,128)(2,1)}, u32[]{:S(2)}, u32[]{:S(2)}) collective-permute-start(bf16[2,512,1024]{2,1,0:T(8,128)(2,1)} %weight_terms.6), channel_id=1, source_target_pairs={{0,8},{4,12},{8,0},{12,4},{16,24},{20,28},{24,16},{28,20},{1,9},{5... | collective-permute-start | bytes 6291464 | tf_op jit(solution)/shard_map/ppermute | solution.py:274
  175.7 50.4 %collective-permute-start.23 = (bf16[2,512,1024]{2,1,0:T(8,128)(2,1)}, bf16[2,512,1024]{2,1,0:T(8,128)(2,1)}, u32[]{:S(2)}, u32[]{:S(2)}) collective-permute-start(bf16[2,512,1024]{2,1,0:T(8,128)(2,1)} %weight_terms.7), channel_id=1, source_target_pairs={{0,16},{4,20},{8,24},{12,28},{16,0},{20,4},{24,8},{28,12},{1,17},{... | collective-permute-start | bytes 6291464 | tf_op jit(solution)/shard_map/ppermute | solution.py:274
  186.5 22.7 %collective-permute-start.21 = (bf16[512,1024]{1,0:T(8,128)(2,1)}, bf16[512,1024]{1,0:T(8,128)(2,1)S(1)}, u32[]{:S(2)}, u32[]{:S(2)}) collective-permute-start(bf16[512,1024]{1,0:T(8,128)(2,1)} %add_convert_fusion.2), channel_id=1, source_target_pairs={{2,1},{3,2},{6,5},{7,6},{10,9},{11,10},{14,13},{15,14},{18,17},{19... | collective-permute-start | bytes 3145736 | tf_op jit(solution)/shard_map/ppermute | solution.py:493
  187.2 25.7 %collective-permute-start.20 = (bf16[512,1024]{1,0:T(8,128)(2,1)}, bf16[512,1024]{1,0:T(8,128)(2,1)}, u32[]{:S(2)}, u32[]{:S(2)}) collective-permute-start(bf16[512,1024]{1,0:T(8,128)(2,1)} %add_convert_fusion.2), channel_id=1, source_target_pairs={{0,1},{1,2},{4,5},{5,6},{8,9},{9,10},{12,13},{13,14},{16,17},{17,1... | collective-permute-start | bytes 3145736 | tf_op jit(solution)/shard_map/ppermute | solution.py:493
  205.2 7.7 %copy-start.9 = (bf16[2,512,1024]{2,1,0:T(8,128)(2,1)S(1)}, bf16[2,512,1024]{2,1,0:T(8,128)(2,1)}, u32[]{:S(2)}) copy-start(bf16[2,512,1024]{2,1,0:T(8,128)(2,1)} %feature_terms.6) | copy-start | bytes 6291460
  209.2 15.2 %copy-start.11 = (bf16[1,512,1024]{2,1,0:T(8,128)(2,1)S(1)}, bf16[1,512,1024]{2,1,0:T(8,128)(2,1)}, u32[]{:S(2)}) copy-start(bf16[1,512,1024]{2,1,0:T(8,128)(2,1)} %weight_terms.8) | copy-start | bytes 3145732
  216.5 12.3 %copy-start.10 = (bf16[1,512,1024]{2,1,0:T(8,128)(2,1)S(1)}, bf16[1,512,1024]{2,1,0:T(8,128)(2,1)}, u32[]{:S(2)}) copy-start(bf16[1,512,1024]{2,1,0:T(8,128)(2,1)} %weight_terms.9) | copy-start | bytes 3145732
  216.5 29.1 %collective-permute-start.25 = (bf16[512,1024]{1,0:T(8,128)(2,1)}, bf16[512,1024]{1,0:T(8,128)(2,1)}, u32[]{:S(2)}, u32[]{:S(2)}) collective-permute-start(bf16[512,1024]{1,0:T(8,128)(2,1)} %get-tuple-element.142), channel_id=1, source_target_pairs={{0,1},{1,2},{2,3},{4,5},{5,6},{6,7},{8,9},{9,10},{10,11},{12,13},{... | collective-permute-start | bytes 3145736 | tf_op jit(solution)/shard_map/ppermute | solution.py:493
  222.9 25.8 %collective-permute-start.26 = (bf16[512,1024]{1,0:T(8,128)(2,1)}, bf16[512,1024]{1,0:T(8,128)(2,1)}, u32[]{:S(2)}, u32[]{:S(2)}) collective-permute-start(bf16[512,1024]{1,0:T(8,128)(2,1)} %get-tuple-element.145), channel_id=1, source_target_pairs={{1,0},{2,1},{3,2},{5,4},{6,5},{7,6},{9,8},{10,9},{11,10},{13,12},{... | collective-permute-start | bytes 3145736 | tf_op jit(solution)/shard_map/ppermute | solution.py:493
  226.1 25.7 %collective-permute-start.24 = (bf16[512,1024]{1,0:T(8,128)(2,1)S(1)}, bf16[512,1024]{1,0:T(8,128)(2,1)}, u32[]{:S(2)}, u32[]{:S(2)}) collective-permute-start(bf16[512,1024]{1,0:T(8,128)(2,1)S(1)} %fusion.34), channel_id=1, source_target_pairs={{0,16},{4,20},{8,24},{12,28},{16,0},{20,4},{24,8},{28,12},{1,17},{... | collective-permute-start | bytes 3145736 | tf_op jit(solution)/shard_map/ppermute | solution.py:274
  230.4 24.9 %collective-permute-start.27 = (bf16[512,1024]{1,0:T(8,128)(2,1)S(1)}, bf16[512,1024]{1,0:T(8,128)(2,1)}, u32[]{:S(2)}, u32[]{:S(2)}) collective-permute-start(bf16[512,1024]{1,0:T(8,128)(2,1)S(1)} %fusion.35), channel_id=1, source_target_pairs={{0,8},{4,12},{8,0},{12,4},{16,24},{20,28},{24,16},{28,20},{1,9},{5... | collective-permute-start | bytes 3145736 | tf_op jit(solution)/shard_map/ppermute | solution.py:274
  241.5 7.1 %copy-start.12 = (bf16[1,512,1024]{2,1,0:T(8,128)(2,1)S(1)}, bf16[1,512,1024]{2,1,0:T(8,128)(2,1)}, u32[]{:S(2)}) copy-start(bf16[1,512,1024]{2,1,0:T(8,128)(2,1)} %feature_terms.7) | copy-start | bytes 3145732
  245.5 6.2 %copy-start.8 = (f32[1,512,1024]{2,1,0:T(8,128)S(1)}, f32[1,512,1024]{2,1,0:T(8,128)}, u32[]{:S(2)}) copy-start(f32[1,512,1024]{2,1,0:T(8,128)} %weight_terms.10) | copy-start | bytes 6291460
  251.8 3.6 %copy-start.7 = (f32[1,512,1024]{2,1,0:T(8,128)S(1)}, f32[1,512,1024]{2,1,0:T(8,128)}, u32[]{:S(2)}) copy-start(f32[1,512,1024]{2,1,0:T(8,128)} %weight_terms.11) | copy-start | bytes 6291460

commit v3 on v2

--- a/solution.py
+++ b/solution.py
@@ -59,30 +59,42 @@
     return jnp.where(one <= two, jnp.exp(-gap), 0.0)
 
 
-def heads_of(per, width):
-    for i in range(per):
-        yield i, pl.program_id(0) * per + i, slice(i * width, (i + 1) * width)
+def each_head(per, width, body, group=2):
+    group = group if per % group == 0 else 1
+
+    def some(number, carry):
+        for j in range(group):
+            i = number * group + j
+            cut = pl.ds(pl.multiple_of(i * width, width), width)
+            body(i, pl.program_id(0) * per + i, cut)
+        return carry
+
+    lax.fori_loop(0, per // group, some, 0)
 
 
 def state_kernel(width, per, cum_ref, k_ref, v_ref, s_ref):
-    for i, head, cut in heads_of(per, width):
+    def one(i, head, cut):
         down = column(cum_ref, head)
         tail = jnp.exp(down[-1:] - down)
         scaled = (k_ref[:, cut].astype(F32) * tail).astype(BF)
         s_ref[i] = dot_tn(scaled, v_ref[:, cut]).astype(BF)
 
+    each_head(per, width, one)
+
 
 def local_kernel(width, per, cum_ref, cumt_ref, q_ref, k_ref, v_ref, mix_ref):
-    for i, head, cut in heads_of(per, width):
+    def one(i, head, cut):
         down, across = column(cum_ref, head), cumt_ref[pl.ds(head, 1), :]
         for rows, seen in tiles(q_ref.shape[0], True):
             scores = dot_nt(q_ref[rows, cut], k_ref[seen, cut])
             weights = (scores * decay_tile(across, down, rows, seen, True)).astype(BF)
             mix_ref[rows, cut] = dot(weights, v_ref[seen, cut]).astype(mix_ref.dtype)
 
+    each_head(per, width, one, 4)
+
 
 def norm_kernel(width, per, cum_ref, q_ref, g_ref, mix_ref, s_ref, att_ref, hg_ref, r_ref):
-    for i, head, cut in heads_of(per, width):
+    def one(i, head, cut):
         grow = jnp.exp(column(cum_ref, head))
         carried = grow * dot(q_ref[:, cut], s_ref[i])
         mixed = mix_ref[:, cut].astype(F32) + carried
@@ -95,9 +107,11 @@
         grown = (q_ref[:, cut].astype(F32) * grow).astype(BF)
         r_ref[i] = dot_tn(grown, head_grad).astype(BF)
 
+    each_head(per, width, one, 4)
+
 
 def back_query_kernel(width, per, cum_ref, cumt_ref, k_ref, v_ref, hg_ref, s_ref, qg_ref):
-    for i, head, cut in heads_of(per, width):
+    def one(i, head, cut):
         down, across = column(cum_ref, head), cumt_ref[pl.ds(head, 1), :]
         grow = jnp.exp(down)
         for rows, seen in tiles(k_ref.shape[0], True):
@@ -106,9 +120,11 @@
             carried = grow[rows] * dot_nt(hg_ref[rows, cut], s_ref[i])
             qg_ref[rows, cut] = (dot(pairs, k_ref[seen, cut]) + carried).astype(BF)
 
+    each_head(per, width, one, 4)
+
 
 def back_keys_kernel(width, per, cum_ref, cumt_ref, q_ref, k_ref, v_ref, hg_ref, kg_ref, vg_ref):
-    for i, head, cut in heads_of(per, width):
+    def one(i, head, cut):
         down, across = column(cum_ref, head), cumt_ref[pl.ds(head, 1), :]
         for rows, seen in tiles(q_ref.shape[0], False):
             decay = decay_tile(across, down, rows, seen, False)
@@ -117,15 +133,19 @@
             weights = (dot_nt(k_ref[rows, cut], q_ref[seen, cut]) * decay).astype(BF)
             vg_ref[rows, cut] = dot(weights, hg_ref[seen, cut]).astype(vg_ref.dtype)
 
+    each_head(per, width, one)
+
 
 def close_kernel(width, per, cum_ref, k_ref, v_ref, kl_ref, vl_ref, r_ref, kg_ref, vg_ref):
-    for i, head, cut in heads_of(per, width):
+    def one(i, head, cut):
         down = column(cum_ref, head)
         tail = jnp.exp(down[-1:] - down)
         key_carried = tail * dot_nt(v_ref[:, cut], r_ref[i])
         value_carried = tail * dot(k_ref[:, cut], r_ref[i])
         kg_ref[:, cut] = (kl_ref[:, cut].astype(F32) + key_carried).astype(BF)
         vg_ref[:, cut] = (vl_ref[:, cut].astype(F32) + value_carried).astype(BF)
+
+    each_head(per, width, one)
 
 
 def per_head(kernel, args, kinds, outs, tokens, heads, width, per, name, limit=60):
@@ -148,61 +168,65 @@
     )(*args)
 
 
-def feature_kernel(count, index_ref, kg_ref, vg_ref, kw_ref, vw_ref, *refs):
-    total = dot_nt(kg_ref[...], kw_ref[...]) + dot_nt(vg_ref[...], vw_ref[...])
-    for r in refs[:count]:
-        total += r[...].astype(F32)
-    refs[count][0] = total.astype(BF)
-
-
-def feature_terms(indices, key_grad, value_grad, key_weight, value_weight, adds, span):
+def feature_kernel(index_ref, kg_ref, vg_ref, kw_ref, vw_ref, out_ref):
+    grads = jnp.concatenate([kg_ref[...], vg_ref[...]], axis=1)
+    weights = jnp.concatenate([kw_ref[...], vw_ref[...]], axis=1)
+    out_ref[0] = dot_nt(grads, weights).astype(BF)
+
+
+def feature_terms(indices, key_grad, value_grad, key_weight, value_weight, span):
     tokens, proj = key_grad.shape
     tile = min(512, span)
     steps = span // tile
+    number = indices.shape[0]
     whole = pl.BlockSpec((tokens, proj), lambda i, j, d: (0, 0))
     weight = pl.BlockSpec((tile, proj), lambda i, j, d: (d[i] * steps + j, 0))
-    number = indices.shape[0]
     return pl.pallas_call(
-        functools.partial(feature_kernel, len(adds)),
+        feature_kernel,
         grid_spec=pltpu.PrefetchScalarGridSpec(
             num_scalar_prefetch=1,
             grid=(number, steps),
-            in_specs=[whole, whole, weight, weight]
-            + [pl.BlockSpec((tokens, tile), lambda i, j, d: (0, j))] * len(adds),
+            in_specs=[whole, whole, weight, weight],
             out_specs=pl.BlockSpec((1, tokens, tile), lambda i, j, d: (i, 0, j)),
         ),
         out_shape=jax.ShapeDtypeStruct((number, tokens, span), BF),
         compiler_params=params(60),
         cost_estimate=SMALL,
         name="feature_terms",
-    )(indices, key_grad, value_grad, key_weight, value_weight, *adds)
-
-
-def weight_kernel(index_ref, fo_ref, fp_ref, go_ref, gp_ref, out_ref):
-    total = dot(fo_ref[0], go_ref[...]) + dot(fp_ref[0], gp_ref[...])
-    out_ref[0] = total.astype(out_ref.dtype)
-
-
-def weight_terms(slots, own_t, partner_t, grad, partner_grad, kind):
+    )(indices, key_grad, value_grad, key_weight, value_weight)
+
+
+def weight_kernel(count, index_ref, fo_ref, fp_ref, go_ref, gp_ref, *refs):
+    turned = jnp.concatenate([fo_ref[0], fp_ref[0]], axis=1)
+    total = dot(turned, jnp.concatenate([go_ref[...], gp_ref[...]], axis=0))
+    for r in refs[:count]:
+        total += r[0].astype(F32)
+    refs[count][0] = total.astype(BF)
+
+
+def weight_terms(slots, own_t, partner_t, grad, partner_grad, adds=()):
     tokens, proj = grad.shape
     span = own_t.shape[1]
     number = slots.shape[0]
-    tile = min(512, proj)
+    tile = proj
     rows = pl.BlockSpec((1, span, tokens), lambda j, i, d: (d[i], 0, 0))
     cols = pl.BlockSpec((tokens, tile), lambda j, i, d: (0, j))
+    extra = [
+        pl.BlockSpec((1, span, tile), lambda j, i, d, last=a.shape[0] - 1: (last, 0, j)) for a in adds
+    ]
     return pl.pallas_call(
-        weight_kernel,
+        functools.partial(weight_kernel, len(adds)),
         grid_spec=pltpu.PrefetchScalarGridSpec(
             num_scalar_prefetch=1,
             grid=(proj // tile, number),
-            in_specs=[rows, rows, cols, cols],
+            in_specs=[rows, rows, cols, cols] + extra,
             out_specs=pl.BlockSpec((1, span, tile), lambda j, i, d: (i, 0, j)),
         ),
-        out_shape=jax.ShapeDtypeStruct((number, span, proj), kind),
+        out_shape=jax.ShapeDtypeStruct((number, span, proj), BF),
         compiler_params=params(60),
         cost_estimate=SMALL,
         name="weight_terms",
-    )(slots, own_t, partner_t, grad, partner_grad)
+    )(slots, own_t, partner_t, grad, partner_grad, *adds)
 
 
 def turn_kernel(aliased, core_ref, *refs):
@@ -338,7 +362,7 @@
     model = key_weight.shape[0]
     heads = log_decay.shape[1]
     width = proj // heads
-    per = 2 if heads % 2 == 0 else 1
+    per = 4 if heads % 4 == 0 else 1
     count = lax.axis_size("head")
     blocks = lax.axis_size("seq")
     here = lax.axis_index("head")
@@ -354,10 +378,12 @@
     def rows_of(weight, index):
         return lax.dynamic_slice_in_dim(weight, index * depth, depth, 0)
 
-    def project(sums, shard, index):
-        key_part = dot(shard, rows_of(key_weight, index))
-        value_part = dot(shard, rows_of(value_weight, index))
-        return [key_part, value_part] if sums is None else [sums[0] + key_part, sums[1] + value_part]
+    def project(sums, shard, key_rows, value_rows):
+        parts = [dot(shard, key_rows), dot(shard, value_rows)]
+        return parts if sums is None else [a + b for a, b in zip(sums, parts)]
+
+    def both_rows(index):
+        return rows_of(key_weight, index), rows_of(value_weight, index)
 
     if chips:
         core = lax.rem(place, 2)
@@ -376,7 +402,7 @@
             slots_of(chip ^ 2),
             slots_of(chip),
         )
-    sums = project(None, features, here)
+    sums = project(None, features, *both_rows(here))
     slots = [features]
     turned = ()
     merged = None
@@ -388,24 +414,32 @@
             got = [up, down]
         else:
             got = [lax.ppermute(merged, "head", upward + downward)]
+        if 2 * step >= count:
+            index = jnp.where(here >= step, here - step, jnp.minimum(here + step, count - 1))
+            rows = [both_rows(index)]
+        else:
+            rows = [
+                both_rows(jnp.minimum(here + step, count - 1)),
+                both_rows(jnp.maximum(here - step, 0)),
+            ]
         if chips and step == count - 2:
             turned = turn_features(core, slots, 0, 5)
-            got, sums, turned, totals, ranks = together(got, sums, turned, totals, ranks)
+            got, sums, turned, totals, ranks, cum, cum_t = together(
+                got, sums, turned, totals, ranks, cum, cum_t
+            )
+        elif step == count - 1:
+            got, sums, rows = together(got, sums, rows)
         else:
             got, sums = together(got, sums)
         if 2 * step >= count:
-            index = jnp.where(here >= step, here - step, jnp.minimum(here + step, count - 1))
             merged = got[0] if len(got) == 1 else got[0] + got[1]
-            shards = [(merged, index)]
+            shards = [merged]
         else:
             up, down = got
-            shards = [
-                (down, jnp.minimum(here + step, count - 1)),
-                (up, jnp.maximum(here - step, 0)),
-            ]
-        slots += [shard for shard, _ in shards]
-        for shard, index in shards:
-            sums = project(sums, shard, index)
+            shards = [down, up]
+        slots += shards
+        for shard, pair in zip(shards, rows):
+            sums = project(sums, shard, *pair)
     key_sum, value_sum = sums
     keys, values = key_sum.astype(BF), value_sum.astype(BF)
 
@@ -471,7 +505,7 @@
 
     def terms(*indices):
         return feature_terms(
-            jnp.stack(indices), key_grad, value_grad, key_weight, value_weight, (), depth
+            jnp.stack(indices), key_grad, value_grad, key_weight, value_weight, depth
         )
 
     def add(*terms):
@@ -517,8 +551,8 @@
     away_x, away_y, one_x, one_y, home = ranks
     partner_key, partner_value = swap(key_grad, 1), swap(value_grad, 1)
 
-    def blocks_for(slot, grad, partner_grad, kind=BF):
-        return weight_terms(slot, own_t, partner_t, grad, partner_grad, kind)
+    def blocks_for(slot, grad, partner_grad, adds=()):
+        return weight_terms(slot, own_t, partner_t, grad, partner_grad, adds)
 
     first = either_term(1)
     got = send(1, first, first)
@@ -547,15 +581,15 @@
     value_sent = add(value_pass[0], got_value[0])
     value_sent, key_grad, value_grad = together(value_sent, key_grad, value_grad)
     got_value_pass = swap(value_sent, 2)
-    key_own = blocks_for(home, key_grad, partner_key, F32)[0]
-    value_own = blocks_for(home, value_grad, partner_value, F32)[0]
+    key_own = blocks_for(home, key_grad, partner_key, (got_key,))[0]
+    value_own = blocks_for(home, value_grad, partner_value, (got_value,))[0]
     feature_own = terms(here)[0]
     up, key_own, value_own = together(up, key_own, value_own)
     feature_grad = add(feature_own, up, down)
     got_key_pass, feature_grad = together(got_key_pass, feature_grad)
-    key_out = (key_own + got_key[1].astype(F32) + got_key_pass.astype(F32)) * norm
+    key_out = (key_own.astype(F32) + got_key_pass.astype(F32)) * norm
     got_value_pass, key_out = together(got_value_pass, key_out)
-    value_out = (value_own + got_value[1].astype(F32) + got_value_pass.astype(F32)) * norm
+    value_out = (value_own.astype(F32) + got_value_pass.astype(F32)) * norm
     return attended, query_grad, feature_grad, key_out, value_out
 
 

time: 260 us -> 256 us (0.985)
  waiting for transfers between devices: 40.2 us -> 37.3 us
  local copies, waits for them, and re-layouts: 2.77 us -> 5.43 us
    dynamic_slice x0 -> x1, local copies, waits for them, and re-layouts: none -> 2.67 us  [rows_of(): return lax.dynamic_slice_in_dim(weight, index * depth, depth, 0)]
    ppermute x1, waiting for transfers between devices: 17.7 us -> 15.1 us  [per_device(): got = [lax.ppermute(merged, 'head', upward + downward)]]
  transfers between devices with their start and end apart: 28 -> 28, of which waited for: 12 -> 13; matrix products, arithmetic and copies ran while one was open for 21% -> 22% of each run, Pallas kernels for 36% -> 36%
where the time goes in v3:
time: 256 us; the launch traced here: 255 us
  Pallas kernels  97.8 us (38%)
  starting transfers between devices  48 us (19%)
  waiting for transfers between devices  37.3 us (15%)
  matrix products  35.7 us (14%)
  other arithmetic  29.6 us (12%)
  local copies, waits for them, and re-layouts  5.43 us (2%)
    dot_general x10, matrix products, dot(): return jnp.dot(a, b, preferred_element_type=F32)  35.7 us
    pallas_call x6, Pallas kernels, per_head(): pl.pallas_call(functools.partial(kernel, width, per), grid=(heads // per,...  31.1 us
    pallas_call x6, Pallas kernels, weight_terms(): pl.pallas_call(functools.partial(weight_kernel, len(adds)), grid_spec=plt...  29.4 us
    pallas_call x4, Pallas kernels, feature_terms(): pl.pallas_call(feature_kernel, grid_spec=pltpu.PrefetchScalarGridSpec(num...  26.1 us
    ppermute x18, starting transfers between devices, swap(): return lax.ppermute(x, 'seq', pairs)  21 us
    ppermute x1, waiting for transfers between devices, per_device(): got = [lax.ppermute(merged, 'head', upward + downward)]  15.1 us
    convert_element_type x5, other arithmetic, add(): return sum((t.astype(F32) for t in terms)).astype(BF)  12.5 us
    ppermute x2, starting transfers between devices, send(): lax.ppermute(up_sum, 'head', upward)  12.2 us
  transfers between devices with their start and end apart: 28, of which 13 were waited for; matrix products, arithmetic and copies ran while one was open for 22% of the time, Pallas kernels for 36%

profile of v3, /device:TPU:0, one launch (start us, length us, event | category | flops | bytes accessed | tf_op | source)
XLA Modules:
  0.0 255.0 jit_solution(4525180092730289924)
XLA Ops:
  1.9 6.5 %collective-permute-start = (bf16[512,1024]{1,0:T(8,128)(2,1)}, bf16[512,1024]{1,0:T(8,128)(2,1)}, u32[]{:S(2)}, u32[]{:S(2)}) collective-permute-start(bf16[512,1024]{1,0:T(8,128)(2,1)} %refs_0_.1), channel_id=1, source_target_pairs={{0,1},{1,2},{2,3},{4,5},{5,6},{6,7},{8,9},{9,10},{10,11},{12,13},{... | collective-permute-start | bytes 3145736 | tf_op jit(solution)/shard_map/ppermute | solution.py:412
  8.5 2.2 reduce-window.6
  11.2 3.2 %fusion.23 = f32[512,1024]{1,0:T(8,128)S(1)} fusion(bf16[512,1024]{1,0:T(8,128)(2,1)} %refs_0_.1, bf16[4096,1024]{1,0:T(8,128)(2,1)} %vw_ref.7, s32[]{:T(128)S(6)} %select_n.201), kind=kOutput, calls=%fused_computation.33 | convolution fusion | flops 1073741824 | bytes 5242884 | tf_op jit(solution)/shard_map/dot_general | solution.py:18
  14.5 4.2 %fusion.20 = f32[512,1024]{1,0:T(8,128)} fusion(bf16[512,1024]{1,0:T(8,128)(2,1)S(1)} %copy-done.17, bf16[4096,1024]{1,0:T(8,128)(2,1)} %kw_ref.7, s32[]{:T(128)S(6)} %select_n.201), kind=kOutput, calls=%fused_computation.32 | convolution fusion | flops 1073741824 | bytes 5242884 | tf_op jit(solution)/shard_map/dot_general | solution.py:18
  19.3 2.0 collective-permute-start.5
  23.0 2.0 collective-permute-start.6
  26.7 2.3 collective-permute-done.1.refs_1_
  32.2 4.5 %fusion.10 = f32[512,1024]{1,0:T(8,128)} fusion(bf16[512,1024]{1,0:T(8,128)(2,1)} %collective-permute-done.1.refs_1_, bf16[4096,1024]{1,0:T(8,128)(2,1)} %vw_ref.7, s32[]{:T(128)S(6)} %select_n.202), kind=kOutput, calls=%fused_computation.21 | convolution fusion | flops 1073741824 | bytes 5242884 | tf_op jit(solution)/shard_map/dot_general | solution.py:18
  36.7 4.5 %fusion.14 = f32[512,1024]{1,0:T(8,128)} fusion(bf16[512,1024]{1,0:T(8,128)(2,1)} %collective-permute-done.1.refs_1_, bf16[4096,1024]{1,0:T(8,128)(2,1)} %kw_ref.7, s32[]{:T(128)S(6)} %select_n.202), kind=kOutput, calls=%fused_computation.26 | convolution fusion | flops 1073741824 | bytes 5242884 | tf_op jit(solution)/shard_map/dot_general | solution.py:18
  41.2 6.6 %turn_features.2 = (bf16[5,512,512]{2,1,0:T(8,128)(2,1)}, bf16[5,512,512]{2,1,0:T(8,128)(2,1)}) custom-call(s32[1]{0:T(128)} %bitcast.2.core_ref, bf16[512,1024]{1,0:T(8,128)(2,1)} %refs_0_.1, bf16[512,1024]{1,0:T(8,128)(2,1)} %collective-permute-done.1.refs_1_, bf16[512,1024]{1,0:T(8,128)(2,1)} %collective-permute-done.refs_2_), custom_call_target="tpu_custom_call" | custom-call | flops 1 | bytes 1 | tf_op jit(solution)/shard_map/turn_features/pallas_call | solution.py:253
  47.8 5.3 %add_add_fusion = f32[512,1024]{1,0:T(8,128)} fusion(f32[512,1024]{1,0:T(8,128)S(1)} %fusion.23, f32[512,1024]{1,0:T(8,128)} %fusion.10, bf16[512,1024]{1,0:T(8,128)(2,1)} %collective-permute-done.refs_2_, bf16[4096,1024]{1,0:T(8,128)(2,1)} %vw_ref.7, s32[]{:T(128)S(6)} %select_n.203), kind=kOutput, calls=%fused_computation.20 | convolution fusion | flops 1074790400 | bytes 9437188 | tf_op jit(solution)/shard_map/dot_general | solution.py:18
  53.1 3.2 %add_add_fusion.1 = f32[512,1024]{1,0:T(8,128)S(1)} fusion(f32[512,1024]{1,0:T(8,128)S(1)} %copy-done.14, f32[512,1024]{1,0:T(8,128)S(1)} %copy-done.15, bf16[512,1024]{1,0:T(8,128)(2,1)} %collective-permute-done.refs_2_, bf16[4096,1024]{1,0:T(8,128)(2,1)} %kw_ref.7, s32[]{:T(128)S(6)} %select_n.203), kind=kOutput, calls=%fused_computation.25 | convolution fusion | flops 1074790400 | bytes 9437188 | tf_op jit(solution)/shard_map/dot_general | solution.py:18
  56.3 4.1 %collective-permute-done.3 = bf16[512,1024]{1,0:T(8,128)(2,1)} collective-permute-done((bf16[512,1024]{1,0:T(8,128)(2,1)}, bf16[512,1024]{1,0:T(8,128)(2,1)}, u32[]{:S(2)}, u32[]{:S(2)}) %collective-permute-start.3) | collective-permute-done | bytes 1048608 | tf_op jit(solution)/shard_map/ppermute | solution.py:413
  63.9 2.7 %constant_dynamic-slice_fusion.6 = (bf16[1024,1024]{1,0:T(8,128)(2,1)S(1)}, bf16[1024,1024]{1,0:T(8,128)(2,1)S(1)}) fusion(bf16[4096,1024]{1,0:T(8,128)(2,1)} %vw_ref.7, s32[]{:T(128)S(6)} %select_n.232, bf16[4096,1024]{1,0:T(8,128)(2,1)} %kw_ref.7), kind=kLoop, calls=%fused_computation.82 | loop fusion | bytes 8388612 | tf_op jit(solution)/shard_map/dynamic_slice | solution.py:379
  66.6 3.0 %fusion.4 = f32[512,1024]{1,0:T(8,128)S(1)} fusion(bf16[512,1024]{1,0:T(8,128)(2,1)S(1)} %add.211.refs_2_, bf16[4096,1024]{1,0:T(8,128)(2,1)} %vw_ref.7, s32[]{:T(128)S(6)} %select_n.230), kind=kOutput, calls=%fused_computation.14 | convolution fusion | flops 1073741824 | bytes 5242884 | tf_op jit(solution)/shard_map/dot_general | solution.py:18
  70.1 2.8 %fusion.6 = f32[512,1024]{1,0:T(8,128)S(1)} fusion(bf16[512,1024]{1,0:T(8,128)(2,1)S(1)} %add.211.refs_2_, bf16[4096,1024]{1,0:T(8,128)(2,1)} %kw_ref.7, s32[]{:T(128)S(6)} %select_n.230), kind=kOutput, calls=%fused_computation.16 | convolution fusion | flops 1073741824 | bytes 5242884 | tf_op jit(solution)/shard_map/dot_general | solution.py:18
  73.4 15.1 %collective-permute-done.7.refs_3_ = bf16[512,1024]{1,0:T(8,128)(2,1)} collective-permute-done((bf16[512,1024]{1,0:T(8,128)(2,1)S(1)}, bf16[512,1024]{1,0:T(8,128)(2,1)}, u32[]{:S(2)}, u32[]{:S(2)}) %collective-permute-start.7) | collective-permute-done | bytes 1048608 | tf_op jit(solution)/shard_map/ppermute | solution.py:416
  88.5 2.5 fusion.57
  91.0 2.5 fusion.58
  95.0 2.0 local_state.1
  101.2 5.3 %local_mix.1.mix_ref = bf16[512,1024]{1,0:T(8,128)(2,1)} custom-call(f32[512,8]{1,0:T(8,128)} %bitcast.63, f32[8,512]{1,0:T(8,128)} %copy.22.cumt_ref, bf16[512,1024]{1,0:T(8,128)(2,1)} %q_ref.5, bf16[512,1024]{1,0:T(8,128)(2,1)} %copy-done, bf16[512,1024]{1,0:T(8,128)(2,1)} %copy-done.1), custom_call_target="tpu_custom_call" | custom-call | flops 1 | bytes 1 | tf_op jit(solution)/shard_map/local_mix/pallas_call | solution.py:159
  106.7 3.7 %collective-permute-start.10 = (bf16[4,128,128]{2,1,0:T(8,128)(2,1)S(1)}, bf16[4,128,128]{2,1,0:T(8,128)(2,1)S(1)}, u32[]{:S(2)}, u32[]{:S(2)}) collective-permute-start(bf16[4,128,128]{2,1,0:T(8,128)(2,1)S(1)} %fusion.33), channel_id=1, source_target_pairs={{0,16},{4,20},{8,24},{12,28},{1,17},{5,21},{9,25},{13,29},{2,18},{... | collective-permute-start | bytes 393224 | tf_op jit(solution)/shard_map/ppermute | solution.py:298
  110.4 4.6 %turn_features.3 = (bf16[5,512,512]{2,1,0:T(8,128)(2,1)}, bf16[5,512,512]{2,1,0:T(8,128)(2,1)}) custom-call(s32[1]{0:T(128)} %bitcast.2.core_ref, bf16[5,512,512]{2,1,0:T(8,128)(2,1)} %get-tuple-element.103.refs_0_, bf16[5,512,512]{2,1,0:T(8,128)(2,1)} %get-tuple-element.104.refs_1_, ...), custom_call_target="tpu_custom_call", output_to_operand_aliasing={{0}: (1, {}), {1}: (2, {})} | custom-call | flops 1 | bytes 1 | tf_op jit(solution)/shard_map/turn_features/pallas_call | solution.py:253
  117.6 5.6 %norm_grad.1 = (bf16[512,1024]{1,0:T(8,128)(2,1)}, bf16[512,1024]{1,0:T(8,128)(2,1)}, bf16[8,128,128]{2,1,0:T(8,128)(2,1)}) custom-call(f32[512,8]{1,0:T(8,128)} %bitcast.64, bf16[512,1024]{1,0:T(8,128)(2,1)} %q_ref.5, bf16[512,1024]{1,0:T(8,128)(2,1)} %g_ref.1, bf16[512,1024]{1,0:T(8,128)(2,1)} %local_mix.1.mix_ref, bf16[8,128,128]{2,1,0:T(8,128)(2,1)} %fusion.28.s_ref), custom_call_target="tpu_custom_call" | custom-call | flops 1 | bytes 1 | tf_op jit(solution)/shard_map/norm_grad/pallas_call | solution.py:159
  126.6 5.3 %back_query.1 = bf16[512,1024]{1,0:T(8,128)(2,1)} custom-call(f32[512,8]{1,0:T(8,128)} %bitcast.65, f32[8,512]{1,0:T(8,128)} %copy.22.cumt_ref, bf16[512,1024]{1,0:T(8,128)(2,1)} %copy-done, bf16[512,1024]{1,0:T(8,128)(2,1)} %copy-done.1, bf16[512,1024]{1,0:T(8,128)(2,1)} %get-tuple-element.112.hg_ref, bf16[8,128,128]{2,1,0:T(8,128)(2,1)} %fusion.28.s_ref), custom_call_target="tpu_custom_call" | custom-call | flops 1 | bytes 1 | tf_op jit(solution)/shard_map/back_query/pallas_call | solution.py:159
  133.4 8.3 %back_keys.1 = (bf16[512,1024]{1,0:T(8,128)(2,1)}, bf16[512,1024]{1,0:T(8,128)(2,1)}) custom-call(f32[512,8]{1,0:T(8,128)} %bitcast.66, f32[8,512]{1,0:T(8,128)} %copy.22.cumt_ref, bf16[512,1024]{1,0:T(8,128)(2,1)} %q_ref.5, bf16[512,1024]{1,0:T(8,128)(2,1)} %copy-done, bf16[512,1024]{1,0:T(8,128)(2,1)} %copy-done.1, bf16[512,1024]{1,0:T(8,128)(2,1)} %get-tuple-element.112.hg_ref), custom_call_target="tpu_custom_call" | custom-call | flops 1 | bytes 1 | tf_op jit(solution)/shard_map/back_keys/pallas_call | solution.py:159
  144.2 4.5 %close_back.1 = (bf16[512,1024]{1,0:T(8,128)(2,1)}, bf16[512,1024]{1,0:T(8,128)(2,1)}) custom-call(f32[512,8]{1,0:T(8,128)} %bitcast.67, bf16[512,1024]{1,0:T(8,128)(2,1)} %copy-done, bf16[512,1024]{1,0:T(8,128)(2,1)} %copy-done.1, bf16[512,1024]{1,0:T(8,128)(2,1)} %get-tuple-element.118.kl_ref, bf16[512,1024]{1,0:T(8,128)(2,1)} %get-tuple-element.119.vl_ref, ...), custom_call_target="tpu_custom_call" | custom-call | flops 1 | bytes 1 | tf_op jit(solution)/shard_map/close_back/pallas_call | solution.py:159
  149.3 5.6 %feature_terms.4 = bf16[1,512,1024]{2,1,0:T(8,128)(2,1)} custom-call(s32[1]{0:T(128)} %bitcast.17.index_ref, bf16[512,1024]{1,0:T(8,128)(2,1)} %get-tuple-element.148.kg_ref.go_ref, bf16[512,1024]{1,0:T(8,128)(2,1)} %get-tuple-element.149.vg_ref.go_ref, bf16[4096,1024]{1,0:T(8,128)(2,1)} %kw_ref.7, bf16[4096,1024]{1,0:T(8,128)(2,1)} %vw_ref.7), custom_call_target="tpu_custom_call" | custom-call | flops 1 | bytes 1 | tf_op jit(solution)/shard_map/feature_terms/pallas_call | solution.py:184
  157.2 6.1 %weight_terms.6 = bf16[2,512,1024]{2,1,0:T(8,128)(2,1)} custom-call(s32[2]{0:T(128)} %get-tuple-element.126.index_ref, bf16[5,512,512]{2,1,0:T(8,128)(2,1)} %get-tuple-element.124.fo_ref, bf16[5,512,512]{2,1,0:T(8,128)(2,1)} %copy-done.3, bf16[512,1024]{1,0:T(8,128)(2,1)} %get-tuple-element.148.kg_ref.go_ref, bf16[512,1024]{1,0:T(8,128)(2,1)} %copy-done.4), custom_call_target="tpu_custom_call" | custom-call | flops 1 | bytes 1 | tf_op jit(solution)/shard_map/weight_terms/pallas_call | solution.py:217
  164.9 6.1 %weight_terms.7 = bf16[2,512,1024]{2,1,0:T(8,128)(2,1)} custom-call(s32[2]{0:T(128)} %get-tuple-element.123.index_ref, bf16[5,512,512]{2,1,0:T(8,128)(2,1)} %get-tuple-element.124.fo_ref, bf16[5,512,512]{2,1,0:T(8,128)(2,1)} %copy-done.3, bf16[512,1024]{1,0:T(8,128)(2,1)} %get-tuple-element.149.vg_ref.go_ref, bf16[512,1024]{1,0:T(8,128)(2,1)} %copy-done.5), custom_call_target="tpu_custom_call" | custom-call | flops 1 | bytes 1 | tf_op jit(solution)/shard_map/weight_terms/pallas_call | solution.py:217
  170.9 2.6 %collective-permute-start.23 = (bf16[2,512,1024]{2,1,0:T(8,128)(2,1)}, bf16[2,512,1024]{2,1,0:T(8,128)(2,1)}, u32[]{:S(2)}, u32[]{:S(2)}) collective-permute-start(bf16[2,512,1024]{2,1,0:T(8,128)(2,1)} %weight_terms.7), channel_id=1, source_target_pairs={{0,16},{4,20},{8,24},{12,28},{16,0},{20,4},{24,8},{28,12},{1,17},{... | collective-permute-start | bytes 6291464 | tf_op jit(solution)/shard_map/ppermute | solution.py:298
  173.6 5.6 %feature_terms.5 = bf16[1,512,1024]{2,1,0:T(8,128)(2,1)} custom-call(s32[1]{0:T(128)} %bitcast.19.index_ref, bf16[512,1024]{1,0:T(8,128)(2,1)} %get-tuple-element.148.kg_ref.go_ref, bf16[512,1024]{1,0:T(8,128)(2,1)} %get-tuple-element.149.vg_ref.go_ref, bf16[4096,1024]{1,0:T(8,128)(2,1)} %kw_ref.7, bf16[4096,1024]{1,0:T(8,128)(2,1)} %vw_ref.7), custom_call_target="tpu_custom_call" | custom-call | flops 1 | bytes 1 | tf_op jit(solution)/shard_map/feature_terms/pallas_call | solution.py:184
  179.4 2.6 %add_convert_fusion.2 = bf16[512,1024]{1,0:T(8,128)(2,1)} fusion(bf16[512,1024]{1,0:T(8,128)(2,1)S(1)} %collective-permute-done.17, bf16[512,1024]{1,0:T(8,128)(2,1)} %bitcast.68), kind=kLoop, calls=%fused_computation.11 | loop fusion | flops 2097152 | bytes 3145728 | tf_op jit(solution)/shard_map/convert_element_type | solution.py:512
  182.7 5.8 %collective-permute-start.20 = (bf16[512,1024]{1,0:T(8,128)(2,1)}, bf16[512,1024]{1,0:T(8,128)(2,1)}, u32[]{:S(2)}, u32[]{:S(2)}) collective-permute-start(bf16[512,1024]{1,0:T(8,128)(2,1)} %add_convert_fusion.2), channel_id=1, source_target_pairs={{0,1},{1,2},{4,5},{5,6},{8,9},{9,10},{12,13},{13,14},{16,17},{17,1... | collective-permute-start | bytes 3145736 | tf_op jit(solution)/shard_map/ppermute | solution.py:527
  189.2 9.4 %feature_terms.6 = bf16[2,512,1024]{2,1,0:T(8,128)(2,1)} custom-call(s32[2]{0:T(128)} %pad_add_fusion.index_ref, bf16[512,1024]{1,0:T(8,128)(2,1)} %get-tuple-element.148.kg_ref.go_ref, bf16[512,1024]{1,0:T(8,128)(2,1)} %get-tuple-element.149.vg_ref.go_ref, bf16[4096,1024]{1,0:T(8,128)(2,1)} %kw_ref.7, bf16[4096,1024]{1,0:T(8,128)(2,1)} %vw_ref.7), custom_call_target="tpu_custom_call" | custom-call | flops 1 | bytes 1 | tf_op jit(solution)/shard_map/feature_terms/pallas_call | solution.py:184
  198.6 4.1 %weight_terms.9 = bf16[1,512,1024]{2,1,0:T(8,128)(2,1)} custom-call(s32[1]{0:T(128)S(6)} %select_n.219.index_ref, bf16[5,512,512]{2,1,0:T(8,128)(2,1)} %get-tuple-element.124.fo_ref, bf16[5,512,512]{2,1,0:T(8,128)(2,1)} %copy-done.3, bf16[512,1024]{1,0:T(8,128)(2,1)} %get-tuple-element.149.vg_ref.go_ref, bf16[512,1024]{1,0:T(8,128)(2,1)} %copy-done.5), custom_call_target="tpu_custom_call" | custom-call | flops 1 | bytes 1 | tf_op jit(solution)/shard_map/weight_terms/pallas_call | solution.py:217
  202.7 4.2 %weight_terms.8 = bf16[1,512,1024]{2,1,0:T(8,128)(2,1)} custom-call(s32[1]{0:T(128)S(6)} %select_n.221.index_ref, bf16[5,512,512]{2,1,0:T(8,128)(2,1)} %get-tuple-element.124.fo_ref, bf16[5,512,512]{2,1,0:T(8,128)(2,1)} %copy-done.3, bf16[512,1024]{1,0:T(8,128)(2,1)} %get-tuple-element.148.kg_ref.go_ref, bf16[512,1024]{1,0:T(8,128)(2,1)} %copy-done.4), custom_call_target="tpu_custom_call" | custom-call | flops 1 | bytes 1 | tf_op jit(solution)/shard_map/weight_terms/pallas_call | solution.py:217
  206.9 3.2 %collective-permute-done.20 = bf16[512,1024]{1,0:T(8,128)(2,1)} collective-permute-done((bf16[512,1024]{1,0:T(8,128)(2,1)}, bf16[512,1024]{1,0:T(8,128)(2,1)}, u32[]{:S(2)}, u32[]{:S(2)}) %collective-permute-start.20) | collective-permute-done | bytes 1048608 | tf_op jit(solution)/shard_map/ppermute | solution.py:527
  210.2 3.5 %fusion.2 = (bf16[512,1024]{1,0:T(8,128)(2,1)}, bf16[512,1024]{1,0:T(8,128)(2,1)}) fusion(bf16[512,1024]{1,0:T(8,128)(2,1)S(1)} %collective-permute-done.21, bf16[2,512,1024]{2,1,0:T(8,128)(2,1)S(1)} %copy-done.7, bf16[512,1024]{1,0:T(8,128)(2,1)} %collective-permute-done.20), kind=kLoop, calls=%fused_computation.4 | loop fusion | flops 4194304 | bytes 6291456 | tf_op jit(solution)/shard_map/convert_element_type | solution.py:512
  213.7 6.4 %collective-permute-start.25 = (bf16[512,1024]{1,0:T(8,128)(2,1)}, bf16[512,1024]{1,0:T(8,128)(2,1)}, u32[]{:S(2)}, u32[]{:S(2)}) collective-permute-start(bf16[512,1024]{1,0:T(8,128)(2,1)} %get-tuple-element.150), channel_id=1, source_target_pairs={{0,1},{1,2},{2,3},{4,5},{5,6},{6,7},{8,9},{9,10},{10,11},{12,13},{... | collective-permute-start | bytes 3145736 | tf_op jit(solution)/shard_map/ppermute | solution.py:527
  223.0 2.7 %collective-permute-start.24 = (bf16[512,1024]{1,0:T(8,128)(2,1)S(1)}, bf16[512,1024]{1,0:T(8,128)(2,1)}, u32[]{:S(2)}, u32[]{:S(2)}) collective-permute-start(bf16[512,1024]{1,0:T(8,128)(2,1)S(1)} %fusion.26), channel_id=1, source_target_pairs={{0,16},{4,20},{8,24},{12,28},{16,0},{20,4},{24,8},{28,12},{1,17},{... | collective-permute-start | bytes 3145736 | tf_op jit(solution)/shard_map/ppermute | solution.py:298
  228.9 4.4 %weight_terms.11 = bf16[1,512,1024]{2,1,0:T(8,128)(2,1)} custom-call(s32[1]{0:T(128)S(6)} %select_n.223.index_ref, bf16[5,512,512]{2,1,0:T(8,128)(2,1)} %get-tuple-element.124.fo_ref, bf16[5,512,512]{2,1,0:T(8,128)(2,1)} %copy-done.3, bf16[512,1024]{1,0:T(8,128)(2,1)} %get-tuple-element.149.vg_ref.go_ref, bf16[512,1024]{1,0:T(8,128)(2,1)} %copy-done.5, ...), custom_call_target="tpu_custom_call" | custom-call | flops 1 | bytes 1 | tf_op jit(solution)/shard_map/weight_terms/pallas_call | solution.py:217
  233.4 5.6 %feature_terms.7 = bf16[1,512,1024]{2,1,0:T(8,128)(2,1)} custom-call(s32[1]{0:T(128)} %bitcast.10.index_ref, bf16[512,1024]{1,0:T(8,128)(2,1)} %get-tuple-element.148.kg_ref.go_ref, bf16[512,1024]{1,0:T(8,128)(2,1)} %get-tuple-element.149.vg_ref.go_ref, bf16[4096,1024]{1,0:T(8,128)(2,1)} %kw_ref.7, bf16[4096,1024]{1,0:T(8,128)(2,1)} %vw_ref.7), custom_call_target="tpu_custom_call" | custom-call | flops 1 | bytes 1 | tf_op jit(solution)/shard_map/feature_terms/pallas_call | solution.py:184
  238.9 4.5 %weight_terms.10 = bf16[1,512,1024]{2,1,0:T(8,128)(2,1)} custom-call(s32[1]{0:T(128)S(6)} %select_n.223.index_ref, bf16[5,512,512]{2,1,0:T(8,128)(2,1)} %get-tuple-element.124.fo_ref, bf16[5,512,512]{2,1,0:T(8,128)(2,1)} %copy-done.3, bf16[512,1024]{1,0:T(8,128)(2,1)} %get-tuple-element.148.kg_ref.go_ref, bf16[512,1024]{1,0:T(8,128)(2,1)} %copy-done.4, ...), custom_call_target="tpu_custom_call" | custom-call | flops 1 | bytes 1 | tf_op jit(solution)/shard_map/weight_terms/pallas_call | solution.py:217
  243.4 2.4 collective-permute-done.26
  245.9 3.1 %fusion.1 = bf16[512,1024]{1,0:T(8,128)(2,1)} fusion(bf16[512,1024]{1,0:T(8,128)(2,1)} %collective-permute-done.26, bf16[512,1024]{1,0:T(8,128)(2,1)} %collective-permute-done.25, bf16[1,512,1024]{2,1,0:T(8,128)(2,1)S(1)} %copy-done.10), kind=kLoop, calls=%fused_computation.2 | loop fusion | flops 3145728 | bytes 4194304 | tf_op jit(solution)/shard_map/convert_element_type | solution.py:512
  249.0 3.0 %add_multiply_fusion.1 = f32[512,1024]{1,0:T(8,128)} fusion(bf16[512,1024]{1,0:T(8,128)(2,1)} %collective-permute-done.24, bf16[512,1024]{1,0:T(8,128)(2,1)S(1)} %bitcast.70), kind=kLoop, calls=%fused_computation.8 | loop fusion | flops 2097152 | bytes 4194304 | tf_op jit(solution)/shard_map/mul | solution.py:590
  252.1 3.0 %add_multiply_fusion = f32[512,1024]{1,0:T(8,128)} fusion(bf16[512,1024]{1,0:T(8,128)(2,1)} %collective-permute-done.27, bf16[512,1024]{1,0:T(8,128)(2,1)S(1)} %bitcast.69), kind=kLoop, calls=%fused_computation.7 | loop fusion | flops 2097152 | bytes 4194304 | tf_op jit(solution)/shard_map/mul | solution.py:592
  (114 shorter events, 41.2 us)
Async XLA Ops:
  0.6 28.4 %collective-permute-start.1 = (bf16[512,1024]{1,0:T(8,128)(2,1)}, bf16[512,1024]{1,0:T(8,128)(2,1)}, u32[]{:S(2)}, u32[]{:S(2)}) collective-permute-start(bf16[512,1024]{1,0:T(8,128)(2,1)} %refs_0_.1), channel_id=1, source_target_pairs={{1,0},{2,1},{3,2},{5,4},{6,5},{7,6},{9,8},{10,9},{11,10},{13,12},{... | collective-permute-start | bytes 3145736 | tf_op jit(solution)/shard_map/ppermute | solution.py:413
  1.9 28.3 %collective-permute-start = (bf16[512,1024]{1,0:T(8,128)(2,1)}, bf16[512,1024]{1,0:T(8,128)(2,1)}, u32[]{:S(2)}, u32[]{:S(2)}) collective-permute-start(bf16[512,1024]{1,0:T(8,128)(2,1)} %refs_0_.1), channel_id=1, source_target_pairs={{0,1},{1,2},{2,3},{4,5},{5,6},{6,7},{8,9},{9,10},{10,11},{12,13},{... | collective-permute-start | bytes 3145736 | tf_op jit(solution)/shard_map/ppermute | solution.py:412
  11.1 89.3 %copy-start.2 = (f32[8,4,128]{0,2,1:T(8,128)}, f32[8,4,128]{0,2,1:T(8,128)S(1)}, u32[]{:S(2)}) copy-start(f32[8,4,128]{0,2,1:T(8,128)S(1)} %copy.21) | copy-start | bytes 49156
  11.1 8.2 %collective-permute-start.4 = (f32[1,8]{1,0:T(1,128)S(1)}, f32[1,8]{1,0:T(1,128)S(1)}, u32[]{:S(2)}, u32[]{:S(2)}) collective-permute-start(f32[1,8]{1,0:T(1,128)S(1)} %slice.29), channel_id=1, source_target_pairs={{0,4},{4,0},{8,12},{12,8},{16,20},{20,16},{24,28},{28,24},{1,5},{5... | collective-permute-start | bytes 104 | tf_op jit(solution)/shard_map/ppermute | solution.py:298
  11.2 3.3 %copy-start.17 = (bf16[512,1024]{1,0:T(8,128)(2,1)S(1)}, bf16[512,1024]{1,0:T(8,128)(2,1)}, u32[]{:S(2)}) copy-start(bf16[512,1024]{1,0:T(8,128)(2,1)} %refs_0_.1) | copy-start | bytes 3145732
  19.3 3.6 %collective-permute-start.5 = (f32[2,8]{1,0:T(2,128)S(1)}, f32[2,8]{1,0:T(2,128)S(1)}, u32[]{:S(2)}, u32[]{:S(2)}) collective-permute-start(f32[2,8]{1,0:T(2,128)S(1)} %pad_maximum_fusion.2), channel_id=1, source_target_pairs={{0,8},{4,12},{8,0},{12,4},{16,24},{20,28},{24,16},{28,20},{1,9},{5... | collective-permute-start | bytes 200 | tf_op jit(solution)/shard_map/ppermute | solution.py:298
  23.0 3.7 %collective-permute-start.6 = (f32[4,8]{1,0:T(4,128)S(1)}, f32[4,8]{1,0:T(4,128)S(1)}, u32[]{:S(2)}, u32[]{:S(2)}) collective-permute-start(f32[4,8]{1,0:T(4,128)S(1)} %pad_maximum_fusion.1), channel_id=1, source_target_pairs={{0,16},{4,20},{8,24},{12,28},{16,0},{20,4},{24,8},{28,12},{1,17},{... | collective-permute-start | bytes 392 | tf_op jit(solution)/shard_map/ppermute | solution.py:298
  30.2 26.1 %collective-permute-start.2 = (bf16[512,1024]{1,0:T(8,128)(2,1)}, bf16[512,1024]{1,0:T(8,128)(2,1)S(1)}, u32[]{:S(2)}, u32[]{:S(2)}) collective-permute-start(bf16[512,1024]{1,0:T(8,128)(2,1)} %collective-permute-done.refs_2_), channel_id=1, source_target_pairs={{1,2},{2,3},{5,6},{6,7},{9,10},{10,11},{13,14},{14,15},{17,18},{18... | collective-permute-start | bytes 3145736 | tf_op jit(solution)/shard_map/ppermute | solution.py:412
  30.9 29.5 %collective-permute-start.3 = (bf16[512,1024]{1,0:T(8,128)(2,1)}, bf16[512,1024]{1,0:T(8,128)(2,1)}, u32[]{:S(2)}, u32[]{:S(2)}) collective-permute-start(bf16[512,1024]{1,0:T(8,128)(2,1)} %collective-permute-done.1.refs_1_), channel_id=1, source_target_pairs={{1,0},{2,1},{5,4},{6,5},{9,8},{10,9},{13,12},{14,13},{17,16},{18,1... | collective-permute-start | bytes 3145736 | tf_op jit(solution)/shard_map/ppermute | solution.py:413
  47.8 5.3 %copy-start.14 = (f32[512,1024]{1,0:T(8,128)S(1)}, f32[512,1024]{1,0:T(8,128)}, u32[]{:S(2)}) copy-start(f32[512,1024]{1,0:T(8,128)} %fusion.20) | copy-start | bytes 6291460
  47.8 5.3 %copy-start.15 = (f32[512,1024]{1,0:T(8,128)S(1)}, f32[512,1024]{1,0:T(8,128)}, u32[]{:S(2)}) copy-start(f32[512,1024]{1,0:T(8,128)} %fusion.14) | copy-start | bytes 6291460
  56.3 4.1 %copy-start.16 = (bf16[512,1024]{1,0:T(8,128)(2,1)}, bf16[512,1024]{1,0:T(8,128)(2,1)S(1)}, u32[]{:S(2)}) copy-start(bf16[512,1024]{1,0:T(8,128)(2,1)S(1)} %collective-permute-done.2) | copy-start | bytes 3145732
  62.4 7.8 %copy-start.11 = (bf16[512,1024]{1,0:T(8,128)(2,1)}, bf16[512,1024]{1,0:T(8,128)(2,1)S(1)}, u32[]{:S(2)}) copy-start(bf16[512,1024]{1,0:T(8,128)(2,1)S(1)} %add.211.refs_2_) | copy-start | bytes 3145732
  62.4 26.1 %collective-permute-start.7 = (bf16[512,1024]{1,0:T(8,128)(2,1)S(1)}, bf16[512,1024]{1,0:T(8,128)(2,1)}, u32[]{:S(2)}, u32[]{:S(2)}) collective-permute-start(bf16[512,1024]{1,0:T(8,128)(2,1)S(1)} %add.211.refs_2_), channel_id=1, source_target_pairs={{2,3},{1,0},{6,7},{5,4},{10,11},{9,8},{14,15},{13,12},{18,19},{17,... | collective-permute-start | bytes 3145736 | tf_op jit(solution)/shard_map/ppermute | solution.py:416
  66.6 3.0 %copy-start.6 = (f32[512,1024]{1,0:T(8,128)S(1)}, f32[512,1024]{1,0:T(8,128)}, u32[]{:S(2)}) copy-start(f32[512,1024]{1,0:T(8,128)} %add_add_fusion) | copy-start | bytes 6291460
  94.0 1.0 copy-start
  95.0 6.2 %copy-start.1 = (bf16[512,1024]{1,0:T(8,128)(2,1)}, bf16[512,1024]{1,0:T(8,128)(2,1)S(1)}, u32[]{:S(2)}) copy-start(bf16[512,1024]{1,0:T(8,128)(2,1)S(1)} %add_convert_fusion.3.v_ref) | copy-start | bytes 3145732
  97.0 1.6 collective-permute-start.8
  98.8 7.8 %collective-permute-start.9 = (bf16[4,128,128]{2,1,0:T(8,128)(2,1)S(1)}, bf16[4,128,128]{2,1,0:T(8,128)(2,1)S(1)}, u32[]{:S(2)}, u32[]{:S(2)}) collective-permute-start(bf16[4,128,128]{2,1,0:T(8,128)(2,1)S(1)} %fusion.31), channel_id=1, source_target_pairs={{0,8},{4,12},{8,0},{12,4},{16,24},{20,28},{24,16},{28,20},{1,9},{5... | collective-permute-start | bytes 393224 | tf_op jit(solution)/shard_map/ppermute | solution.py:298
  106.7 8.3 %collective-permute-start.10 = (bf16[4,128,128]{2,1,0:T(8,128)(2,1)S(1)}, bf16[4,128,128]{2,1,0:T(8,128)(2,1)S(1)}, u32[]{:S(2)}, u32[]{:S(2)}) collective-permute-start(bf16[4,128,128]{2,1,0:T(8,128)(2,1)S(1)} %fusion.33), channel_id=1, source_target_pairs={{0,16},{4,20},{8,24},{12,28},{1,17},{5,21},{9,25},{13,29},{2,18},{... | collective-permute-start | bytes 393224 | tf_op jit(solution)/shard_map/ppermute | solution.py:298
  115.2 1.4 collective-permute-start.11
  117.4 24.3 %collective-permute-start.15 = (bf16[5,512,512]{2,1,0:T(8,128)(2,1)}, bf16[5,512,512]{2,1,0:T(8,128)(2,1)S(1)}, u32[]{:S(2)}, u32[]{:S(2)}) collective-permute-start(bf16[5,512,512]{2,1,0:T(8,128)(2,1)} %get-tuple-element.117), channel_id=1, source_target_pairs={{0,4},{4,0},{8,12},{12,8},{16,20},{20,16},{24,28},{28,24},{1,5},{5... | collective-permute-start | bytes 7864328 | tf_op jit(solution)/shard_map/ppermute | solution.py:298
  123.1 1.7 collective-permute-start.12
  126.0 6.0 %collective-permute-start.13 = (bf16[4,128,128]{2,1,0:T(8,128)(2,1)S(1)}, bf16[4,128,128]{2,1,0:T(8,128)(2,1)S(1)}, u32[]{:S(2)}, u32[]{:S(2)}) collective-permute-start(bf16[4,128,128]{2,1,0:T(8,128)(2,1)S(1)} %fusion.36), channel_id=1, source_target_pairs={{0,8},{4,12},{8,0},{12,4},{16,24},{20,28},{24,16},{28,20},{1,9},{5... | collective-permute-start | bytes 393224 | tf_op jit(solution)/shard_map/ppermute | solution.py:298
  132.1 9.6 %collective-permute-start.14 = (bf16[4,128,128]{2,1,0:T(8,128)(2,1)S(1)}, bf16[4,128,128]{2,1,0:T(8,128)(2,1)S(1)}, u32[]{:S(2)}, u32[]{:S(2)}) collective-permute-start(bf16[4,128,128]{2,1,0:T(8,128)(2,1)S(1)} %fusion.38), channel_id=1, source_target_pairs={{16,0},{20,4},{24,8},{28,12},{17,1},{21,5},{25,9},{29,13},{18,2},{... | collective-permute-start | bytes 393224 | tf_op jit(solution)/shard_map/ppermute | solution.py:298
  141.7 6.9 %copy-start.3 = (bf16[5,512,512]{2,1,0:T(8,128)(2,1)}, bf16[5,512,512]{2,1,0:T(8,128)(2,1)S(1)}, u32[]{:S(2)}) copy-start(bf16[5,512,512]{2,1,0:T(8,128)(2,1)S(1)} %collective-permute-done.15.fp_ref) | copy-start | bytes 7864324
  141.9 1.4 collective-permute-start.16
  148.7 7.6 %collective-permute-start.18 = (bf16[512,1024]{1,0:T(8,128)(2,1)}, bf16[512,1024]{1,0:T(8,128)(2,1)S(1)}, u32[]{:S(2)}, u32[]{:S(2)}) collective-permute-start(bf16[512,1024]{1,0:T(8,128)(2,1)} %get-tuple-element.148.kg_ref.go_ref), channel_id=1, source_target_pairs={{0,4},{4,0},{8,12},{12,8},{16,20},{20,16},{24,28},{28,24},{1,5},{5... | collective-permute-start | bytes 3145736 | tf_op jit(solution)/shard_map/ppermute | solution.py:298
  148.9 14.4 %collective-permute-start.19 = (bf16[512,1024]{1,0:T(8,128)(2,1)}, bf16[512,1024]{1,0:T(8,128)(2,1)S(1)}, u32[]{:S(2)}, u32[]{:S(2)}) collective-permute-start(bf16[512,1024]{1,0:T(8,128)(2,1)} %get-tuple-element.149.vg_ref.go_ref), channel_id=1, source_target_pairs={{0,4},{4,0},{8,12},{12,8},{16,20},{20,16},{24,28},{28,24},{1,5},{5... | collective-permute-start | bytes 3145736 | tf_op jit(solution)/shard_map/ppermute | solution.py:298
  154.8 24.6 %collective-permute-start.17 = (bf16[512,1024]{1,0:T(8,128)(2,1)}, bf16[512,1024]{1,0:T(8,128)(2,1)S(1)}, u32[]{:S(2)}, u32[]{:S(2)}) collective-permute-start(bf16[512,1024]{1,0:T(8,128)(2,1)} %bitcast.71), channel_id=1, source_target_pairs={{0,1},{3,2},{4,5},{7,6},{8,9},{11,10},{12,13},{15,14},{16,17},{19,... | collective-permute-start | bytes 3145736 | tf_op jit(solution)/shard_map/ppermute | solution.py:526
  156.2 1.0 copy-start.4
  163.3 1.6 copy-start.5
  163.3 50.4 %collective-permute-start.22 = (bf16[2,512,1024]{2,1,0:T(8,128)(2,1)}, bf16[2,512,1024]{2,1,0:T(8,128)(2,1)}, u32[]{:S(2)}, u32[]{:S(2)}) collective-permute-start(bf16[2,512,1024]{2,1,0:T(8,128)(2,1)} %weight_terms.6), channel_id=1, source_target_pairs={{0,8},{4,12},{8,0},{12,4},{16,24},{20,28},{24,16},{28,20},{1,9},{5... | collective-permute-start | bytes 6291464 | tf_op jit(solution)/shard_map/ppermute | solution.py:298
  170.9 52.1 %collective-permute-start.23 = (bf16[2,512,1024]{2,1,0:T(8,128)(2,1)}, bf16[2,512,1024]{2,1,0:T(8,128)(2,1)}, u32[]{:S(2)}, u32[]{:S(2)}) collective-permute-start(bf16[2,512,1024]{2,1,0:T(8,128)(2,1)} %weight_terms.7), channel_id=1, source_target_pairs={{0,16},{4,20},{8,24},{12,28},{16,0},{20,4},{24,8},{28,12},{1,17},{... | collective-permute-start | bytes 6291464 | tf_op jit(solution)/shard_map/ppermute | solution.py:298
  182.0 24.9 %collective-permute-start.21 = (bf16[512,1024]{1,0:T(8,128)(2,1)}, bf16[512,1024]{1,0:T(8,128)(2,1)S(1)}, u32[]{:S(2)}, u32[]{:S(2)}) collective-permute-start(bf16[512,1024]{1,0:T(8,128)(2,1)} %add_convert_fusion.2), channel_id=1, source_target_pairs={{2,1},{3,2},{6,5},{7,6},{10,9},{11,10},{14,13},{15,14},{18,17},{19... | collective-permute-start | bytes 3145736 | tf_op jit(solution)/shard_map/ppermute | solution.py:527
  182.7 27.4 %collective-permute-start.20 = (bf16[512,1024]{1,0:T(8,128)(2,1)}, bf16[512,1024]{1,0:T(8,128)(2,1)}, u32[]{:S(2)}, u32[]{:S(2)}) collective-permute-start(bf16[512,1024]{1,0:T(8,128)(2,1)} %add_convert_fusion.2), channel_id=1, source_target_pairs={{0,1},{1,2},{4,5},{5,6},{8,9},{9,10},{12,13},{13,14},{16,17},{17,1... | collective-permute-start | bytes 3145736 | tf_op jit(solution)/shard_map/ppermute | solution.py:527
  202.7 7.5 %copy-start.7 = (bf16[2,512,1024]{2,1,0:T(8,128)(2,1)S(1)}, bf16[2,512,1024]{2,1,0:T(8,128)(2,1)}, u32[]{:S(2)}) copy-start(bf16[2,512,1024]{2,1,0:T(8,128)(2,1)} %feature_terms.6) | copy-start | bytes 6291460
  206.9 14.5 %copy-start.9 = (bf16[1,512,1024]{2,1,0:T(8,128)(2,1)S(1)}, bf16[1,512,1024]{2,1,0:T(8,128)(2,1)}, u32[]{:S(2)}) copy-start(bf16[1,512,1024]{2,1,0:T(8,128)(2,1)} %weight_terms.8) | copy-start | bytes 3145732
  213.7 12.1 %copy-start.8 = (bf16[1,512,1024]{2,1,0:T(8,128)(2,1)S(1)}, bf16[1,512,1024]{2,1,0:T(8,128)(2,1)}, u32[]{:S(2)}) copy-start(bf16[1,512,1024]{2,1,0:T(8,128)(2,1)} %weight_terms.9) | copy-start | bytes 3145732
  213.7 29.8 %collective-permute-start.25 = (bf16[512,1024]{1,0:T(8,128)(2,1)}, bf16[512,1024]{1,0:T(8,128)(2,1)}, u32[]{:S(2)}, u32[]{:S(2)}) collective-permute-start(bf16[512,1024]{1,0:T(8,128)(2,1)} %get-tuple-element.150), channel_id=1, source_target_pairs={{0,1},{1,2},{2,3},{4,5},{5,6},{6,7},{8,9},{9,10},{10,11},{12,13},{... | collective-permute-start | bytes 3145736 | tf_op jit(solution)/shard_map/ppermute | solution.py:527
  220.1 25.8 %collective-permute-start.26 = (bf16[512,1024]{1,0:T(8,128)(2,1)}, bf16[512,1024]{1,0:T(8,128)(2,1)}, u32[]{:S(2)}, u32[]{:S(2)}) collective-permute-start(bf16[512,1024]{1,0:T(8,128)(2,1)} %get-tuple-element.153), channel_id=1, source_target_pairs={{1,0},{2,1},{3,2},{5,4},{6,5},{7,6},{9,8},{10,9},{11,10},{13,12},{... | collective-permute-start | bytes 3145736 | tf_op jit(solution)/shard_map/ppermute | solution.py:527
  223.0 26.0 %collective-permute-start.24 = (bf16[512,1024]{1,0:T(8,128)(2,1)S(1)}, bf16[512,1024]{1,0:T(8,128)(2,1)}, u32[]{:S(2)}, u32[]{:S(2)}) collective-permute-start(bf16[512,1024]{1,0:T(8,128)(2,1)S(1)} %fusion.26), channel_id=1, source_target_pairs={{0,16},{4,20},{8,24},{12,28},{16,0},{20,4},{24,8},{28,12},{1,17},{... | collective-permute-start | bytes 3145736 | tf_op jit(solution)/shard_map/ppermute | solution.py:298
  227.4 24.7 %collective-permute-start.27 = (bf16[512,1024]{1,0:T(8,128)(2,1)S(1)}, bf16[512,1024]{1,0:T(8,128)(2,1)}, u32[]{:S(2)}, u32[]{:S(2)}) collective-permute-start(bf16[512,1024]{1,0:T(8,128)(2,1)S(1)} %fusion.27), channel_id=1, source_target_pairs={{0,8},{4,12},{8,0},{12,4},{16,24},{20,28},{24,16},{28,20},{1,9},{5... | collective-permute-start | bytes 3145736 | tf_op jit(solution)/shard_map/ppermute | solution.py:298
  238.9 6.9 %copy-start.10 = (bf16[1,512,1024]{2,1,0:T(8,128)(2,1)S(1)}, bf16[1,512,1024]{2,1,0:T(8,128)(2,1)}, u32[]{:S(2)}) copy-start(bf16[1,512,1024]{2,1,0:T(8,128)(2,1)} %feature_terms.7) | copy-start | bytes 3145732
  243.4 5.6 %copy-start.13 = (bf16[1,512,1024]{2,1,0:T(8,128)(2,1)S(1)}, bf16[1,512,1024]{2,1,0:T(8,128)(2,1)}, u32[]{:S(2)}) copy-start(bf16[1,512,1024]{2,1,0:T(8,128)(2,1)} %weight_terms.10) | copy-start | bytes 3145732
  249.0 3.1 %copy-start.12 = (bf16[1,512,1024]{2,1,0:T(8,128)(2,1)S(1)}, bf16[1,512,1024]{2,1,0:T(8,128)(2,1)}, u32[]{:S(2)}) copy-start(bf16[1,512,1024]{2,1,0:T(8,128)(2,1)} %weight_terms.11) | copy-start | bytes 3145732

commit v4 on v3

--- a/solution.py
+++ b/solution.py
@@ -79,7 +79,7 @@
         scaled = (k_ref[:, cut].astype(F32) * tail).astype(BF)
         s_ref[i] = dot_tn(scaled, v_ref[:, cut]).astype(BF)
 
-    each_head(per, width, one)
+    each_head(per, width, one, 4)
 
 
 def local_kernel(width, per, cum_ref, cumt_ref, q_ref, k_ref, v_ref, mix_ref):
@@ -145,7 +145,7 @@
         kg_ref[:, cut] = (kl_ref[:, cut].astype(F32) + key_carried).astype(BF)
         vg_ref[:, cut] = (vl_ref[:, cut].astype(F32) + value_carried).astype(BF)
 
-    each_head(per, width, one)
+    each_head(per, width, one, 4)
 
 
 def per_head(kernel, args, kinds, outs, tokens, heads, width, per, name, limit=60):

time: 256 us -> 256 us (level)
  no operation moved by 1% of the time
where the time goes in v4:
time: 256 us; the launch traced here: 255 us
  Pallas kernels  97.5 us (38%)
  starting transfers between devices  48 us (19%)
  waiting for transfers between devices  37.3 us (15%)
  matrix products  35.7 us (14%)
  other arithmetic  29.6 us (12%)
  local copies, waits for them, and re-layouts  5.43 us (2%)
    dot_general x10, matrix products, dot(): return jnp.dot(a, b, preferred_element_type=F32)  35.7 us
    pallas_call x6, Pallas kernels, per_head(): pl.pallas_call(functools.partial(kernel, width, per), grid=(heads // per,...  30.8 us
    pallas_call x6, Pallas kernels, weight_terms(): pl.pallas_call(functools.partial(weight_kernel, len(adds)), grid_spec=plt...  29.4 us
    pallas_call x4, Pallas kernels, feature_terms(): pl.pallas_call(feature_kernel, grid_spec=pltpu.PrefetchScalarGridSpec(num...  26.1 us
    ppermute x18, starting transfers between devices, swap(): return lax.ppermute(x, 'seq', pairs)  21 us
    ppermute x1, waiting for transfers between devices, per_device(): got = [lax.ppermute(merged, 'head', upward + downward)]  15.1 us
    convert_element_type x5, other arithmetic, add(): return sum((t.astype(F32) for t in terms)).astype(BF)  12.5 us
    ppermute x2, starting transfers between devices, send(): lax.ppermute(up_sum, 'head', upward)  12.2 us
  transfers between devices with their start and end apart: 28, of which 13 were waited for; matrix products, arithmetic and copies ran while one was open for 22% of the time, Pallas kernels for 36%

profile of v4, /device:TPU:0, one launch (start us, length us, event | category | flops | bytes accessed | tf_op | source)
XLA Modules:
  0.0 254.7 jit_solution(3885816651004644743)
XLA Ops:
  1.9 6.5 %collective-permute-start = (bf16[512,1024]{1,0:T(8,128)(2,1)}, bf16[512,1024]{1,0:T(8,128)(2,1)}, u32[]{:S(2)}, u32[]{:S(2)}) collective-permute-start(bf16[512,1024]{1,0:T(8,128)(2,1)} %refs_0_.1), channel_id=1, source_target_pairs={{0,1},{1,2},{2,3},{4,5},{5,6},{6,7},{8,9},{9,10},{10,11},{12,13},{... | collective-permute-start | bytes 3145736 | tf_op jit(solution)/shard_map/ppermute | solution.py:412
  8.5 2.2 reduce-window.6
  11.2 3.2 %fusion.23 = f32[512,1024]{1,0:T(8,128)S(1)} fusion(bf16[512,1024]{1,0:T(8,128)(2,1)} %refs_0_.1, bf16[4096,1024]{1,0:T(8,128)(2,1)} %vw_ref.7, s32[]{:T(128)S(6)} %select_n.201), kind=kOutput, calls=%fused_computation.33 | convolution fusion | flops 1073741824 | bytes 5242884 | tf_op jit(solution)/shard_map/dot_general | solution.py:18
  14.5 4.2 %fusion.20 = f32[512,1024]{1,0:T(8,128)} fusion(bf16[512,1024]{1,0:T(8,128)(2,1)S(1)} %copy-done.17, bf16[4096,1024]{1,0:T(8,128)(2,1)} %kw_ref.7, s32[]{:T(128)S(6)} %select_n.201), kind=kOutput, calls=%fused_computation.32 | convolution fusion | flops 1073741824 | bytes 5242884 | tf_op jit(solution)/shard_map/dot_general | solution.py:18
  19.3 2.0 collective-permute-start.5
  23.0 2.0 collective-permute-start.6
  26.7 2.3 collective-permute-done.1.refs_1_
  32.2 4.5 %fusion.10 = f32[512,1024]{1,0:T(8,128)} fusion(bf16[512,1024]{1,0:T(8,128)(2,1)} %collective-permute-done.1.refs_1_, bf16[4096,1024]{1,0:T(8,128)(2,1)} %vw_ref.7, s32[]{:T(128)S(6)} %select_n.202), kind=kOutput, calls=%fused_computation.21 | convolution fusion | flops 1073741824 | bytes 5242884 | tf_op jit(solution)/shard_map/dot_general | solution.py:18
  36.7 4.5 %fusion.14 = f32[512,1024]{1,0:T(8,128)} fusion(bf16[512,1024]{1,0:T(8,128)(2,1)} %collective-permute-done.1.refs_1_, bf16[4096,1024]{1,0:T(8,128)(2,1)} %kw_ref.7, s32[]{:T(128)S(6)} %select_n.202), kind=kOutput, calls=%fused_computation.26 | convolution fusion | flops 1073741824 | bytes 5242884 | tf_op jit(solution)/shard_map/dot_general | solution.py:18
  41.2 6.6 %turn_features.2 = (bf16[5,512,512]{2,1,0:T(8,128)(2,1)}, bf16[5,512,512]{2,1,0:T(8,128)(2,1)}) custom-call(s32[1]{0:T(128)} %bitcast.2.core_ref, bf16[512,1024]{1,0:T(8,128)(2,1)} %refs_0_.1, bf16[512,1024]{1,0:T(8,128)(2,1)} %collective-permute-done.1.refs_1_, bf16[512,1024]{1,0:T(8,128)(2,1)} %collective-permute-done.refs_2_), custom_call_target="tpu_custom_call" | custom-call | flops 1 | bytes 1 | tf_op jit(solution)/shard_map/turn_features/pallas_call | solution.py:253
  47.8 5.3 %add_add_fusion = f32[512,1024]{1,0:T(8,128)} fusion(f32[512,1024]{1,0:T(8,128)S(1)} %fusion.23, f32[512,1024]{1,0:T(8,128)} %fusion.10, bf16[512,1024]{1,0:T(8,128)(2,1)} %collective-permute-done.refs_2_, bf16[4096,1024]{1,0:T(8,128)(2,1)} %vw_ref.7, s32[]{:T(128)S(6)} %select_n.203), kind=kOutput, calls=%fused_computation.20 | convolution fusion | flops 1074790400 | bytes 9437188 | tf_op jit(solution)/shard_map/dot_general | solution.py:18
  53.1 3.2 %add_add_fusion.1 = f32[512,1024]{1,0:T(8,128)S(1)} fusion(f32[512,1024]{1,0:T(8,128)S(1)} %copy-done.14, f32[512,1024]{1,0:T(8,128)S(1)} %copy-done.15, bf16[512,1024]{1,0:T(8,128)(2,1)} %collective-permute-done.refs_2_, bf16[4096,1024]{1,0:T(8,128)(2,1)} %kw_ref.7, s32[]{:T(128)S(6)} %select_n.203), kind=kOutput, calls=%fused_computation.25 | convolution fusion | flops 1074790400 | bytes 9437188 | tf_op jit(solution)/shard_map/dot_general | solution.py:18
  56.3 4.1 %collective-permute-done.3 = bf16[512,1024]{1,0:T(8,128)(2,1)} collective-permute-done((bf16[512,1024]{1,0:T(8,128)(2,1)}, bf16[512,1024]{1,0:T(8,128)(2,1)}, u32[]{:S(2)}, u32[]{:S(2)}) %collective-permute-start.3) | collective-permute-done | bytes 1048608 | tf_op jit(solution)/shard_map/ppermute | solution.py:413
  60.4 1.9 add.211.refs_2_
  63.9 2.7 %constant_dynamic-slice_fusion.6 = (bf16[1024,1024]{1,0:T(8,128)(2,1)S(1)}, bf16[1024,1024]{1,0:T(8,128)(2,1)S(1)}) fusion(bf16[4096,1024]{1,0:T(8,128)(2,1)} %vw_ref.7, s32[]{:T(128)S(6)} %select_n.232, bf16[4096,1024]{1,0:T(8,128)(2,1)} %kw_ref.7), kind=kLoop, calls=%fused_computation.82 | loop fusion | bytes 8388612 | tf_op jit(solution)/shard_map/dynamic_slice | solution.py:379
  66.6 3.0 %fusion.4 = f32[512,1024]{1,0:T(8,128)S(1)} fusion(bf16[512,1024]{1,0:T(8,128)(2,1)S(1)} %add.211.refs_2_, bf16[4096,1024]{1,0:T(8,128)(2,1)} %vw_ref.7, s32[]{:T(128)S(6)} %select_n.230), kind=kOutput, calls=%fused_computation.14 | convolution fusion | flops 1073741824 | bytes 5242884 | tf_op jit(solution)/shard_map/dot_general | solution.py:18
  70.1 2.8 %fusion.6 = f32[512,1024]{1,0:T(8,128)S(1)} fusion(bf16[512,1024]{1,0:T(8,128)(2,1)S(1)} %add.211.refs_2_, bf16[4096,1024]{1,0:T(8,128)(2,1)} %kw_ref.7, s32[]{:T(128)S(6)} %select_n.230), kind=kOutput, calls=%fused_computation.16 | convolution fusion | flops 1073741824 | bytes 5242884 | tf_op jit(solution)/shard_map/dot_general | solution.py:18
  73.4 15.1 %collective-permute-done.7.refs_3_ = bf16[512,1024]{1,0:T(8,128)(2,1)} collective-permute-done((bf16[512,1024]{1,0:T(8,128)(2,1)S(1)}, bf16[512,1024]{1,0:T(8,128)(2,1)}, u32[]{:S(2)}, u32[]{:S(2)}) %collective-permute-start.7) | collective-permute-done | bytes 1048608 | tf_op jit(solution)/shard_map/ppermute | solution.py:416
  88.5 2.5 fusion.57
  91.0 2.5 fusion.58
  101.1 5.3 %local_mix.1.mix_ref = bf16[512,1024]{1,0:T(8,128)(2,1)} custom-call(f32[512,8]{1,0:T(8,128)} %bitcast.63, f32[8,512]{1,0:T(8,128)} %copy.22.cumt_ref, bf16[512,1024]{1,0:T(8,128)(2,1)} %q_ref.5, bf16[512,1024]{1,0:T(8,128)(2,1)} %copy-done, bf16[512,1024]{1,0:T(8,128)(2,1)} %copy-done.1), custom_call_target="tpu_custom_call" | custom-call | flops 1 | bytes 1 | tf_op jit(solution)/shard_map/local_mix/pallas_call | solution.py:159
  106.6 3.7 %collective-permute-start.10 = (bf16[4,128,128]{2,1,0:T(8,128)(2,1)S(1)}, bf16[4,128,128]{2,1,0:T(8,128)(2,1)S(1)}, u32[]{:S(2)}, u32[]{:S(2)}) collective-permute-start(bf16[4,128,128]{2,1,0:T(8,128)(2,1)S(1)} %fusion.33), channel_id=1, source_target_pairs={{0,16},{4,20},{8,24},{12,28},{1,17},{5,21},{9,25},{13,29},{2,18},{... | collective-permute-start | bytes 393224 | tf_op jit(solution)/shard_map/ppermute | solution.py:298
  110.3 4.6 %turn_features.3 = (bf16[5,512,512]{2,1,0:T(8,128)(2,1)}, bf16[5,512,512]{2,1,0:T(8,128)(2,1)}) custom-call(s32[1]{0:T(128)} %bitcast.2.core_ref, bf16[5,512,512]{2,1,0:T(8,128)(2,1)} %get-tuple-element.103.refs_0_, bf16[5,512,512]{2,1,0:T(8,128)(2,1)} %get-tuple-element.104.refs_1_, ...), custom_call_target="tpu_custom_call", output_to_operand_aliasing={{0}: (1, {}), {1}: (2, {})} | custom-call | flops 1 | bytes 1 | tf_op jit(solution)/shard_map/turn_features/pallas_call | solution.py:253
  117.5 5.6 %norm_grad.1 = (bf16[512,1024]{1,0:T(8,128)(2,1)}, bf16[512,1024]{1,0:T(8,128)(2,1)}, bf16[8,128,128]{2,1,0:T(8,128)(2,1)}) custom-call(f32[512,8]{1,0:T(8,128)} %bitcast.64, bf16[512,1024]{1,0:T(8,128)(2,1)} %q_ref.5, bf16[512,1024]{1,0:T(8,128)(2,1)} %g_ref.1, bf16[512,1024]{1,0:T(8,128)(2,1)} %local_mix.1.mix_ref, bf16[8,128,128]{2,1,0:T(8,128)(2,1)} %fusion.28.s_ref), custom_call_target="tpu_custom_call" | custom-call | flops 1 | bytes 1 | tf_op jit(solution)/shard_map/norm_grad/pallas_call | solution.py:159
  126.5 5.3 %back_query.1 = bf16[512,1024]{1,0:T(8,128)(2,1)} custom-call(f32[512,8]{1,0:T(8,128)} %bitcast.65, f32[8,512]{1,0:T(8,128)} %copy.22.cumt_ref, bf16[512,1024]{1,0:T(8,128)(2,1)} %copy-done, bf16[512,1024]{1,0:T(8,128)(2,1)} %copy-done.1, bf16[512,1024]{1,0:T(8,128)(2,1)} %get-tuple-element.112.hg_ref, bf16[8,128,128]{2,1,0:T(8,128)(2,1)} %fusion.28.s_ref), custom_call_target="tpu_custom_call" | custom-call | flops 1 | bytes 1 | tf_op jit(solution)/shard_map/back_query/pallas_call | solution.py:159
  133.3 8.3 %back_keys.1 = (bf16[512,1024]{1,0:T(8,128)(2,1)}, bf16[512,1024]{1,0:T(8,128)(2,1)}) custom-call(f32[512,8]{1,0:T(8,128)} %bitcast.66, f32[8,512]{1,0:T(8,128)} %copy.22.cumt_ref, bf16[512,1024]{1,0:T(8,128)(2,1)} %q_ref.5, bf16[512,1024]{1,0:T(8,128)(2,1)} %copy-done, bf16[512,1024]{1,0:T(8,128)(2,1)} %copy-done.1, bf16[512,1024]{1,0:T(8,128)(2,1)} %get-tuple-element.112.hg_ref), custom_call_target="tpu_custom_call" | custom-call | flops 1 | bytes 1 | tf_op jit(solution)/shard_map/back_keys/pallas_call | solution.py:159
  144.0 4.3 %close_back.1 = (bf16[512,1024]{1,0:T(8,128)(2,1)}, bf16[512,1024]{1,0:T(8,128)(2,1)}) custom-call(f32[512,8]{1,0:T(8,128)} %bitcast.67, bf16[512,1024]{1,0:T(8,128)(2,1)} %copy-done, bf16[512,1024]{1,0:T(8,128)(2,1)} %copy-done.1, bf16[512,1024]{1,0:T(8,128)(2,1)} %get-tuple-element.118.kl_ref, bf16[512,1024]{1,0:T(8,128)(2,1)} %get-tuple-element.119.vl_ref, ...), custom_call_target="tpu_custom_call" | custom-call | flops 1 | bytes 1 | tf_op jit(solution)/shard_map/close_back/pallas_call | solution.py:159
  148.9 5.6 %feature_terms.4 = bf16[1,512,1024]{2,1,0:T(8,128)(2,1)} custom-call(s32[1]{0:T(128)} %bitcast.17.index_ref, bf16[512,1024]{1,0:T(8,128)(2,1)} %get-tuple-element.148.kg_ref.go_ref, bf16[512,1024]{1,0:T(8,128)(2,1)} %get-tuple-element.149.vg_ref.go_ref, bf16[4096,1024]{1,0:T(8,128)(2,1)} %kw_ref.7, bf16[4096,1024]{1,0:T(8,128)(2,1)} %vw_ref.7), custom_call_target="tpu_custom_call" | custom-call | flops 1 | bytes 1 | tf_op jit(solution)/shard_map/feature_terms/pallas_call | solution.py:184
  156.9 6.1 %weight_terms.6 = bf16[2,512,1024]{2,1,0:T(8,128)(2,1)} custom-call(s32[2]{0:T(128)} %get-tuple-element.126.index_ref, bf16[5,512,512]{2,1,0:T(8,128)(2,1)} %get-tuple-element.124.fo_ref, bf16[5,512,512]{2,1,0:T(8,128)(2,1)} %copy-done.3, bf16[512,1024]{1,0:T(8,128)(2,1)} %get-tuple-element.148.kg_ref.go_ref, bf16[512,1024]{1,0:T(8,128)(2,1)} %copy-done.4), custom_call_target="tpu_custom_call" | custom-call | flops 1 | bytes 1 | tf_op jit(solution)/shard_map/weight_terms/pallas_call | solution.py:217
  164.5 6.1 %weight_terms.7 = bf16[2,512,1024]{2,1,0:T(8,128)(2,1)} custom-call(s32[2]{0:T(128)} %get-tuple-element.123.index_ref, bf16[5,512,512]{2,1,0:T(8,128)(2,1)} %get-tuple-element.124.fo_ref, bf16[5,512,512]{2,1,0:T(8,128)(2,1)} %copy-done.3, bf16[512,1024]{1,0:T(8,128)(2,1)} %get-tuple-element.149.vg_ref.go_ref, bf16[512,1024]{1,0:T(8,128)(2,1)} %copy-done.5), custom_call_target="tpu_custom_call" | custom-call | flops 1 | bytes 1 | tf_op jit(solution)/shard_map/weight_terms/pallas_call | solution.py:217
  170.6 2.6 %collective-permute-start.23 = (bf16[2,512,1024]{2,1,0:T(8,128)(2,1)}, bf16[2,512,1024]{2,1,0:T(8,128)(2,1)}, u32[]{:S(2)}, u32[]{:S(2)}) collective-permute-start(bf16[2,512,1024]{2,1,0:T(8,128)(2,1)} %weight_terms.7), channel_id=1, source_target_pairs={{0,16},{4,20},{8,24},{12,28},{16,0},{20,4},{24,8},{28,12},{1,17},{... | collective-permute-start | bytes 6291464 | tf_op jit(solution)/shard_map/ppermute | solution.py:298
  173.3 5.6 %feature_terms.5 = bf16[1,512,1024]{2,1,0:T(8,128)(2,1)} custom-call(s32[1]{0:T(128)} %bitcast.19.index_ref, bf16[512,1024]{1,0:T(8,128)(2,1)} %get-tuple-element.148.kg_ref.go_ref, bf16[512,1024]{1,0:T(8,128)(2,1)} %get-tuple-element.149.vg_ref.go_ref, bf16[4096,1024]{1,0:T(8,128)(2,1)} %kw_ref.7, bf16[4096,1024]{1,0:T(8,128)(2,1)} %vw_ref.7), custom_call_target="tpu_custom_call" | custom-call | flops 1 | bytes 1 | tf_op jit(solution)/shard_map/feature_terms/pallas_call | solution.py:184
  179.1 2.6 %add_convert_fusion.2 = bf16[512,1024]{1,0:T(8,128)(2,1)} fusion(bf16[512,1024]{1,0:T(8,128)(2,1)S(1)} %collective-permute-done.17, bf16[512,1024]{1,0:T(8,128)(2,1)} %bitcast.68), kind=kLoop, calls=%fused_computation.11 | loop fusion | flops 2097152 | bytes 3145728 | tf_op jit(solution)/shard_map/convert_element_type | solution.py:512
  182.4 5.8 %collective-permute-start.20 = (bf16[512,1024]{1,0:T(8,128)(2,1)}, bf16[512,1024]{1,0:T(8,128)(2,1)}, u32[]{:S(2)}, u32[]{:S(2)}) collective-permute-start(bf16[512,1024]{1,0:T(8,128)(2,1)} %add_convert_fusion.2), channel_id=1, source_target_pairs={{0,1},{1,2},{4,5},{5,6},{8,9},{9,10},{12,13},{13,14},{16,17},{17,1... | collective-permute-start | bytes 3145736 | tf_op jit(solution)/shard_map/ppermute | solution.py:527
  188.9 9.4 %feature_terms.6 = bf16[2,512,1024]{2,1,0:T(8,128)(2,1)} custom-call(s32[2]{0:T(128)} %pad_add_fusion.index_ref, bf16[512,1024]{1,0:T(8,128)(2,1)} %get-tuple-element.148.kg_ref.go_ref, bf16[512,1024]{1,0:T(8,128)(2,1)} %get-tuple-element.149.vg_ref.go_ref, bf16[4096,1024]{1,0:T(8,128)(2,1)} %kw_ref.7, bf16[4096,1024]{1,0:T(8,128)(2,1)} %vw_ref.7), custom_call_target="tpu_custom_call" | custom-call | flops 1 | bytes 1 | tf_op jit(solution)/shard_map/feature_terms/pallas_call | solution.py:184
  198.3 4.1 %weight_terms.9 = bf16[1,512,1024]{2,1,0:T(8,128)(2,1)} custom-call(s32[1]{0:T(128)S(6)} %select_n.219.index_ref, bf16[5,512,512]{2,1,0:T(8,128)(2,1)} %get-tuple-element.124.fo_ref, bf16[5,512,512]{2,1,0:T(8,128)(2,1)} %copy-done.3, bf16[512,1024]{1,0:T(8,128)(2,1)} %get-tuple-element.149.vg_ref.go_ref, bf16[512,1024]{1,0:T(8,128)(2,1)} %copy-done.5), custom_call_target="tpu_custom_call" | custom-call | flops 1 | bytes 1 | tf_op jit(solution)/shard_map/weight_terms/pallas_call | solution.py:217
  202.4 4.2 %weight_terms.8 = bf16[1,512,1024]{2,1,0:T(8,128)(2,1)} custom-call(s32[1]{0:T(128)S(6)} %select_n.221.index_ref, bf16[5,512,512]{2,1,0:T(8,128)(2,1)} %get-tuple-element.124.fo_ref, bf16[5,512,512]{2,1,0:T(8,128)(2,1)} %copy-done.3, bf16[512,1024]{1,0:T(8,128)(2,1)} %get-tuple-element.148.kg_ref.go_ref, bf16[512,1024]{1,0:T(8,128)(2,1)} %copy-done.4), custom_call_target="tpu_custom_call" | custom-call | flops 1 | bytes 1 | tf_op jit(solution)/shard_map/weight_terms/pallas_call | solution.py:217
  206.6 3.2 %collective-permute-done.20 = bf16[512,1024]{1,0:T(8,128)(2,1)} collective-permute-done((bf16[512,1024]{1,0:T(8,128)(2,1)}, bf16[512,1024]{1,0:T(8,128)(2,1)}, u32[]{:S(2)}, u32[]{:S(2)}) %collective-permute-start.20) | collective-permute-done | bytes 1048608 | tf_op jit(solution)/shard_map/ppermute | solution.py:527
  209.8 3.5 %fusion.2 = (bf16[512,1024]{1,0:T(8,128)(2,1)}, bf16[512,1024]{1,0:T(8,128)(2,1)}) fusion(bf16[512,1024]{1,0:T(8,128)(2,1)S(1)} %collective-permute-done.21, bf16[2,512,1024]{2,1,0:T(8,128)(2,1)S(1)} %copy-done.7, bf16[512,1024]{1,0:T(8,128)(2,1)} %collective-permute-done.20), kind=kLoop, calls=%fused_computation.4 | loop fusion | flops 4194304 | bytes 6291456 | tf_op jit(solution)/shard_map/convert_element_type | solution.py:512
  213.4 6.4 %collective-permute-start.25 = (bf16[512,1024]{1,0:T(8,128)(2,1)}, bf16[512,1024]{1,0:T(8,128)(2,1)}, u32[]{:S(2)}, u32[]{:S(2)}) collective-permute-start(bf16[512,1024]{1,0:T(8,128)(2,1)} %get-tuple-element.150), channel_id=1, source_target_pairs={{0,1},{1,2},{2,3},{4,5},{5,6},{6,7},{8,9},{9,10},{10,11},{12,13},{... | collective-permute-start | bytes 3145736 | tf_op jit(solution)/shard_map/ppermute | solution.py:527
  222.7 2.7 %collective-permute-start.24 = (bf16[512,1024]{1,0:T(8,128)(2,1)S(1)}, bf16[512,1024]{1,0:T(8,128)(2,1)}, u32[]{:S(2)}, u32[]{:S(2)}) collective-permute-start(bf16[512,1024]{1,0:T(8,128)(2,1)S(1)} %fusion.26), channel_id=1, source_target_pairs={{0,16},{4,20},{8,24},{12,28},{16,0},{20,4},{24,8},{28,12},{1,17},{... | collective-permute-start | bytes 3145736 | tf_op jit(solution)/shard_map/ppermute | solution.py:298
  228.6 4.4 %weight_terms.11 = bf16[1,512,1024]{2,1,0:T(8,128)(2,1)} custom-call(s32[1]{0:T(128)S(6)} %select_n.223.index_ref, bf16[5,512,512]{2,1,0:T(8,128)(2,1)} %get-tuple-element.124.fo_ref, bf16[5,512,512]{2,1,0:T(8,128)(2,1)} %copy-done.3, bf16[512,1024]{1,0:T(8,128)(2,1)} %get-tuple-element.149.vg_ref.go_ref, bf16[512,1024]{1,0:T(8,128)(2,1)} %copy-done.5, ...), custom_call_target="tpu_custom_call" | custom-call | flops 1 | bytes 1 | tf_op jit(solution)/shard_map/weight_terms/pallas_call | solution.py:217
  233.0 5.6 %feature_terms.7 = bf16[1,512,1024]{2,1,0:T(8,128)(2,1)} custom-call(s32[1]{0:T(128)} %bitcast.10.index_ref, bf16[512,1024]{1,0:T(8,128)(2,1)} %get-tuple-element.148.kg_ref.go_ref, bf16[512,1024]{1,0:T(8,128)(2,1)} %get-tuple-element.149.vg_ref.go_ref, bf16[4096,1024]{1,0:T(8,128)(2,1)} %kw_ref.7, bf16[4096,1024]{1,0:T(8,128)(2,1)} %vw_ref.7), custom_call_target="tpu_custom_call" | custom-call | flops 1 | bytes 1 | tf_op jit(solution)/shard_map/feature_terms/pallas_call | solution.py:184
  238.6 4.5 %weight_terms.10 = bf16[1,512,1024]{2,1,0:T(8,128)(2,1)} custom-call(s32[1]{0:T(128)S(6)} %select_n.223.index_ref, bf16[5,512,512]{2,1,0:T(8,128)(2,1)} %get-tuple-element.124.fo_ref, bf16[5,512,512]{2,1,0:T(8,128)(2,1)} %copy-done.3, bf16[512,1024]{1,0:T(8,128)(2,1)} %get-tuple-element.148.kg_ref.go_ref, bf16[512,1024]{1,0:T(8,128)(2,1)} %copy-done.4, ...), custom_call_target="tpu_custom_call" | custom-call | flops 1 | bytes 1 | tf_op jit(solution)/shard_map/weight_terms/pallas_call | solution.py:217
  243.1 2.4 collective-permute-done.26
  245.6 3.1 %fusion.1 = bf16[512,1024]{1,0:T(8,128)(2,1)} fusion(bf16[512,1024]{1,0:T(8,128)(2,1)} %collective-permute-done.26, bf16[512,1024]{1,0:T(8,128)(2,1)} %collective-permute-done.25, bf16[1,512,1024]{2,1,0:T(8,128)(2,1)S(1)} %copy-done.10), kind=kLoop, calls=%fused_computation.2 | loop fusion | flops 3145728 | bytes 4194304 | tf_op jit(solution)/shard_map/convert_element_type | solution.py:512
  248.7 3.0 %add_multiply_fusion.1 = f32[512,1024]{1,0:T(8,128)} fusion(bf16[512,1024]{1,0:T(8,128)(2,1)} %collective-permute-done.24, bf16[512,1024]{1,0:T(8,128)(2,1)S(1)} %bitcast.70), kind=kLoop, calls=%fused_computation.8 | loop fusion | flops 2097152 | bytes 4194304 | tf_op jit(solution)/shard_map/mul | solution.py:590
  251.7 3.0 %add_multiply_fusion = f32[512,1024]{1,0:T(8,128)} fusion(bf16[512,1024]{1,0:T(8,128)(2,1)} %collective-permute-done.27, bf16[512,1024]{1,0:T(8,128)(2,1)S(1)} %bitcast.69), kind=kLoop, calls=%fused_computation.7 | loop fusion | flops 2097152 | bytes 4194304 | tf_op jit(solution)/shard_map/mul | solution.py:592
  (114 shorter events, 41.1 us)
Async XLA Ops:
  0.6 28.4 %collective-permute-start.1 = (bf16[512,1024]{1,0:T(8,128)(2,1)}, bf16[512,1024]{1,0:T(8,128)(2,1)}, u32[]{:S(2)}, u32[]{:S(2)}) collective-permute-start(bf16[512,1024]{1,0:T(8,128)(2,1)} %refs_0_.1), channel_id=1, source_target_pairs={{1,0},{2,1},{3,2},{5,4},{6,5},{7,6},{9,8},{10,9},{11,10},{13,12},{... | collective-permute-start | bytes 3145736 | tf_op jit(solution)/shard_map/ppermute | solution.py:413
  1.9 28.3 %collective-permute-start = (bf16[512,1024]{1,0:T(8,128)(2,1)}, bf16[512,1024]{1,0:T(8,128)(2,1)}, u32[]{:S(2)}, u32[]{:S(2)}) collective-permute-start(bf16[512,1024]{1,0:T(8,128)(2,1)} %refs_0_.1), channel_id=1, source_target_pairs={{0,1},{1,2},{2,3},{4,5},{5,6},{6,7},{8,9},{9,10},{10,11},{12,13},{... | collective-permute-start | bytes 3145736 | tf_op jit(solution)/shard_map/ppermute | solution.py:412
  11.1 89.2 %copy-start.2 = (f32[8,4,128]{0,2,1:T(8,128)}, f32[8,4,128]{0,2,1:T(8,128)S(1)}, u32[]{:S(2)}) copy-start(f32[8,4,128]{0,2,1:T(8,128)S(1)} %copy.21) | copy-start | bytes 49156
  11.1 8.2 %collective-permute-start.4 = (f32[1,8]{1,0:T(1,128)S(1)}, f32[1,8]{1,0:T(1,128)S(1)}, u32[]{:S(2)}, u32[]{:S(2)}) collective-permute-start(f32[1,8]{1,0:T(1,128)S(1)} %slice.29), channel_id=1, source_target_pairs={{0,4},{4,0},{8,12},{12,8},{16,20},{20,16},{24,28},{28,24},{1,5},{5... | collective-permute-start | bytes 104 | tf_op jit(solution)/shard_map/ppermute | solution.py:298
  11.2 3.3 %copy-start.17 = (bf16[512,1024]{1,0:T(8,128)(2,1)S(1)}, bf16[512,1024]{1,0:T(8,128)(2,1)}, u32[]{:S(2)}) copy-start(bf16[512,1024]{1,0:T(8,128)(2,1)} %refs_0_.1) | copy-start | bytes 3145732
  19.3 3.6 %collective-permute-start.5 = (f32[2,8]{1,0:T(2,128)S(1)}, f32[2,8]{1,0:T(2,128)S(1)}, u32[]{:S(2)}, u32[]{:S(2)}) collective-permute-start(f32[2,8]{1,0:T(2,128)S(1)} %pad_maximum_fusion.2), channel_id=1, source_target_pairs={{0,8},{4,12},{8,0},{12,4},{16,24},{20,28},{24,16},{28,20},{1,9},{5... | collective-permute-start | bytes 200 | tf_op jit(solution)/shard_map/ppermute | solution.py:298
  23.0 3.7 %collective-permute-start.6 = (f32[4,8]{1,0:T(4,128)S(1)}, f32[4,8]{1,0:T(4,128)S(1)}, u32[]{:S(2)}, u32[]{:S(2)}) collective-permute-start(f32[4,8]{1,0:T(4,128)S(1)} %pad_maximum_fusion.1), channel_id=1, source_target_pairs={{0,16},{4,20},{8,24},{12,28},{16,0},{20,4},{24,8},{28,12},{1,17},{... | collective-permute-start | bytes 392 | tf_op jit(solution)/shard_map/ppermute | solution.py:298
  30.2 26.1 %collective-permute-start.2 = (bf16[512,1024]{1,0:T(8,128)(2,1)}, bf16[512,1024]{1,0:T(8,128)(2,1)S(1)}, u32[]{:S(2)}, u32[]{:S(2)}) collective-permute-start(bf16[512,1024]{1,0:T(8,128)(2,1)} %collective-permute-done.refs_2_), channel_id=1, source_target_pairs={{1,2},{2,3},{5,6},{6,7},{9,10},{10,11},{13,14},{14,15},{17,18},{18... | collective-permute-start | bytes 3145736 | tf_op jit(solution)/shard_map/ppermute | solution.py:412
  30.9 29.5 %collective-permute-start.3 = (bf16[512,1024]{1,0:T(8,128)(2,1)}, bf16[512,1024]{1,0:T(8,128)(2,1)}, u32[]{:S(2)}, u32[]{:S(2)}) collective-permute-start(bf16[512,1024]{1,0:T(8,128)(2,1)} %collective-permute-done.1.refs_1_), channel_id=1, source_target_pairs={{1,0},{2,1},{5,4},{6,5},{9,8},{10,9},{13,12},{14,13},{17,16},{18,1... | collective-permute-start | bytes 3145736 | tf_op jit(solution)/shard_map/ppermute | solution.py:413
  47.8 5.3 %copy-start.14 = (f32[512,1024]{1,0:T(8,128)S(1)}, f32[512,1024]{1,0:T(8,128)}, u32[]{:S(2)}) copy-start(f32[512,1024]{1,0:T(8,128)} %fusion.20) | copy-start | bytes 6291460
  47.8 5.3 %copy-start.15 = (f32[512,1024]{1,0:T(8,128)S(1)}, f32[512,1024]{1,0:T(8,128)}, u32[]{:S(2)}) copy-start(f32[512,1024]{1,0:T(8,128)} %fusion.14) | copy-start | bytes 6291460
  56.3 4.1 %copy-start.16 = (bf16[512,1024]{1,0:T(8,128)(2,1)}, bf16[512,1024]{1,0:T(8,128)(2,1)S(1)}, u32[]{:S(2)}) copy-start(bf16[512,1024]{1,0:T(8,128)(2,1)S(1)} %collective-permute-done.2) | copy-start | bytes 3145732
  62.4 7.8 %copy-start.11 = (bf16[512,1024]{1,0:T(8,128)(2,1)}, bf16[512,1024]{1,0:T(8,128)(2,1)S(1)}, u32[]{:S(2)}) copy-start(bf16[512,1024]{1,0:T(8,128)(2,1)S(1)} %add.211.refs_2_) | copy-start | bytes 3145732
  62.4 26.1 %collective-permute-start.7 = (bf16[512,1024]{1,0:T(8,128)(2,1)S(1)}, bf16[512,1024]{1,0:T(8,128)(2,1)}, u32[]{:S(2)}, u32[]{:S(2)}) collective-permute-start(bf16[512,1024]{1,0:T(8,128)(2,1)S(1)} %add.211.refs_2_), channel_id=1, source_target_pairs={{2,3},{1,0},{6,7},{5,4},{10,11},{9,8},{14,15},{13,12},{18,19},{17,... | collective-permute-start | bytes 3145736 | tf_op jit(solution)/shard_map/ppermute | solution.py:416
  66.6 3.0 %copy-start.6 = (f32[512,1024]{1,0:T(8,128)S(1)}, f32[512,1024]{1,0:T(8,128)}, u32[]{:S(2)}) copy-start(f32[512,1024]{1,0:T(8,128)} %add_add_fusion) | copy-start | bytes 6291460
  94.0 1.0 copy-start
  95.0 6.0 %copy-start.1 = (bf16[512,1024]{1,0:T(8,128)(2,1)}, bf16[512,1024]{1,0:T(8,128)(2,1)S(1)}, u32[]{:S(2)}) copy-start(bf16[512,1024]{1,0:T(8,128)(2,1)S(1)} %add_convert_fusion.3.v_ref) | copy-start | bytes 3145732
  96.9 1.6 collective-permute-start.8
  98.7 7.8 %collective-permute-start.9 = (bf16[4,128,128]{2,1,0:T(8,128)(2,1)S(1)}, bf16[4,128,128]{2,1,0:T(8,128)(2,1)S(1)}, u32[]{:S(2)}, u32[]{:S(2)}) collective-permute-start(bf16[4,128,128]{2,1,0:T(8,128)(2,1)S(1)} %fusion.31), channel_id=1, source_target_pairs={{0,8},{4,12},{8,0},{12,4},{16,24},{20,28},{24,16},{28,20},{1,9},{5... | collective-permute-start | bytes 393224 | tf_op jit(solution)/shard_map/ppermute | solution.py:298
  106.6 8.3 %collective-permute-start.10 = (bf16[4,128,128]{2,1,0:T(8,128)(2,1)S(1)}, bf16[4,128,128]{2,1,0:T(8,128)(2,1)S(1)}, u32[]{:S(2)}, u32[]{:S(2)}) collective-permute-start(bf16[4,128,128]{2,1,0:T(8,128)(2,1)S(1)} %fusion.33), channel_id=1, source_target_pairs={{0,16},{4,20},{8,24},{12,28},{1,17},{5,21},{9,25},{13,29},{2,18},{... | collective-permute-start | bytes 393224 | tf_op jit(solution)/shard_map/ppermute | solution.py:298
  115.0 1.4 collective-permute-start.11
  117.3 24.3 %collective-permute-start.15 = (bf16[5,512,512]{2,1,0:T(8,128)(2,1)}, bf16[5,512,512]{2,1,0:T(8,128)(2,1)S(1)}, u32[]{:S(2)}, u32[]{:S(2)}) collective-permute-start(bf16[5,512,512]{2,1,0:T(8,128)(2,1)} %get-tuple-element.117), channel_id=1, source_target_pairs={{0,4},{4,0},{8,12},{12,8},{16,20},{20,16},{24,28},{28,24},{1,5},{5... | collective-permute-start | bytes 7864328 | tf_op jit(solution)/shard_map/ppermute | solution.py:298
  123.0 1.7 collective-permute-start.12
  125.8 6.0 %collective-permute-start.13 = (bf16[4,128,128]{2,1,0:T(8,128)(2,1)S(1)}, bf16[4,128,128]{2,1,0:T(8,128)(2,1)S(1)}, u32[]{:S(2)}, u32[]{:S(2)}) collective-permute-start(bf16[4,128,128]{2,1,0:T(8,128)(2,1)S(1)} %fusion.36), channel_id=1, source_target_pairs={{0,8},{4,12},{8,0},{12,4},{16,24},{20,28},{24,16},{28,20},{1,9},{5... | collective-permute-start | bytes 393224 | tf_op jit(solution)/shard_map/ppermute | solution.py:298
  132.0 9.6 %collective-permute-start.14 = (bf16[4,128,128]{2,1,0:T(8,128)(2,1)S(1)}, bf16[4,128,128]{2,1,0:T(8,128)(2,1)S(1)}, u32[]{:S(2)}, u32[]{:S(2)}) collective-permute-start(bf16[4,128,128]{2,1,0:T(8,128)(2,1)S(1)} %fusion.38), channel_id=1, source_target_pairs={{16,0},{20,4},{24,8},{28,12},{17,1},{21,5},{25,9},{29,13},{18,2},{... | collective-permute-start | bytes 393224 | tf_op jit(solution)/shard_map/ppermute | solution.py:298
  141.6 6.8 %copy-start.3 = (bf16[5,512,512]{2,1,0:T(8,128)(2,1)}, bf16[5,512,512]{2,1,0:T(8,128)(2,1)S(1)}, u32[]{:S(2)}) copy-start(bf16[5,512,512]{2,1,0:T(8,128)(2,1)S(1)} %collective-permute-done.15.fp_ref) | copy-start | bytes 7864324
  141.8 1.4 collective-permute-start.16
  148.4 7.6 %collective-permute-start.18 = (bf16[512,1024]{1,0:T(8,128)(2,1)}, bf16[512,1024]{1,0:T(8,128)(2,1)S(1)}, u32[]{:S(2)}, u32[]{:S(2)}) collective-permute-start(bf16[512,1024]{1,0:T(8,128)(2,1)} %get-tuple-element.148.kg_ref.go_ref), channel_id=1, source_target_pairs={{0,4},{4,0},{8,12},{12,8},{16,20},{20,16},{24,28},{28,24},{1,5},{5... | collective-permute-start | bytes 3145736 | tf_op jit(solution)/shard_map/ppermute | solution.py:298
  148.6 14.4 %collective-permute-start.19 = (bf16[512,1024]{1,0:T(8,128)(2,1)}, bf16[512,1024]{1,0:T(8,128)(2,1)S(1)}, u32[]{:S(2)}, u32[]{:S(2)}) collective-permute-start(bf16[512,1024]{1,0:T(8,128)(2,1)} %get-tuple-element.149.vg_ref.go_ref), channel_id=1, source_target_pairs={{0,4},{4,0},{8,12},{12,8},{16,20},{20,16},{24,28},{28,24},{1,5},{5... | collective-permute-start | bytes 3145736 | tf_op jit(solution)/shard_map/ppermute | solution.py:298
  154.5 24.6 %collective-permute-start.17 = (bf16[512,1024]{1,0:T(8,128)(2,1)}, bf16[512,1024]{1,0:T(8,128)(2,1)S(1)}, u32[]{:S(2)}, u32[]{:S(2)}) collective-permute-start(bf16[512,1024]{1,0:T(8,128)(2,1)} %bitcast.71), channel_id=1, source_target_pairs={{0,1},{3,2},{4,5},{7,6},{8,9},{11,10},{12,13},{15,14},{16,17},{19,... | collective-permute-start | bytes 3145736 | tf_op jit(solution)/shard_map/ppermute | solution.py:526
  155.9 1.0 copy-start.4
  163.0 1.6 copy-start.5
  163.0 50.4 %collective-permute-start.22 = (bf16[2,512,1024]{2,1,0:T(8,128)(2,1)}, bf16[2,512,1024]{2,1,0:T(8,128)(2,1)}, u32[]{:S(2)}, u32[]{:S(2)}) collective-permute-start(bf16[2,512,1024]{2,1,0:T(8,128)(2,1)} %weight_terms.6), channel_id=1, source_target_pairs={{0,8},{4,12},{8,0},{12,4},{16,24},{20,28},{24,16},{28,20},{1,9},{5... | collective-permute-start | bytes 6291464 | tf_op jit(solution)/shard_map/ppermute | solution.py:298
  170.6 52.1 %collective-permute-start.23 = (bf16[2,512,1024]{2,1,0:T(8,128)(2,1)}, bf16[2,512,1024]{2,1,0:T(8,128)(2,1)}, u32[]{:S(2)}, u32[]{:S(2)}) collective-permute-start(bf16[2,512,1024]{2,1,0:T(8,128)(2,1)} %weight_terms.7), channel_id=1, source_target_pairs={{0,16},{4,20},{8,24},{12,28},{16,0},{20,4},{24,8},{28,12},{1,17},{... | collective-permute-start | bytes 6291464 | tf_op jit(solution)/shard_map/ppermute | solution.py:298
  181.7 24.9 %collective-permute-start.21 = (bf16[512,1024]{1,0:T(8,128)(2,1)}, bf16[512,1024]{1,0:T(8,128)(2,1)S(1)}, u32[]{:S(2)}, u32[]{:S(2)}) collective-permute-start(bf16[512,1024]{1,0:T(8,128)(2,1)} %add_convert_fusion.2), channel_id=1, source_target_pairs={{2,1},{3,2},{6,5},{7,6},{10,9},{11,10},{14,13},{15,14},{18,17},{19... | collective-permute-start | bytes 3145736 | tf_op jit(solution)/shard_map/ppermute | solution.py:527
  182.4 27.4 %collective-permute-start.20 = (bf16[512,1024]{1,0:T(8,128)(2,1)}, bf16[512,1024]{1,0:T(8,128)(2,1)}, u32[]{:S(2)}, u32[]{:S(2)}) collective-permute-start(bf16[512,1024]{1,0:T(8,128)(2,1)} %add_convert_fusion.2), channel_id=1, source_target_pairs={{0,1},{1,2},{4,5},{5,6},{8,9},{9,10},{12,13},{13,14},{16,17},{17,1... | collective-permute-start | bytes 3145736 | tf_op jit(solution)/shard_map/ppermute | solution.py:527
  202.4 7.5 %copy-start.7 = (bf16[2,512,1024]{2,1,0:T(8,128)(2,1)S(1)}, bf16[2,512,1024]{2,1,0:T(8,128)(2,1)}, u32[]{:S(2)}) copy-start(bf16[2,512,1024]{2,1,0:T(8,128)(2,1)} %feature_terms.6) | copy-start | bytes 6291460
  206.6 14.4 %copy-start.9 = (bf16[1,512,1024]{2,1,0:T(8,128)(2,1)S(1)}, bf16[1,512,1024]{2,1,0:T(8,128)(2,1)}, u32[]{:S(2)}) copy-start(bf16[1,512,1024]{2,1,0:T(8,128)(2,1)} %weight_terms.8) | copy-start | bytes 3145732
  213.4 12.1 %copy-start.8 = (bf16[1,512,1024]{2,1,0:T(8,128)(2,1)S(1)}, bf16[1,512,1024]{2,1,0:T(8,128)(2,1)}, u32[]{:S(2)}) copy-start(bf16[1,512,1024]{2,1,0:T(8,128)(2,1)} %weight_terms.9) | copy-start | bytes 3145732
  213.4 29.8 %collective-permute-start.25 = (bf16[512,1024]{1,0:T(8,128)(2,1)}, bf16[512,1024]{1,0:T(8,128)(2,1)}, u32[]{:S(2)}, u32[]{:S(2)}) collective-permute-start(bf16[512,1024]{1,0:T(8,128)(2,1)} %get-tuple-element.150), channel_id=1, source_target_pairs={{0,1},{1,2},{2,3},{4,5},{5,6},{6,7},{8,9},{9,10},{10,11},{12,13},{... | collective-permute-start | bytes 3145736 | tf_op jit(solution)/shard_map/ppermute | solution.py:527
  219.8 25.8 %collective-permute-start.26 = (bf16[512,1024]{1,0:T(8,128)(2,1)}, bf16[512,1024]{1,0:T(8,128)(2,1)}, u32[]{:S(2)}, u32[]{:S(2)}) collective-permute-start(bf16[512,1024]{1,0:T(8,128)(2,1)} %get-tuple-element.153), channel_id=1, source_target_pairs={{1,0},{2,1},{3,2},{5,4},{6,5},{7,6},{9,8},{10,9},{11,10},{13,12},{... | collective-permute-start | bytes 3145736 | tf_op jit(solution)/shard_map/ppermute | solution.py:527
  222.7 26.0 %collective-permute-start.24 = (bf16[512,1024]{1,0:T(8,128)(2,1)S(1)}, bf16[512,1024]{1,0:T(8,128)(2,1)}, u32[]{:S(2)}, u32[]{:S(2)}) collective-permute-start(bf16[512,1024]{1,0:T(8,128)(2,1)S(1)} %fusion.26), channel_id=1, source_target_pairs={{0,16},{4,20},{8,24},{12,28},{16,0},{20,4},{24,8},{28,12},{1,17},{... | collective-permute-start | bytes 3145736 | tf_op jit(solution)/shard_map/ppermute | solution.py:298
  227.1 24.7 %collective-permute-start.27 = (bf16[512,1024]{1,0:T(8,128)(2,1)S(1)}, bf16[512,1024]{1,0:T(8,128)(2,1)}, u32[]{:S(2)}, u32[]{:S(2)}) collective-permute-start(bf16[512,1024]{1,0:T(8,128)(2,1)S(1)} %fusion.27), channel_id=1, source_target_pairs={{0,8},{4,12},{8,0},{12,4},{16,24},{20,28},{24,16},{28,20},{1,9},{5... | collective-permute-start | bytes 3145736 | tf_op jit(solution)/shard_map/ppermute | solution.py:298
  238.6 6.9 %copy-start.10 = (bf16[1,512,1024]{2,1,0:T(8,128)(2,1)S(1)}, bf16[1,512,1024]{2,1,0:T(8,128)(2,1)}, u32[]{:S(2)}) copy-start(bf16[1,512,1024]{2,1,0:T(8,128)(2,1)} %feature_terms.7) | copy-start | bytes 3145732
  243.1 5.6 %copy-start.13 = (bf16[1,512,1024]{2,1,0:T(8,128)(2,1)S(1)}, bf16[1,512,1024]{2,1,0:T(8,128)(2,1)}, u32[]{:S(2)}) copy-start(bf16[1,512,1024]{2,1,0:T(8,128)(2,1)} %weight_terms.10) | copy-start | bytes 3145732
  248.7 3.1 %copy-start.12 = (bf16[1,512,1024]{2,1,0:T(8,128)(2,1)S(1)}, bf16[1,512,1024]{2,1,0:T(8,128)(2,1)}, u32[]{:S(2)}) copy-start(bf16[1,512,1024]{2,1,0:T(8,128)(2,1)} %weight_terms.11) | copy-start | bytes 3145732
